TPU v7x, 512 devices: a whole 4x8x8 slice. The times are simulated.
512 devices in a mesh: gx: 16 (over y, core), gy: 4 (over z_lo), gz: 8 (over x, z_hi).
Axes of the slice: x: 4, y: 8, z: 8 (z_hi: 2, z_lo: 4; z = z_hi * 4 + z_lo), core: 2. Of those that a mesh axis runs over, the one named last changes fastest.
Arguments:
- centre_coef: float32 [16384, 3], P(('gx', 'gy', 'gz')), may hold values from -6 to 6
- centre_index: int32 [16384], P(('gx', 'gy', 'gz')), may hold values from 0 to 65535, as said below
- stiff_factor: float32 [256, 256, 1024], P('gx', 'gy', 'gz'), may hold values from 0.5 to 4
- prev_disp: float32 [3, 256, 256, 1024], P(None, 'gx', 'gy', 'gz'), may hold values from -6 to 6
Outputs:
- displacement: float32 [3, 256, 256, 1024], P(None, 'gx', 'gy', 'gz')
Inputs may be any that keep to these rules, and one draw needn't show every extreme that they name: `centre_index`: distinct wall nodes; the first and the last wall node are always among them.
All inputs are finite; a program needn't handle non-finite values.
Results may differ from a plain program's by a relative error of at most 0.0003.
Values sent between devices are 32-bit elements; how exact they have to be, the bound alone decides.
No kernel may reach another device: no remote copies, remote signals or barrier semaphores. Data moves between devices by JAX's collectives and lax.ppermute only.
A program may use at most 128 MiB of HBM per device.

v0:
```python
import jax
import jax.numpy as jnp
from jax import lax
from jax.sharding import PartitionSpec as P

LZ = 1
SWEEPS = 3


RADIUS = 0.02
OMEGA = 0.8
NEIGHBOURS = ((1, 0, 0), (-1, 0, 0), (0, 1, 0), (0, -1, 0), (0, 0, 1), (0, 0, -1))


def extended(shard, sides, width):
    for axis, dim in sides:
        size, length = (lax.axis_size(axis), shard.shape[dim])
        up = [(i, (i + 1) % size) for i in range(size - 1)]
        down = [(j, i) for i, j in up]
        last = lax.slice_in_dim(shard, length - width, length, axis=dim)
        first = lax.slice_in_dim(shard, 0, width, axis=dim)
        before = lax.ppermute(last, axis, up)
        after = lax.ppermute(first, axis, down)
        shard = jnp.concatenate([before, shard, after], axis=dim)
    return shard


def interior(array, offset):
    ext_x, ext_y, ext_z = array.shape[-3:]
    return array[
        ...,
        1 + offset[0] : ext_x - 1 + offset[0],
        1 + offset[1] : ext_y - 1 + offset[1],
        1 + offset[2] : ext_z - 1 + offset[2],
    ]


def relax_sweep(field_ext, stiff_ext, frozen):
    centre_stiff = interior(stiff_ext, (0, 0, 0))
    current = interior(field_ext, (0, 0, 0))
    flux_total = jnp.zeros_like(current)
    diagonal = jnp.zeros_like(centre_stiff)
    for offset in NEIGHBOURS:
        face = 0.5 * (centre_stiff + interior(stiff_ext, offset))
        flux_total = flux_total + face * interior(field_ext, offset)
        diagonal = diagonal + face
    updated = (1.0 - OMEGA) * current + OMEGA * (flux_total / diagonal)
    updated = jnp.where(frozen, current, updated)
    return updated


def wendland(dist_sq):
    ratio = jnp.sqrt(dist_sq) / RADIUS
    lead = jnp.maximum(1.0 - ratio, 0.0)
    return lead * lead * lead * lead * (4.0 * ratio + 1.0)


def kernel_sum(coef, index, node_x, node_y, node_z, count_x, count_y):
    centre_x = ((index // count_y).astype(jnp.float32) + 0.5) / count_x
    centre_y = ((index % count_y).astype(jnp.float32) + 0.5) / count_y
    dist_sq = (
        (node_x[None, :] - centre_x[:, None]) ** 2
        + (node_y[None, :] - centre_y[:, None]) ** 2
        + (node_z**2)[None, :]
    )
    weights = wendland(dist_sq)
    return jnp.dot(
        coef.T, weights, precision=lax.Precision.HIGHEST, preferred_element_type=jnp.float32
    )


def body(centre_coef, centre_index, stiff_factor, prev_disp):
    cells_x, cells_y, cells_z = stiff_factor.shape
    count_x = cells_x * lax.axis_size("gx")
    count_y = cells_y * lax.axis_size("gy")
    count_z = cells_z * lax.axis_size("gz")
    block_x = lax.axis_index("gx")
    block_y = lax.axis_index("gy")
    block_z = lax.axis_index("gz")
    layer_count = cells_x * cells_y * LZ
    node_ids = jnp.arange(layer_count, dtype=jnp.int32)
    global_x = block_x * cells_x + node_ids // (cells_y * LZ)
    global_y = block_y * cells_y + node_ids // LZ % cells_y
    global_z = node_ids % LZ
    node_x = (global_x.astype(jnp.float32) + 0.5) / count_x
    node_y = (global_y.astype(jnp.float32) + 0.5) / count_y
    node_z = (global_z.astype(jnp.float32) + 0.5) / count_z
    coef_piece = lax.all_gather(centre_coef, ("gx", "gy", "gz"), axis=0, tiled=True)
    index_piece = lax.all_gather(centre_index, ("gx", "gy", "gz"), axis=0, tiled=True)
    rows = index_piece.shape[0]

    def step(total, block):
        return (
            total + kernel_sum(block[0], block[1], node_x, node_y, node_z, count_x, count_y),
            None,
        )

    total, unused = lax.scan(
        step,
        jnp.zeros((3, node_ids.shape[0]), jnp.float32),
        (coef_piece.reshape(rows // 128, 128, 3), index_piece.reshape(rows // 128, 128)),
    )
    rbf = total.reshape(3, cells_x, cells_y, LZ)
    head = jnp.where(block_z == 0, rbf, prev_disp[..., :LZ])
    field = jnp.concatenate([head, prev_disp[..., LZ:]], axis=3)
    plane_z = block_z * cells_z + jnp.arange(cells_z, dtype=jnp.int32)
    stiffness = stiff_factor * (float(count_z) / (plane_z.astype(jnp.float32) + 0.5))
    frozen = plane_z < LZ
    stiff_ext = extended(stiffness, (("gx", 0), ("gy", 1), ("gz", 2)), 1)
    for sweep_no in range(SWEEPS):
        field_ext = extended(field, (("gx", 1), ("gy", 2), ("gz", 3)), 1)
        field = relax_sweep(field_ext, stiff_ext, frozen)
    return field


def solution(mesh):
    placed = (
        P(("gx", "gy", "gz"), None),
        P(("gx", "gy", "gz")),
        P("gx", "gy", "gz"),
        P(None, "gx", "gy", "gz"),
    )
    return jax.shard_map(
        body, mesh=mesh, in_specs=placed, out_specs=P(None, "gx", "gy", "gz"), check_vma=False
    )
```

profile of v0, /device:TPU:1, one launch (start us, length us, event | category | flops | bytes accessed | tf_op | source)
XLA Modules:
  0.0 1811.4 jit_solution(15925442470161995799)
XLA Ops:
  10.4 8.8 collective-permute-start
  21.1 1399.5 %all-gather = f32[512,32,3]{1,2,0:T(4,128)} all-gather(f32[1,32,3]{1,2,0:T(4,128)} %bitcast.27), channel_id=1, replica_groups=mesh['gx'=16,'gy'=4,'gz'=8] {'gx','gy','gz'}, dimensions={0}, use_global_device_ids=true | all-gather | bytes 196992 | tf_op jit(solution)/shard_map/all_gather | solution.py:88
  1423.2 211.8 %while.14 = (s32[]{:T(128)}, f32[3,1024]{1,0:T(4,128)S(1)}, f32[128,128,3]{1,0,2:T(8,128)S(1)}, s32[128,128]{1,0:T(8,128)}, s32[]{:T(128)}, /*index=5*/s32[]{:T(128)}, s32[]{:T(128)}, s32[]{:T(128)}) while((s32[]{:T(128)}, f32[3,1024]{1,0:T(4,128)S(1)}, f32[128,128,3]{1,0,2:T(8,128)S(1)}, s32[128,128]{1,0:T(8,128)}, s32[]{:T(128)}, ...), condition=%wide.region_1.2_spmd.clone, body=%wide.region_0.1_spmd.clone.sunk | while | flops 6714627 | bytes 49271 | solution.py:98
  1639.9 7.7 collective-permute-start.3
  1651.1 2.1 copy.140
  1656.0 8.5 collective-permute-start.10
  1666.6 6.4 collective-permute-start.7
  1678.5 2.6 fusion.118
  1681.1 3.1 copy.138
  1684.1 2.4 copy.143
  1690.0 3.8 add_add_fusion
  1700.6 2.8 copy.139
  1703.4 2.8 copy.144
  1706.2 8.4 fusion.85
  1714.6 4.5 collective-permute-start.13
  1721.1 4.0 collective-permute-done.12
  1726.4 4.9 collective-permute-start.15
  1734.6 2.4 copy.152
  1739.3 8.9 collective-permute-start.17
  1748.2 2.0 copy.153
  1750.3 2.1 copy.155
  1752.3 6.6 fusion.70
  1758.9 3.0 collective-permute-start.19
  1763.8 4.0 collective-permute-done.18
  1769.2 4.6 collective-permute-start.21
  1775.1 2.6 fusion.116
  1777.7 2.4 copy.162
  1781.5 2.4 copy.164
  1783.9 9.4 collective-permute-start.23
  1793.4 2.0 copy.163
  1795.4 2.1 copy.165
  1797.5 7.1 fusion.55
  (751 shorter events, 259.0 us)
Async XLA Ops:
  6.5 1414.1 %copy-start.7 = (f32[3,16,64,128]{3,2,1,0:T(8,128)S(1)}, f32[3,16,64,128]{3,2,1,0:T(8,128)}, u32[]{:S(2)}) copy-start(f32[3,16,64,128]{3,2,1,0:T(8,128)} %param.9) | copy-start | bytes 4718596
  6.5 1416.7 %all-reduce.3.cloned.1.call-start = ((), (), s32[]{:S(2)}) async-start(), calls=%async_computation | async-start | bytes 131072
  10.4 1625.3 %collective-permute-start = (f32[1,64,128]{2,0,1:T(1,128)S(1)}, f32[1,64,128]{2,0,1:T(1,128)S(1)}, u32[]{:S(2)}, u32[]{:S(2)}) collective-permute-start(f32[1,64,128]{2,0,1:T(1,128)S(1)} %get-tuple-element.221), channel_id=1, source_target_pairs={{32,0},{64,32},{96,64},{128,96},{160,128},{192,160},{224,192},{256... | collective-permute-start | bytes 98312 | tf_op jit(solution)/shard_map/ppermute | solution.py:23
  19.2 1616.5 %collective-permute-start.2 = (f32[1,64,128]{2,0,1:T(1,128)S(1)}, f32[1,64,128]{2,0,1:T(1,128)S(1)}, u32[]{:S(2)}, u32[]{:S(2)}) collective-permute-start(f32[1,64,128]{2,0,1:T(1,128)S(1)} %get-tuple-element.222), channel_id=1, source_target_pairs={{0,32},{32,64},{64,96},{96,128},{128,160},{160,192},{192,224},{224... | collective-permute-start | bytes 98312 | tf_op jit(solution)/shard_map/ppermute | solution.py:22
  1636.5 13.1 collective-permute-start.6
  1637.7 11.9 collective-permute-start.4
  1639.9 24.6 %collective-permute-start.3 = (f32[3,1,64,128]{3,2,1,0:T(8,128)}, f32[3,1,64,128]{3,2,1,0:T(8,128)S(1)}, u32[]{:S(2)}, u32[]{:S(2)}) collective-permute-start(f32[3,1,64,128]{3,2,1,0:T(8,128)} %get-tuple-element.201), channel_id=1, source_target_pairs={{0,32},{32,64},{64,96},{96,128},{128,160},{160,192},{192,224},{224... | collective-permute-start | bytes 294920 | tf_op jit(solution)/shard_map/ppermute | solution.py:22
  1647.7 16.8 collective-permute-start.1
  1654.7 20.3 %collective-permute-start.8 = (f32[18,66,1]{1,0,2:T(8,128)S(1)}, f32[18,66,1]{1,0,2:T(8,128)S(1)}, u32[]{:S(2)}, u32[]{:S(2)}) collective-permute-start(f32[18,66,1]{1,0,2:T(8,128)S(1)} %copy.133), channel_id=1, source_target_pairs={{1,0},{2,1},{3,2},{4,3},{5,4},{6,5},{7,6},{9,8},{10,9},{11,10},{12... | collective-permute-start | bytes 14264 | tf_op jit(solution)/shard_map/ppermute | solution.py:23
  1656.0 17.0 collective-permute-start.10
  1665.3 11.0 collective-permute-start.5
  1666.6 10.5 collective-permute-start.7
  1673.0 33.2 %copy-start.9 = (pred[128]{0:T(512)(128)(4,1)}, pred[128]{0:T(512)(128)(4,1)S(1)}, u32[]{:S(2)}) copy-start(pred[128]{0:T(512)(128)(4,1)S(1)} %fusion.109) | copy-start | bytes 388
  1686.6 16.8 collective-permute-start.11
  1688.5 12.0 collective-permute-start.9
  1714.6 18.1 copy-start
  1714.6 6.4 collective-permute-start.13
  1719.1 5.9 collective-permute-start.12
  1725.1 6.2 collective-permute-start.14
  1726.4 5.9 collective-permute-start.15
  1737.1 11.2 collective-permute-start.16
  1739.3 13.0 copy-start.10
  1739.3 11.0 collective-permute-start.17
  1758.9 4.9 collective-permute-start.19
  1761.9 5.9 collective-permute-start.18
  1767.9 5.9 collective-permute-start.20
  1769.2 5.6 collective-permute-start.21
  1780.2 13.2 collective-permute-start.22
  1783.9 13.6 copy-start.4
  1783.9 13.6 copy-start.5
  1783.9 13.6 copy-start.6
  1783.9 11.5 collective-permute-start.23
  (4 other events, 26.3 us)
Sparse Core Ops, SparseCore 0:
  12.3 267.0 all-reduce.2
where the time goes:
time: 1830 us; the launch traced here: 1810 us
  blocking collectives  1400 us (77%)
  other arithmetic  122 us (7%)
  matrix products  114 us (6%)
  starting transfers between devices  88.3 us (5%)
  local copies, waits for them, and re-layouts  59.3 us (3%)
    all_gather x1, blocking collectives, body(): lax.all_gather(centre_coef, ('gx', 'gy', 'gz'), axis=0, tiled=True)  1400 us
    dot_general x128, matrix products, kernel_sum(): jnp.dot(coef.T, weights, precision=lax.Precision.HIGHEST, preferred_eleme...  114 us
    div x128, other arithmetic, kernel_sum(): centre_x = ((index // count_y).astype(jnp.float32) + 0.5) / count_x  89.3 us
    ppermute x12, starting transfers between devices, extended(): before = lax.ppermute(last, axis, up)  63.1 us
  transfers between devices with their start and end apart: 25, of which 4 were waited for; matrix products, arithmetic and copies ran while one was open for 13% of the time, Pallas kernels for 0%

commit v1 on v0

v1 whole, which is shorter than its diff:
```python
import functools
import math

import jax
import jax.numpy as jnp
from jax import lax
from jax.experimental import pallas as pl
from jax.experimental.pallas import tpu as pltpu
from jax.sharding import PartitionSpec as P

SWEEPS = 3
RADIUS = 0.02
OMEGA = 0.8

HALO = 3
TOP = 8
WIN = 72
ROWS = 88
LANES = 128
VMEM_LIMIT = 40 * 1024 * 1024


def lane_ids(rows=WIN):
    return lax.broadcasted_iota(jnp.int32, (rows, LANES), 1)


def roll_lanes(value, shift):
    if isinstance(shift, int):
        shift = shift % LANES
        if shift == 0:
            return value
    return pltpu.roll(value, shift, 1)


def kernel_call(kernel, name, outs, flops, args, scratch=()):
    moved = sum(math.prod(a.shape) * 4 for a in (*args, *outs))
    return pl.pallas_call(
        kernel,
        name=name,
        out_shape=outs,
        in_specs=[pl.BlockSpec(memory_space=pltpu.VMEM)] * len(args),
        out_specs=tuple(pl.BlockSpec(memory_space=pltpu.VMEM) for _ in outs),
        scratch_shapes=list(scratch),
        compiler_params=pltpu.CompilerParams(vmem_limit_bytes=VMEM_LIMIT),
        cost_estimate=pl.CostEstimate(flops=flops, bytes_accessed=moved, transcendentals=0),
    )(*args)


def f32(*shape):
    return jax.ShapeDtypeStruct(shape, jnp.float32)


def pack_z_kernel(prev_ref, stiff_ref, low_ref, high_ref, ylow_ref, yhigh_ref):
    cells_x, cells_y, cells_z = stiff_ref.shape
    lane = lax.broadcasted_iota(jnp.int32, (8, LANES), 1)
    place = lane % 8
    pick = jnp.where(place <= 3, jnp.clip(3 - place, 0, 2), cells_z - 1 - jnp.clip(place - 4, 0, 2))
    for tile in range(cells_y // 8):
        rows = pl.ds(8 * tile, 8)
        edges = []
        for ch in range(4):
            edge = jnp.zeros((8, LANES), jnp.float32)
            for x in range(cells_x):
                value = prev_ref[ch, x, rows, :] if ch < 3 else stiff_ref[x, rows, :]
                picked = jnp.take_along_axis(value, pick, axis=1)
                edge = jnp.where(lane // 8 == x, picked, edge)
            edges.append(edge)
        for pair in range(2):
            even, odd = edges[2 * pair], edges[2 * pair + 1]
            low_ref[pair, rows, :] = jnp.where(place <= 3, even, roll_lanes(odd, 3))
            high_ref[pair, rows, :] = jnp.where(place >= 4, even, roll_lanes(odd, -3))
    for ch in range(4):
        for x in range(cells_x):
            at = pl.ds((ch * cells_x + x) * HALO, HALO)
            if ch < 3:
                ylow_ref[at, :] = prev_ref[ch, x, :HALO, :]
                yhigh_ref[at, :] = prev_ref[ch, x, cells_y - HALO :, :]
            else:
                ylow_ref[at, :] = stiff_ref[x, :HALO, :]
                yhigh_ref[at, :] = stiff_ref[x, cells_y - HALO :, :]


def pack_y_kernel(above_ref, below_ref, ylow_ref, yhigh_ref, edge_ref, outlow_ref, outhigh_ref):
    rows = above_ref.shape[1]
    place = lane_ids(rows) % 8
    upper = (place >= 1) & (place <= 3)
    lower = (place >= 4) & (place <= 6)
    base = ylow_ref.shape[0]
    outlow_ref[:base, :] = ylow_ref[...]
    outhigh_ref[:base, :] = yhigh_ref[...]
    for ch in range(4):
        above, below = above_ref[ch // 2], below_ref[ch // 2]
        if ch % 2:
            above, below = roll_lanes(above, -3), roll_lanes(below, 3)
        edge = jnp.where(upper, above, jnp.where(lower, below, 0.0))
        edge_ref[ch] = edge
        at = pl.ds(base + ch * HALO, HALO)
        outlow_ref[at, :] = edge[:HALO]
        outhigh_ref[at, :] = edge[rows - HALO :]
    rest = outlow_ref.shape[0] - base - 4 * HALO
    outlow_ref[base + 4 * HALO :, :] = jnp.zeros((rest, LANES), jnp.float32)
    outhigh_ref[base + 4 * HALO :, :] = jnp.zeros((rest, LANES), jnp.float32)


def pack_x_kernel(prev_ref, stiff_ref, edge_ref, yabove_ref, ybelow_ref, low_ref, high_ref, wide_ref):
    cells_x, cells_y, _ = stiff_ref.shape
    lane = lane_ids()
    base = 4 * cells_x * HALO
    rest = WIN - 2 - cells_y - HALO
    low = jnp.zeros((WIN, LANES), jnp.float32)
    high = low
    for ch in range(4):
        for p in range(HALO):
            for out, x in ((low_ref, p), (high_ref, cells_x - HALO + p)):
                at = (ch * cells_x + x) * HALO
                plane = ch * HALO + p
                out[plane, 0:2, :] = ybelow_ref[at + 1 : at + HALO, :]
                out[plane, 2 : 2 + cells_y, :] = prev_ref[ch, x] if ch < 3 else stiff_ref[x]
                out[plane, 2 + cells_y : 2 + cells_y + HALO, :] = yabove_ref[at : at + HALO, :]
                out[plane, 2 + cells_y + HALO :, :] = jnp.zeros((rest, LANES), jnp.float32)
        at = base + ch * HALO
        wide_ref[ch, 0:2, :] = ybelow_ref[at + 1 : at + HALO, :]
        wide_ref[ch, 2 : 2 + cells_y, :] = edge_ref[ch]
        wide_ref[ch, 2 + cells_y : 2 + cells_y + HALO, :] = yabove_ref[at : at + HALO, :]
        wide_ref[ch, 2 + cells_y + HALO :, :] = jnp.zeros((rest, LANES), jnp.float32)
        turned = roll_lanes(wide_ref[ch], 32 * ch)
        at_low = (lane - 32 * ch) & (LANES - 1)
        low = jnp.where(at_low < 8 * HALO, turned, low)
        high = jnp.where(at_low >= LANES - 8 * HALO, turned, high)
    low_ref[4 * HALO] = low
    high_ref[4 * HALO] = high


def stencil(count_x, count_y, count_z):
    table = {}
    for step_x in range(int(RADIUS * count_x) + 2):
        for step_y in range(int(RADIUS * count_y) + 2):
            square = (step_x / count_x) ** 2 + (step_y / count_y) ** 2 + (0.5 / count_z) ** 2
            ratio = math.sqrt(square) / RADIUS
            lead = max(1.0 - ratio, 0.0)
            if lead > 0.0:
                table[step_x, step_y] = lead**4 * (4.0 * ratio + 1.0)
    return table


REACH_X = 8
REACH_Y = 8
GRID_X = 32
GRID_Y = 80


def rbf_kernel(table, cells_x, cells_y, count_y, centres_ref, out_ref, grid_ref):
    slots = centres_ref.shape[0] // 4
    first_x = (lax.axis_index("gx") * cells_x - REACH_X).astype(jnp.float32)
    first_y = (lax.axis_index("gy") * cells_y - REACH_Y).astype(jnp.float32)
    quarter = lane_ids(slots) // 32
    fields = []
    for f in range(4):
        field = jnp.zeros((slots, LANES), jnp.float32)
        for k in range(4):
            part = roll_lanes(centres_ref[k * slots : (k + 1) * slots, :], 32 * (k - f))
            field = jnp.where(quarter == k, part, field)
        fields.append(field)
    index = fields[3]
    at_x = jnp.floor(index * (1.0 / count_y))
    at_y = index - at_x * count_y - first_y
    at_x = at_x - first_x
    heads = [f.astype(jnp.bfloat16).astype(jnp.float32) for f in fields[:3]]
    tails = [f - h for f, h in zip(fields[:3], heads)]
    row_y = lax.broadcasted_iota(jnp.int32, (GRID_Y, LANES), 0).astype(jnp.float32)
    row_x = lax.broadcasted_iota(jnp.int32, (GRID_X, LANES), 0).astype(jnp.float32)
    total = jnp.zeros((GRID_Y, 2 * LANES), jnp.float32)
    blank = jnp.zeros((LANES - 3 * GRID_X, LANES), jnp.float32)
    for q in range(0, slots, 2):
        left, right = [], []
        for r in (q, q + 1):
            hit_y = at_y[r : r + 1, :] == row_y
            hit_x = at_x[r : r + 1, :] == row_x
            left.append(jnp.where(hit_y, 1.0, 0.0).astype(jnp.bfloat16))
            pieces = []
            for group in (heads, tails):
                pieces += [jnp.where(hit_x, g[r : r + 1, :], 0.0) for g in group]
                pieces.append(blank)
            right.append(jnp.concatenate(pieces, axis=0).astype(jnp.bfloat16))
        total = total + lax.dot_general(
            jnp.concatenate(left, axis=1),
            jnp.concatenate(right, axis=1),
            (((1,), (1,)), ((), ())),
            preferred_element_type=jnp.float32,
        )
    grid = total[:, :LANES] + total[:, LANES:]
    reach_x = max(a for a, _ in table)
    reach_y = max(b for _, b in table)
    result = jnp.zeros((WIN, LANES), jnp.float32)
    for step_x in range(reach_x + 1):
        value = roll_lanes(grid, HALO - REACH_X + step_x)
        if step_x:
            value = value + roll_lanes(grid, HALO - REACH_X - step_x)
        grid_ref[:GRID_Y, :] = value
        for step_y in range(reach_y + 1):
            phi = table.get((step_x, step_y))
            if phi is None:
                continue
            start = REACH_Y - 2
            part = grid_ref[start + step_y : start + step_y + WIN, :]
            if step_y:
                part = part + grid_ref[start - step_y : start - step_y + WIN, :]
            result = result + phi * part
    for k in range(out_ref.shape[0]):
        out_ref[k] = result


def sweep_kernel(
    count_z,
    prev_ref,
    stiff_ref,
    wide_ref,
    yabove_ref,
    ybelow_ref,
    xabove_ref,
    xbelow_ref,
    rbf_ref,
    out_ref,
    u_ref,
    s_ref,
    w_ref,
    e_ref,
    es_ref,
    ew_ref,
    c_ref,
):
    cells_x, cells_y, cells_z = stiff_ref.shape
    ext = cells_x + 2 * HALO
    block_z = lax.axis_index("gz")
    window = pl.ds(TOP, WIN)
    before = pl.ds(TOP - 1, WIN)
    after = pl.ds(TOP + 1, WIN)
    lane = lane_ids()
    place = lane % 8
    group = lane // 8

    deep = (block_z * cells_z + lane_ids(1)).astype(jnp.float32) + 0.5
    scale = count_z / deep
    edge_z = jnp.where(place <= 3, cells_z + 3 - place, 3 - place)
    edge_scale = count_z / ((block_z * cells_z + edge_z).astype(jnp.float32) + 0.5)

    main = pl.ds(TOP + 2, cells_y)
    for ch in range(4):
        for x in range(cells_x):
            at = (ch * cells_x + x) * HALO
            low, high = ybelow_ref[at : at + HALO, :], yabove_ref[at : at + HALO, :]
            if ch < 3:
                u_ref[0, ch, HALO + x, main, :] = prev_ref[ch, x]
                u_ref[0, ch, HALO + x, TOP - 1 : TOP + 2, :] = low
                u_ref[0, ch, HALO + x, TOP + 2 + cells_y : TOP + 2 + cells_y + HALO, :] = high
            else:
                s_ref[HALO + x, main, :] = stiff_ref[x] * scale
                s_ref[HALO + x, TOP - 1 : TOP + 2, :] = low * scale
                s_ref[HALO + x, TOP + 2 + cells_y : TOP + 2 + cells_y + HALO, :] = high * scale
        for p in range(HALO):
            for source, x in ((xbelow_ref, p), (xabove_ref, HALO + cells_x + p)):
                if ch < 3:
                    u_ref[0, ch, x, window, :] = source[ch * HALO + p]
                else:
                    s_ref[x, window, :] = source[ch * HALO + p] * scale
        above = roll_lanes(xabove_ref[4 * HALO], -32 * ch)
        below = roll_lanes(xbelow_ref[4 * HALO], -32 * ch)
        side = jnp.where(lane < 8 * HALO, above, jnp.where(lane >= LANES - 8 * HALO, below, 0.0))
        if ch < 3:
            e_ref[0, ch, 0, window, :] = wide_ref[ch]
            e_ref[0, ch, 1, window, :] = side
        else:
            es_ref[0, window, :] = wide_ref[ch] * edge_scale
            es_ref[1, window, :] = side * edge_scale

    first = (lane == 0) & (block_z == 0)

    @pl.when(block_z == 0)
    def _():
        rbf = rbf_ref[0]
        for k in range(1, rbf_ref.shape[0]):
            rbf = rbf + rbf_ref[k]

        def layer(x, carry):
            own = first & (s_ref[x, window, :] > 0.0)
            for ch in range(3):
                column = pltpu.roll(rbf, (2 * LANES - 32 * ch - x) % LANES, 1)
                u_ref[0, ch, x, window, :] = jnp.where(own, column, u_ref[0, ch, x, window, :])
            return carry

        lax.fori_loop(0, ext, layer, 0)

    def spot(x):
        return ((x + 13) // 16 + 1) % 2, (x + 13) % 16

    def z_pair(value, edge):
        down = jnp.where(lane == 0, edge, roll_lanes(value, 1))
        up = jnp.where(lane == LANES - 1, edge, roll_lanes(value, -1))
        return down, up

    def at_edge(g):
        return (group == g) & ((place == 3) | (place == 4))

    def normalised(own, others):
        faces = [0.5 * (own + other) for other in others]
        total = functools.reduce(lambda a, b: a + b, faces)
        factor = jnp.where(own > 0.0, OMEGA / jnp.where(own > 0.0, total, 1.0), 0.0)
        return [face * factor for face in faces]

    c_ref[...] = jnp.zeros_like(c_ref)

    def weigh(x, carry):
        own = s_ref[x, window, :]
        tile, g = spot(x)
        edge = pltpu.roll(es_ref[tile, window, :], LANES - 4 - 8 * g, 1)
        down, up = z_pair(own, edge)
        others = (s_ref[x - 1, window, :], s_ref[x + 1, window, :], s_ref[x, before, :], s_ref[x, after, :], down, up)
        for k, weight in enumerate(normalised(own, others)):
            w_ref[k, x] = weight
        c_ref[0, tile] = jnp.where(at_edge(g), pltpu.roll(own, 8 * g + 4, 1), c_ref[0, tile])
        return carry

    lax.fori_loop(1, ext - 1, weigh, 0)

    def edge_neighbours(ref, tile, middle):
        own, other = ref[tile, window, :], ref[1 - tile, window, :]
        left = jnp.where(lane >= 8, roll_lanes(own, 8), roll_lanes(other, 8))
        right = jnp.where(lane < LANES - 8, roll_lanes(own, -8), roll_lanes(other, -8))
        minus = jnp.where(place == 4, middle, roll_lanes(own, 1))
        plus = jnp.where(place == 3, middle, roll_lanes(own, -1))
        return own, (left, right, ref[tile, before, :], ref[tile, after, :], minus, plus)

    for tile in range(2):
        own, others = edge_neighbours(es_ref, tile, c_ref[0, tile])
        for k, weight in enumerate(normalised(own, others)):
            ew_ref[k, tile] = weight

    for sweep in range(SWEEPS):
        now, later = sweep % 2, (sweep + 1) % 2
        last = sweep == SWEEPS - 1

        def relax(x, carry):
            tile, g = spot(x)
            weights = [w_ref[k, x] for k in range(6)]
            for ch in range(3):
                own = u_ref[now, ch, x, window, :]
                edge = pltpu.roll(e_ref[now, ch, tile, window, :], LANES - 4 - 8 * g, 1)
                down, up = z_pair(own, edge)
                others = (
                    u_ref[now, ch, x - 1, window, :],
                    u_ref[now, ch, x + 1, window, :],
                    u_ref[now, ch, x, before, :],
                    u_ref[now, ch, x, after, :],
                    down,
                    up,
                )
                new = (1.0 - OMEGA) * own
                for weight, other in zip(weights, others):
                    new = new + weight * other
                new = jnp.where(first, own, new)
                if last:
                    out_ref[ch, x - HALO] = new[2 : 2 + cells_y]
                else:
                    u_ref[later, ch, x, window, :] = new
                    c_ref[ch, tile] = jnp.where(at_edge(g), pltpu.roll(own, 8 * g + 4, 1), c_ref[ch, tile])
            return carry

        lax.fori_loop(1 + sweep, ext - 1 - sweep, relax, 0)
        if not last:
            for ch in range(3):
                for tile in range(2):
                    own, others = edge_neighbours(e_ref.at[now, ch], tile, c_ref[ch, tile])
                    new = (1.0 - OMEGA) * own
                    for k, other in enumerate(others):
                        new = new + ew_ref[k, tile] * other
                    e_ref[later, ch, tile, window, :] = new


def step(value, axis, by):
    size = lax.axis_size(axis)
    return lax.ppermute(value, axis, [(i, i + by) for i in range(size) if 0 <= i + by < size])


def body(centre_coef, centre_index, stiff_factor, prev_disp):
    cells_x, cells_y, cells_z = stiff_factor.shape
    count_x = cells_x * lax.axis_size("gx")
    count_y = cells_y * lax.axis_size("gy")
    count_z = cells_z * lax.axis_size("gz")
    blocks = lax.axis_size("gx") * lax.axis_size("gy")
    depth = lax.axis_size("gz")

    row = jnp.concatenate([centre_coef.T, centre_index.astype(jnp.float32)[None]], axis=0).reshape(1, 1, LANES)
    centres = lax.all_to_all(jnp.broadcast_to(row, (blocks, 1, LANES)), ("gx", "gy"), 0, 0, tiled=True)
    centres = centres.reshape(blocks, LANES)

    rows_y = 4 * cells_x * HALO
    low, high, ylow, yhigh = kernel_call(
        pack_z_kernel,
        "pack_z",
        (f32(2, cells_y, LANES), f32(2, cells_y, LANES), f32(rows_y, LANES), f32(rows_y, LANES)),
        1 << 21,
        (prev_disp, stiff_factor),
    )
    zabove, zbelow = step(low, "gz", -1), step(high, "gz", 1)

    table = stencil(count_x, count_y, count_z)
    (share,) = kernel_call(
        functools.partial(rbf_kernel, table, cells_x, cells_y, count_y),
        "rbf",
        (f32(depth, WIN, LANES),),
        1 << 24,
        (centres,),
        (pltpu.VMEM((ROWS, LANES), jnp.float32),),
    )
    shares = lax.all_to_all(share, "gz", 0, 0, tiled=True)

    rows_all = -(-(rows_y + 4 * HALO) // 8) * 8
    edge, ylow, yhigh = kernel_call(
        pack_y_kernel,
        "pack_y",
        (f32(4, cells_y, LANES), f32(rows_all, LANES), f32(rows_all, LANES)),
        1 << 18,
        (zabove, zbelow, ylow, yhigh),
    )
    yabove, ybelow = step(ylow, "gy", -1), step(yhigh, "gy", 1)

    xlow, xhigh, wide = kernel_call(
        pack_x_kernel,
        "pack_x",
        (f32(4 * HALO + 1, WIN, LANES), f32(4 * HALO + 1, WIN, LANES), f32(4, WIN, LANES)),
        1 << 18,
        (prev_disp, stiff_factor, edge, yabove, ybelow),
    )
    xabove, xbelow = step(xlow, "gx", -1), step(xhigh, "gx", 1)

    ext = cells_x + 2 * HALO
    (out,) = kernel_call(
        functools.partial(sweep_kernel, float(count_z)),
        "sweeps",
        (f32(3, cells_x, cells_y, LANES),),
        1 << 25,
        (prev_disp, stiff_factor, wide, yabove, ybelow, xabove, xbelow, shares),
        (
            pltpu.VMEM((2, 3, ext, ROWS, LANES), jnp.float32),
            pltpu.VMEM((ext, ROWS, LANES), jnp.float32),
            pltpu.VMEM((6, ext, WIN, LANES), jnp.float32),
            pltpu.VMEM((2, 3, 2, ROWS, LANES), jnp.float32),
            pltpu.VMEM((2, ROWS, LANES), jnp.float32),
            pltpu.VMEM((6, 2, WIN, LANES), jnp.float32),
            pltpu.VMEM((3, 2, WIN, LANES), jnp.float32),
        ),
    )
    return out


def solution(mesh):
    placed = (
        P(("gx", "gy", "gz"), None),
        P(("gx", "gy", "gz")),
        P("gx", "gy", "gz"),
        P(None, "gx", "gy", "gz"),
    )
    return jax.shard_map(
        body, mesh=mesh, in_specs=placed, out_specs=P(None, "gx", "gy", "gz"), check_vma=False
    )
```

time: 1830 us -> 90.9 us (0.05)
  blocking collectives: 1400 us -> 21.6 us
  other arithmetic: 122 us -> 0.01 us
  matrix products: 114 us -> 0 us
  local copies, waits for them, and re-layouts: 59.3 us -> 5.03 us
  starting transfers between devices: 88.3 us -> 35 us
  Pallas kernels: 0 us -> 21.3 us
    all_gather x1 -> x0, blocking collectives: 1400 us -> none  [body(): lax.all_gather(centre_coef, ('gx', 'gy', 'gz'), axis=0, tiled=True)]
    dot_general x128 -> x0, matrix products: 114 us -> none  [kernel_sum(): jnp.dot(coef.T, weights, precision=lax.Precision.HIGHEST, preferred_eleme...]
    div x385 -> x0, other arithmetic: 91.7 us -> none  [the longest x128 89.3 us: kernel_sum(): centre_x = ((index // count_y).astype(jnp.float32) + 0.5) / count_x]
    ppermute x24 -> x6, starting transfers between devices: 88.3 us -> 24.2 us  [step(): lax.ppermute(value, axis, [(i, i + by) for i in range(size) if 0 <= i + b...]
    slice x16 -> x0, local copies, waits for them, and re-layouts: 26.3 us -> none  [the longest x8 16.6 us: extended(): first = lax.slice_in_dim(shard, 0, width, axis=dim)]
    select_n x4 -> x0, other arithmetic: 22 us -> none  [the longest x3 22 us: relax_sweep(): updated = jnp.where(frozen, current, updated)]
    all_to_all x0 -> x1, blocking collectives: none -> 21.6 us  [body(): lax.all_to_all(jnp.broadcast_to(row, (blocks, 1, LANES)), ('gx', 'gy'), 0...]
    pallas_call x0 -> x5, Pallas kernels: none -> 21.3 us  [kernel_call(): pl.pallas_call(kernel, name=name, out_shape=outs, in_specs=[pl.BlockSpec(...]
  transfers between devices with their start and end apart: 25 -> 7, of which waited for: 4 -> 4; matrix products, arithmetic and copies ran while one was open for 13% -> 0% of each run, Pallas kernels for 0% -> 3%
where the time goes in v1:
time: 90.9 us; the launch traced here: 90.4 us
  starting transfers between devices  35 us (39%)
  blocking collectives  21.6 us (24%)
  Pallas kernels  21.3 us (23%)
  waiting for transfers between devices  7.22 us (8%)
  local copies, waits for them, and re-layouts  5.03 us (6%)
    ppermute x6, starting transfers between devices, step(): lax.ppermute(value, axis, [(i, i + by) for i in range(size) if 0 <= i + b...  24.2 us
    all_to_all x1, blocking collectives, body(): lax.all_to_all(jnp.broadcast_to(row, (blocks, 1, LANES)), ('gx', 'gy'), 0...  21.6 us
    pallas_call x5, Pallas kernels, kernel_call(): pl.pallas_call(kernel, name=name, out_shape=outs, in_specs=[pl.BlockSpec(...  21.3 us
    all_to_all x1, starting transfers between devices, body(): shares = lax.all_to_all(share, 'gz', 0, 0, tiled=True)  10.8 us
    unnamed x20, local copies, waits for them, and re-layouts  4.93 us
    ppermute x6, waiting for transfers between devices, step(): lax.ppermute(value, axis, [(i, i + by) for i in range(size) if 0 <= i + b...  4.23 us
    all_to_all x1, waiting for transfers between devices, body(): shares = lax.all_to_all(share, 'gz', 0, 0, tiled=True)  2.99 us
  transfers between devices with their start and end apart: 7, of which 4 were waited for; matrix products, arithmetic and copies ran while one was open for 0% of the time, Pallas kernels for 3%

profile of v1, /device:TPU:1, one launch (start us, length us, event | category | flops | bytes accessed | tf_op | source)
XLA Modules:
  0.0 90.4 jit_solution(14895367353659098823)
XLA Ops:
  0.0 1.4 %copy-done = f32[3,16,64,128]{3,2,1,0:T(8,128)S(1)} copy-done((f32[3,16,64,128]{3,2,1,0:T(8,128)S(1)}, f32[3,16,64,128]{3,2,1,0:T(8,128)}, u32[]{:S(2)}) %copy-start) | copy-done | bytes 1572888
  1.4 1.0 %copy-done.2 = f32[16,64,128]{2,1,0:T(8,128)S(1)} copy-done((f32[16,64,128]{2,1,0:T(8,128)S(1)}, f32[16,64,128]{2,1,0:T(8,128)}, u32[]{:S(2)}) %copy-start.2) | copy-done | bytes 524312
  2.5 1.1 %pack_z.1 = (f32[2,64,128]{2,1,0:T(8,128)S(1)}, f32[2,64,128]{2,1,0:T(8,128)S(1)}, f32[192,128]{1,0:T(8,128)S(1)}, f32[192,128]{1,0:T(8,128)S(1)}) custom-call(f32[3,16,64,128]{3,2,1,0:T(8,128)S(1)} %copy-done, f32[16,64,128]{2,1,0:T(8,128)S(1)} %copy-done.2), custom_call_target="tpu_custom_call" | custom-call | flops 2097152 | bytes 2424832 | tf_op jit(solution)/shard_map/pack_z/pallas_call | solution.py:37
  3.6 1.3 %collective-permute-start = (f32[2,64,128]{2,1,0:T(8,128)S(1)}, f32[2,64,128]{2,1,0:T(8,128)S(1)}, u32[]{:S(2)}, u32[]{:S(2)}) collective-permute-start(f32[2,64,128]{2,1,0:T(8,128)S(1)} %get-tuple-element.15), channel_id=1, source_target_pairs={{1,0},{2,1},{3,2},{4,3},{5,4},{6,5},{7,6},{9,8},{10,9},{11,10},{12... | collective-permute-start | bytes 196616 | tf_op jit(solution)/shard_map/ppermute | solution.py:381
  4.9 12.1 %collective-permute-start.1 = (f32[2,64,128]{2,1,0:T(8,128)S(1)}, f32[2,64,128]{2,1,0:T(8,128)S(1)}, u32[]{:S(2)}, u32[]{:S(2)}) collective-permute-start(f32[2,64,128]{2,1,0:T(8,128)S(1)} %get-tuple-element.16), channel_id=1, source_target_pairs={{0,1},{1,2},{2,3},{3,4},{4,5},{5,6},{6,7},{8,9},{9,10},{10,11},{11... | collective-permute-start | bytes 196616 | tf_op jit(solution)/shard_map/ppermute | solution.py:381
  17.0 0.0 copy-done.9
  17.0 0.0 collective-permute-done.above_ref
  17.0 1.3 %collective-permute-done.1.below_ref = f32[2,64,128]{2,1,0:T(8,128)S(1)} collective-permute-done((f32[2,64,128]{2,1,0:T(8,128)S(1)}, f32[2,64,128]{2,1,0:T(8,128)S(1)}, u32[]{:S(2)}, u32[]{:S(2)}) %collective-permute-start.1) | collective-permute-done | bytes 65568 | tf_op jit(solution)/shard_map/ppermute | solution.py:381
  18.3 0.1 pack_y.1
  18.4 1.3 %collective-permute-start.2 = (f32[208,128]{1,0:T(8,128)S(1)}, f32[208,128]{1,0:T(8,128)S(1)}, u32[]{:S(2)}, u32[]{:S(2)}) collective-permute-start(f32[208,128]{1,0:T(8,128)S(1)} %get-tuple-element.20), channel_id=1, source_target_pairs={{8,0},{16,8},{24,16},{9,1},{17,9},{25,17},{10,2},{18,10},{26,18},{... | collective-permute-start | bytes 319496 | tf_op jit(solution)/shard_map/ppermute | solution.py:381
  19.7 4.0 %collective-permute-start.3 = (f32[208,128]{1,0:T(8,128)S(1)}, f32[208,128]{1,0:T(8,128)S(1)}, u32[]{:S(2)}, u32[]{:S(2)}) collective-permute-start(f32[208,128]{1,0:T(8,128)S(1)} %get-tuple-element.21), channel_id=1, source_target_pairs={{0,8},{8,16},{16,24},{1,9},{9,17},{17,25},{2,10},{10,18},{18,26},{... | collective-permute-start | bytes 319496 | tf_op jit(solution)/shard_map/ppermute | solution.py:381
  23.7 0.0 copy-done.8
  23.7 0.1 broadcast_in_dim.11
  23.8 21.6 %all_to_all.10 = f32[64,1,128]{2,1,0:T(1,128)S(1)} all-to-all(f32[64,1,128]{2,1,0:T(1,128)S(1)} %broadcast_in_dim.12), channel_id=1, replica_groups=mesh['gx'=16,'gy'=4,'gz'=8] {'gx','gy'}, dimensions={0} | all-to-all | bytes 65536 | tf_op jit(solution)/shard_map/all_to_all | solution.py:393
  45.5 1.5 %rbf.1 = f32[8,72,128]{2,1,0:T(8,128)} custom-call(f32[64,128]{1,0:T(8,128)S(1)} %bitcast.4), custom_call_target="tpu_custom_call" | custom-call | flops 16777216 | bytes 327680 | tf_op jit(solution)/shard_map/rbf/pallas_call | solution.py:37
  47.0 10.8 %all-to-all-start.1 = ((f32[8,72,128]{2,1,0:T(8,128)}), f32[8,72,128]{2,1,0:T(8,128)S(1)}, u32[]{:S(2)}, u32[]{:S(2)}) async-start(f32[8,72,128]{2,1,0:T(8,128)} %rbf.1), calls=%async_computation.1 | async-start | bytes 589824 | tf_op jit(solution)/shard_map/all_to_all | solution.py:415
  57.7 0.0 collective-permute-done.2.yabove_ref
  57.7 0.0 collective-permute-done.3.ybelow_ref
  57.7 0.0 copy-start.4
  57.8 0.0 copy-done.1
  57.8 0.0 copy-done.3
  57.8 1.1 %pack_x.1 = (f32[13,72,128]{2,1,0:T(8,128)}, f32[13,72,128]{2,1,0:T(8,128)}, f32[4,72,128]{2,1,0:T(8,128)S(1)}) custom-call(f32[3,16,64,128]{3,2,1,0:T(8,128)S(1)} %copy-done.1, f32[16,64,128]{2,1,0:T(8,128)S(1)} %copy-done.3, f32[4,64,128]{2,1,0:T(8,128)S(1)} %get-tuple-element.19.edge_ref, f32[208,128]{1,0:T(8,128)S(1)} %collective-permute-done.2.yabove_ref, ...), custom_call_target="tpu_custom_call" | custom-call | flops 262144 | bytes 3547136 | tf_op jit(solution)/shard_map/pack_x/pallas_call | solution.py:37
  58.8 0.0 copy-done.4
  58.8 0.7 copy-done.6
  59.5 3.1 %collective-permute-start.4 = (f32[13,72,128]{2,1,0:T(8,128)}, f32[13,72,128]{2,1,0:T(8,128)S(1)}, u32[]{:S(2)}, u32[]{:S(2)}) collective-permute-start(f32[13,72,128]{2,1,0:T(8,128)} %get-tuple-element.23), channel_id=1, source_target_pairs={{32,0},{64,32},{96,64},{128,96},{160,128},{192,160},{224,192},{256... | collective-permute-start | bytes 1437704 | tf_op jit(solution)/shard_map/ppermute | solution.py:381
  62.6 2.4 %collective-permute-start.5 = (f32[13,72,128]{2,1,0:T(8,128)}, f32[13,72,128]{2,1,0:T(8,128)S(1)}, u32[]{:S(2)}, u32[]{:S(2)}) collective-permute-start(f32[13,72,128]{2,1,0:T(8,128)} %get-tuple-element.24), channel_id=1, source_target_pairs={{0,32},{32,64},{64,96},{96,128},{128,160},{160,192},{192,224},{224... | collective-permute-start | bytes 1437704 | tf_op jit(solution)/shard_map/ppermute | solution.py:381
  65.1 3.0 %all-to-all-done.1.rbf_ref = f32[8,72,128]{2,1,0:T(8,128)S(1)} async-done(((f32[8,72,128]{2,1,0:T(8,128)}), f32[8,72,128]{2,1,0:T(8,128)S(1)}, u32[]{:S(2)}, u32[]{:S(2)}) %all-to-all-start.1) | async-done | bytes 294944 | tf_op jit(solution)/shard_map/all_to_all | solution.py:415
  68.0 2.0 %collective-permute-done.4.xabove_ref = f32[13,72,128]{2,1,0:T(8,128)S(1)} collective-permute-done((f32[13,72,128]{2,1,0:T(8,128)}, f32[13,72,128]{2,1,0:T(8,128)S(1)}, u32[]{:S(2)}, u32[]{:S(2)}) %collective-permute-start.4) | collective-permute-done | bytes 479264 | tf_op jit(solution)/shard_map/ppermute | solution.py:381
  70.0 1.0 %collective-permute-done.5.xbelow_ref = f32[13,72,128]{2,1,0:T(8,128)S(1)} collective-permute-done((f32[13,72,128]{2,1,0:T(8,128)}, f32[13,72,128]{2,1,0:T(8,128)S(1)}, u32[]{:S(2)}, u32[]{:S(2)}) %collective-permute-start.5) | collective-permute-done | bytes 479264 | tf_op jit(solution)/shard_map/ppermute | solution.py:381
  71.0 0.9 copy-done.5
  71.9 0.9 %copy-done.7 = f32[4,72,128]{2,1,0:T(8,128)S(1)} copy-done((f32[4,72,128]{2,1,0:T(8,128)S(1)}, f32[4,72,128]{2,1,0:T(8,128)}, u32[]{:S(2)}) %copy-start.7) | copy-done | bytes 147480
  72.8 17.6 %sweeps.1 = f32[3,16,64,128]{3,2,1,0:T(8,128)} custom-call(f32[3,16,64,128]{3,2,1,0:T(8,128)S(1)} %copy-done.1, f32[16,64,128]{2,1,0:T(8,128)S(1)} %copy-done.3, f32[4,72,128]{2,1,0:T(8,128)S(1)} %copy-done.7, f32[208,128]{1,0:T(8,128)S(1)} %collective-permute-done.2.yabove_ref, f32[208,128]{1,0:T(8,128)S(1)} %copy-done.5, ...), custom_call_target="tpu_custom_call" | custom-call | flops 33554432 | bytes 5283840 | tf_op jit(solution)/shard_map/sweeps/pallas_call | solution.py:37
  (12 shorter events, 0.0 us)
Async XLA Ops:
  0.0 1.4 %copy-start = (f32[3,16,64,128]{3,2,1,0:T(8,128)S(1)}, f32[3,16,64,128]{3,2,1,0:T(8,128)}, u32[]{:S(2)}) copy-start(f32[3,16,64,128]{3,2,1,0:T(8,128)} %prev_ref.5) | copy-start | bytes 4718596
  1.4 1.0 %copy-start.2 = (f32[16,64,128]{2,1,0:T(8,128)S(1)}, f32[16,64,128]{2,1,0:T(8,128)}, u32[]{:S(2)}) copy-start(f32[16,64,128]{2,1,0:T(8,128)} %stiff_ref.5) | copy-start | bytes 1572868
  2.5 14.5 %copy-start.9 = (s32[32]{0:T(128)S(1)}, s32[32]{0:T(128)}, u32[]{:S(2)}) copy-start(s32[32]{0:T(128)} %param.5) | copy-start | bytes 388
  2.5 21.3 %copy-start.8 = (f32[32,3]{0,1:T(4,128)S(1)}, f32[32,3]{0,1:T(4,128)}, u32[]{:S(2)}) copy-start(f32[32,3]{0,1:T(4,128)} %param.4) | copy-start | bytes 1156
  2.5 55.3 %copy-start.1 = (f32[3,16,64,128]{3,2,1,0:T(8,128)S(1)}, f32[3,16,64,128]{3,2,1,0:T(8,128)}, u32[]{:S(2)}) copy-start(f32[3,16,64,128]{3,2,1,0:T(8,128)} %prev_ref.5) | copy-start | bytes 4718596
  2.5 55.3 %copy-start.3 = (f32[16,64,128]{2,1,0:T(8,128)S(1)}, f32[16,64,128]{2,1,0:T(8,128)}, u32[]{:S(2)}) copy-start(f32[16,64,128]{2,1,0:T(8,128)} %stiff_ref.5) | copy-start | bytes 1572868
  3.6 13.4 %collective-permute-start = (f32[2,64,128]{2,1,0:T(8,128)S(1)}, f32[2,64,128]{2,1,0:T(8,128)S(1)}, u32[]{:S(2)}, u32[]{:S(2)}) collective-permute-start(f32[2,64,128]{2,1,0:T(8,128)S(1)} %get-tuple-element.15), channel_id=1, source_target_pairs={{1,0},{2,1},{3,2},{4,3},{5,4},{6,5},{7,6},{9,8},{10,9},{11,10},{12... | collective-permute-start | bytes 196616 | tf_op jit(solution)/shard_map/ppermute | solution.py:381
  4.9 13.4 %collective-permute-start.1 = (f32[2,64,128]{2,1,0:T(8,128)S(1)}, f32[2,64,128]{2,1,0:T(8,128)S(1)}, u32[]{:S(2)}, u32[]{:S(2)}) collective-permute-start(f32[2,64,128]{2,1,0:T(8,128)S(1)} %get-tuple-element.16), channel_id=1, source_target_pairs={{0,1},{1,2},{2,3},{3,4},{4,5},{5,6},{6,7},{8,9},{9,10},{10,11},{11... | collective-permute-start | bytes 196616 | tf_op jit(solution)/shard_map/ppermute | solution.py:381
  18.4 39.3 %collective-permute-start.2 = (f32[208,128]{1,0:T(8,128)S(1)}, f32[208,128]{1,0:T(8,128)S(1)}, u32[]{:S(2)}, u32[]{:S(2)}) collective-permute-start(f32[208,128]{1,0:T(8,128)S(1)} %get-tuple-element.20), channel_id=1, source_target_pairs={{8,0},{16,8},{24,16},{9,1},{17,9},{25,17},{10,2},{18,10},{26,18},{... | collective-permute-start | bytes 319496 | tf_op jit(solution)/shard_map/ppermute | solution.py:381
  19.7 38.0 %collective-permute-start.3 = (f32[208,128]{1,0:T(8,128)S(1)}, f32[208,128]{1,0:T(8,128)S(1)}, u32[]{:S(2)}, u32[]{:S(2)}) collective-permute-start(f32[208,128]{1,0:T(8,128)S(1)} %get-tuple-element.21), channel_id=1, source_target_pairs={{0,8},{8,16},{16,24},{1,9},{9,17},{17,25},{2,10},{10,18},{18,26},{... | collective-permute-start | bytes 319496 | tf_op jit(solution)/shard_map/ppermute | solution.py:381
  47.0 21.1 %all-to-all-start.1 = ((f32[8,72,128]{2,1,0:T(8,128)}), f32[8,72,128]{2,1,0:T(8,128)S(1)}, u32[]{:S(2)}, u32[]{:S(2)}) async-start(f32[8,72,128]{2,1,0:T(8,128)} %rbf.1), calls=%async_computation.1 | async-start | bytes 589824 | tf_op jit(solution)/shard_map/all_to_all | solution.py:415
  57.7 1.1 %copy-start.4 = (f32[208,128]{1,0:T(8,128)}, f32[208,128]{1,0:T(8,128)S(1)}, u32[]{:S(2)}) copy-start(f32[208,128]{1,0:T(8,128)S(1)} %collective-permute-done.3.ybelow_ref) | copy-start | bytes 319492
  58.8 0.7 copy-start.6
  59.5 10.5 %collective-permute-start.4 = (f32[13,72,128]{2,1,0:T(8,128)}, f32[13,72,128]{2,1,0:T(8,128)S(1)}, u32[]{:S(2)}, u32[]{:S(2)}) collective-permute-start(f32[13,72,128]{2,1,0:T(8,128)} %get-tuple-element.23), channel_id=1, source_target_pairs={{32,0},{64,32},{96,64},{128,96},{160,128},{192,160},{224,192},{256... | collective-permute-start | bytes 1437704 | tf_op jit(solution)/shard_map/ppermute | solution.py:381
  62.6 8.4 %collective-permute-start.5 = (f32[13,72,128]{2,1,0:T(8,128)}, f32[13,72,128]{2,1,0:T(8,128)S(1)}, u32[]{:S(2)}, u32[]{:S(2)}) collective-permute-start(f32[13,72,128]{2,1,0:T(8,128)} %get-tuple-element.24), channel_id=1, source_target_pairs={{0,32},{32,64},{64,96},{96,128},{128,160},{160,192},{192,224},{224... | collective-permute-start | bytes 1437704 | tf_op jit(solution)/shard_map/ppermute | solution.py:381
  71.0 0.9 copy-start.5
  71.9 0.9 %copy-start.7 = (f32[4,72,128]{2,1,0:T(8,128)S(1)}, f32[4,72,128]{2,1,0:T(8,128)}, u32[]{:S(2)}) copy-start(f32[4,72,128]{2,1,0:T(8,128)} %copy-done.6) | copy-start | bytes 442372

commit v2 on v1

--- a/solution.py
+++ b/solution.py
@@ -17,7 +17,7 @@
 WIN = 72
 ROWS = 88
 LANES = 128
-VMEM_LIMIT = 40 * 1024 * 1024
+VMEM_LIMIT = 20 * 1024 * 1024
 
 
 def lane_ids(rows=WIN):
@@ -32,18 +32,18 @@
     return pltpu.roll(value, shift, 1)
 
 
-def kernel_call(kernel, name, outs, flops, args, scratch=()):
+def kernel_call(kernel, name, outs, flops, args, scratch=(), after=(), limit=VMEM_LIMIT):
     moved = sum(math.prod(a.shape) * 4 for a in (*args, *outs))
     return pl.pallas_call(
         kernel,
         name=name,
         out_shape=outs,
-        in_specs=[pl.BlockSpec(memory_space=pltpu.VMEM)] * len(args),
+        in_specs=[pl.BlockSpec(memory_space=pltpu.VMEM)] * len(args) + [pl.BlockSpec(memory_space=pl.ANY)] * len(after),
         out_specs=tuple(pl.BlockSpec(memory_space=pltpu.VMEM) for _ in outs),
         scratch_shapes=list(scratch),
-        compiler_params=pltpu.CompilerParams(vmem_limit_bytes=VMEM_LIMIT),
+        compiler_params=pltpu.CompilerParams(vmem_limit_bytes=limit),
         cost_estimate=pl.CostEstimate(flops=flops, bytes_accessed=moved, transcendentals=0),
-    )(*args)
+    )(*args, *after)
 
 
 def f32(*shape):
@@ -80,7 +80,7 @@
                 yhigh_ref[at, :] = stiff_ref[x, cells_y - HALO :, :]
 
 
-def pack_y_kernel(above_ref, below_ref, ylow_ref, yhigh_ref, edge_ref, outlow_ref, outhigh_ref):
+def pack_y_kernel(above_ref, below_ref, ylow_ref, yhigh_ref, _, edge_ref, outlow_ref, outhigh_ref):
     rows = above_ref.shape[1]
     place = lane_ids(rows) % 8
     upper = (place >= 1) & (place <= 3)
@@ -288,7 +288,7 @@
                 u_ref[0, ch, x, window, :] = jnp.where(own, column, u_ref[0, ch, x, window, :])
             return carry
 
-        lax.fori_loop(0, ext, layer, 0)
+        lax.fori_loop(0, ext, layer, 0, unroll=11)
 
     def spot(x):
         return ((x + 13) // 16 + 1) % 2, (x + 13) % 16
@@ -320,7 +320,7 @@
         c_ref[0, tile] = jnp.where(at_edge(g), pltpu.roll(own, 8 * g + 4, 1), c_ref[0, tile])
         return carry
 
-    lax.fori_loop(1, ext - 1, weigh, 0)
+    lax.fori_loop(1, ext - 1, weigh, 0, unroll=4)
 
     def edge_neighbours(ref, tile, middle):
         own, other = ref[tile, window, :], ref[1 - tile, window, :]
@@ -365,7 +365,7 @@
                     c_ref[ch, tile] = jnp.where(at_edge(g), pltpu.roll(own, 8 * g + 4, 1), c_ref[ch, tile])
             return carry
 
-        lax.fori_loop(1 + sweep, ext - 1 - sweep, relax, 0)
+        lax.fori_loop(1 + sweep, ext - 1 - sweep, relax, 0, unroll=4)
         if not last:
             for ch in range(3):
                 for tile in range(2):
@@ -421,6 +421,7 @@
         (f32(4, cells_y, LANES), f32(rows_all, LANES), f32(rows_all, LANES)),
         1 << 18,
         (zabove, zbelow, ylow, yhigh),
+        after=(share,),
     )
     yabove, ybelow = step(ylow, "gy", -1), step(yhigh, "gy", 1)
 

time: 90.9 us -> 79.5 us (0.87)
  blocking collectives: 21.6 us -> 0 us
  starting transfers between devices: 35 us -> 48.4 us
  Pallas kernels: 21.3 us -> 16.1 us
  other arithmetic: 0.01 us -> 1.35 us
    all_to_all x1 -> x0, blocking collectives: 21.6 us -> none  [body(): lax.all_to_all(jnp.broadcast_to(row, (blocks, 1, LANES)), ('gx', 'gy'), 0...]
    all_to_all x0 -> x1, starting transfers between devices: none -> 14.6 us  [body(): lax.all_to_all(jnp.broadcast_to(row, (blocks, 1, LANES)), ('gx', 'gy'), 0...]
    pallas_call x5, Pallas kernels: 21.3 us -> 16.1 us  [kernel_call(): pl.pallas_call(kernel, name=name, out_shape=outs, in_specs=[pl.BlockSpec(...]
    ppermute x6, starting transfers between devices: 24.2 us -> 21.8 us  [step(): lax.ppermute(value, axis, [(i, i + by) for i in range(size) if 0 <= i + b...]
    all_to_all x1, starting transfers between devices: 10.8 us -> 12 us  [body(): shares = lax.all_to_all(share, 'gz', 0, 0, tiled=True)]
    all_to_all x1, waiting for transfers between devices: 2.99 us -> 1.85 us  [body(): shares = lax.all_to_all(share, 'gz', 0, 0, tiled=True)]
    unnamed x20 -> x16, local copies, waits for them, and re-layouts: 4.93 us -> 4.92 us
  transfers between devices with their start and end apart: 7 -> 8, of which waited for: 4 -> 4; matrix products, arithmetic and copies ran while one was open for 0% -> 0% of each run, Pallas kernels for 3% -> 5%
where the time goes in v2:
time: 79.5 us; the launch traced here: 78.3 us
  starting transfers between devices  48.4 us (61%)
  Pallas kernels  16.1 us (20%)
  waiting for transfers between devices  6.73 us (8%)
  local copies, waits for them, and re-layouts  5.64 us (7%)
  other arithmetic  1.35 us (2%)
    ppermute x6, starting transfers between devices, step(): lax.ppermute(value, axis, [(i, i + by) for i in range(size) if 0 <= i + b...  21.8 us
    pallas_call x5, Pallas kernels, kernel_call(): pl.pallas_call(kernel, name=name, out_shape=outs, in_specs=[pl.BlockSpec(...  16.1 us
    all_to_all x1, starting transfers between devices, body(): lax.all_to_all(jnp.broadcast_to(row, (blocks, 1, LANES)), ('gx', 'gy'), 0...  14.6 us
    all_to_all x1, starting transfers between devices, body(): shares = lax.all_to_all(share, 'gz', 0, 0, tiled=True)  12 us
    unnamed x16, local copies, waits for them, and re-layouts  4.92 us
    ppermute x6, waiting for transfers between devices, step(): lax.ppermute(value, axis, [(i, i + by) for i in range(size) if 0 <= i + b...  4.88 us
    all_to_all x1, waiting for transfers between devices, body(): shares = lax.all_to_all(share, 'gz', 0, 0, tiled=True)  1.85 us
  transfers between devices with their start and end apart: 8, of which 4 were waited for; matrix products, arithmetic and copies ran while one was open for 0% of the time, Pallas kernels for 5%

profile of v2, /device:TPU:1, one launch (start us, length us, event | category | flops | bytes accessed | tf_op | source)
XLA Modules:
  0.0 78.3 jit_solution(1730218775912394689)
XLA Ops:
  0.0 0.7 convert_bitcast_fusion
  0.7 0.7 pad_maximum_fusion
  1.3 0.1 broadcast_in_dim.11
  1.4 0.6 broadcast_in_dim.12
  2.1 14.6 %all-to-all-start = ((f32[64,1,128]{2,1,0:T(1,128)}), f32[64,1,128]{2,1,0:T(1,128)S(1)}, u32[]{:S(2)}, u32[]{:S(2)}) async-start(f32[64,1,128]{2,1,0:T(1,128)} %broadcast_in_dim.12), calls=%async_computation | async-start | bytes 65536 | tf_op jit(solution)/shard_map/all_to_all | solution.py:393
  16.7 0.0 copy-start
  16.7 1.4 %copy-done = f32[3,16,64,128]{3,2,1,0:T(8,128)S(1)} copy-done((f32[3,16,64,128]{3,2,1,0:T(8,128)S(1)}, f32[3,16,64,128]{3,2,1,0:T(8,128)}, u32[]{:S(2)}) %copy-start) | copy-done | bytes 1572888
  18.1 1.0 %copy-done.2 = f32[16,64,128]{2,1,0:T(8,128)S(1)} copy-done((f32[16,64,128]{2,1,0:T(8,128)S(1)}, f32[16,64,128]{2,1,0:T(8,128)}, u32[]{:S(2)}) %copy-start.2) | copy-done | bytes 524312
  19.1 1.1 %pack_z.1 = (f32[2,64,128]{2,1,0:T(8,128)S(1)}, f32[2,64,128]{2,1,0:T(8,128)S(1)}, f32[192,128]{1,0:T(8,128)S(1)}, f32[192,128]{1,0:T(8,128)S(1)}) custom-call(f32[3,16,64,128]{3,2,1,0:T(8,128)S(1)} %copy-done, f32[16,64,128]{2,1,0:T(8,128)S(1)} %copy-done.2), custom_call_target="tpu_custom_call" | custom-call | flops 2097152 | bytes 2424832 | tf_op jit(solution)/shard_map/pack_z/pallas_call | solution.py:37
  20.3 1.3 %collective-permute-start = (f32[2,64,128]{2,1,0:T(8,128)S(1)}, f32[2,64,128]{2,1,0:T(8,128)S(1)}, u32[]{:S(2)}, u32[]{:S(2)}) collective-permute-start(f32[2,64,128]{2,1,0:T(8,128)S(1)} %get-tuple-element.15), channel_id=1, source_target_pairs={{1,0},{2,1},{3,2},{4,3},{5,4},{6,5},{7,6},{9,8},{10,9},{11,10},{12... | collective-permute-start | bytes 196616 | tf_op jit(solution)/shard_map/ppermute | solution.py:381
  21.5 8.6 %collective-permute-start.1 = (f32[2,64,128]{2,1,0:T(8,128)S(1)}, f32[2,64,128]{2,1,0:T(8,128)S(1)}, u32[]{:S(2)}, u32[]{:S(2)}) collective-permute-start(f32[2,64,128]{2,1,0:T(8,128)S(1)} %get-tuple-element.16), channel_id=1, source_target_pairs={{0,1},{1,2},{2,3},{3,4},{4,5},{5,6},{6,7},{8,9},{9,10},{10,11},{11... | collective-permute-start | bytes 196616 | tf_op jit(solution)/shard_map/ppermute | solution.py:381
  30.1 0.0 all-to-all-done
  30.1 1.5 %rbf.1._ = f32[8,72,128]{2,1,0:T(8,128)} custom-call(f32[64,128]{1,0:T(8,128)S(1)} %bitcast.4), custom_call_target="tpu_custom_call" | custom-call | flops 16777216 | bytes 327680 | tf_op jit(solution)/shard_map/rbf/pallas_call | solution.py:37
  31.6 0.0 collective-permute-done.above_ref
  31.6 0.8 collective-permute-done.1.below_ref
  32.4 0.1 pack_y.1
  32.5 1.3 %collective-permute-start.2 = (f32[208,128]{1,0:T(8,128)S(1)}, f32[208,128]{1,0:T(8,128)S(1)}, u32[]{:S(2)}, u32[]{:S(2)}) collective-permute-start(f32[208,128]{1,0:T(8,128)S(1)} %get-tuple-element.20), channel_id=1, source_target_pairs={{8,0},{16,8},{24,16},{9,1},{17,9},{25,17},{10,2},{18,10},{26,18},{... | collective-permute-start | bytes 319496 | tf_op jit(solution)/shard_map/ppermute | solution.py:381
  33.8 4.0 %collective-permute-start.3 = (f32[208,128]{1,0:T(8,128)S(1)}, f32[208,128]{1,0:T(8,128)S(1)}, u32[]{:S(2)}, u32[]{:S(2)}) collective-permute-start(f32[208,128]{1,0:T(8,128)S(1)} %get-tuple-element.21), channel_id=1, source_target_pairs={{0,8},{8,16},{16,24},{1,9},{9,17},{17,25},{2,10},{10,18},{18,26},{... | collective-permute-start | bytes 319496 | tf_op jit(solution)/shard_map/ppermute | solution.py:381
  37.8 12.0 %all-to-all-start.1 = ((f32[8,72,128]{2,1,0:T(8,128)}), f32[8,72,128]{2,1,0:T(8,128)S(1)}, u32[]{:S(2)}, u32[]{:S(2)}) async-start(f32[8,72,128]{2,1,0:T(8,128)} %rbf.1._), calls=%async_computation.1 | async-start | bytes 589824 | tf_op jit(solution)/shard_map/all_to_all | solution.py:415
  49.8 0.0 collective-permute-done.2.yabove_ref
  49.8 0.0 collective-permute-done.3.ybelow_ref
  49.8 0.0 copy-start.4
  49.8 1.1 %pack_x.1 = (f32[13,72,128]{2,1,0:T(8,128)}, f32[13,72,128]{2,1,0:T(8,128)}, f32[4,72,128]{2,1,0:T(8,128)S(1)}) custom-call(f32[3,16,64,128]{3,2,1,0:T(8,128)S(1)} %copy-done.1, f32[16,64,128]{2,1,0:T(8,128)S(1)} %copy-done.3, f32[4,64,128]{2,1,0:T(8,128)S(1)} %get-tuple-element.19.edge_ref, f32[208,128]{1,0:T(8,128)S(1)} %collective-permute-done.2.yabove_ref, ...), custom_call_target="tpu_custom_call" | custom-call | flops 262144 | bytes 3547136 | tf_op jit(solution)/shard_map/pack_x/pallas_call | solution.py:37
  50.9 0.7 copy-done.6
  51.5 3.5 %collective-permute-start.4 = (f32[13,72,128]{2,1,0:T(8,128)}, f32[13,72,128]{2,1,0:T(8,128)S(1)}, u32[]{:S(2)}, u32[]{:S(2)}) collective-permute-start(f32[13,72,128]{2,1,0:T(8,128)} %get-tuple-element.23), channel_id=1, source_target_pairs={{32,0},{64,32},{96,64},{128,96},{160,128},{192,160},{224,192},{256... | collective-permute-start | bytes 1437704 | tf_op jit(solution)/shard_map/ppermute | solution.py:381
  55.0 3.2 %collective-permute-start.5 = (f32[13,72,128]{2,1,0:T(8,128)}, f32[13,72,128]{2,1,0:T(8,128)S(1)}, u32[]{:S(2)}, u32[]{:S(2)}) collective-permute-start(f32[13,72,128]{2,1,0:T(8,128)} %get-tuple-element.24), channel_id=1, source_target_pairs={{0,32},{32,64},{64,96},{96,128},{128,160},{160,192},{192,224},{224... | collective-permute-start | bytes 1437704 | tf_op jit(solution)/shard_map/ppermute | solution.py:381
  58.2 1.8 %all-to-all-done.1.rbf_ref = f32[8,72,128]{2,1,0:T(8,128)S(1)} async-done(((f32[8,72,128]{2,1,0:T(8,128)}), f32[8,72,128]{2,1,0:T(8,128)S(1)}, u32[]{:S(2)}, u32[]{:S(2)}) %all-to-all-start.1) | async-done | bytes 294944 | tf_op jit(solution)/shard_map/all_to_all | solution.py:415
  60.1 2.8 %collective-permute-done.4.xabove_ref = f32[13,72,128]{2,1,0:T(8,128)S(1)} collective-permute-done((f32[13,72,128]{2,1,0:T(8,128)}, f32[13,72,128]{2,1,0:T(8,128)S(1)}, u32[]{:S(2)}, u32[]{:S(2)}) %collective-permute-start.4) | collective-permute-done | bytes 479264 | tf_op jit(solution)/shard_map/ppermute | solution.py:381
  62.9 1.3 %collective-permute-done.5.xbelow_ref = f32[13,72,128]{2,1,0:T(8,128)S(1)} collective-permute-done((f32[13,72,128]{2,1,0:T(8,128)}, f32[13,72,128]{2,1,0:T(8,128)S(1)}, u32[]{:S(2)}, u32[]{:S(2)}) %collective-permute-start.5) | collective-permute-done | bytes 479264 | tf_op jit(solution)/shard_map/ppermute | solution.py:381
  64.2 0.9 %copy-done.5 = f32[208,128]{1,0:T(8,128)S(1)} copy-done((f32[208,128]{1,0:T(8,128)S(1)}, f32[208,128]{1,0:T(8,128)}, u32[]{:S(2)}) %copy-start.5) | copy-done | bytes 106520
  65.1 0.9 %copy-done.7 = f32[4,72,128]{2,1,0:T(8,128)S(1)} copy-done((f32[4,72,128]{2,1,0:T(8,128)S(1)}, f32[4,72,128]{2,1,0:T(8,128)}, u32[]{:S(2)}) %copy-start.7) | copy-done | bytes 147480
  66.0 12.3 %sweeps.1 = f32[3,16,64,128]{3,2,1,0:T(8,128)} custom-call(f32[3,16,64,128]{3,2,1,0:T(8,128)S(1)} %copy-done.1, f32[16,64,128]{2,1,0:T(8,128)S(1)} %copy-done.3, f32[4,72,128]{2,1,0:T(8,128)S(1)} %copy-done.7, f32[208,128]{1,0:T(8,128)S(1)} %collective-permute-done.2.yabove_ref, f32[208,128]{1,0:T(8,128)S(1)} %copy-done.5, ...), custom_call_target="tpu_custom_call" | custom-call | flops 33554432 | bytes 5283840 | tf_op jit(solution)/shard_map/sweeps/pallas_call | solution.py:37
  (9 shorter events, 0.0 us)
Async XLA Ops:
  2.1 28.1 %all-to-all-start = ((f32[64,1,128]{2,1,0:T(1,128)}), f32[64,1,128]{2,1,0:T(1,128)S(1)}, u32[]{:S(2)}, u32[]{:S(2)}) async-start(f32[64,1,128]{2,1,0:T(1,128)} %broadcast_in_dim.12), calls=%async_computation | async-start | bytes 65536 | tf_op jit(solution)/shard_map/all_to_all | solution.py:393
  16.7 1.4 %copy-start = (f32[3,16,64,128]{3,2,1,0:T(8,128)S(1)}, f32[3,16,64,128]{3,2,1,0:T(8,128)}, u32[]{:S(2)}) copy-start(f32[3,16,64,128]{3,2,1,0:T(8,128)} %prev_ref.5) | copy-start | bytes 4718596
  18.1 1.0 %copy-start.2 = (f32[16,64,128]{2,1,0:T(8,128)S(1)}, f32[16,64,128]{2,1,0:T(8,128)}, u32[]{:S(2)}) copy-start(f32[16,64,128]{2,1,0:T(8,128)} %stiff_ref.5) | copy-start | bytes 1572868
  19.1 30.7 %copy-start.1 = (f32[3,16,64,128]{3,2,1,0:T(8,128)S(1)}, f32[3,16,64,128]{3,2,1,0:T(8,128)}, u32[]{:S(2)}) copy-start(f32[3,16,64,128]{3,2,1,0:T(8,128)} %prev_ref.5) | copy-start | bytes 4718596
  19.1 30.7 %copy-start.3 = (f32[16,64,128]{2,1,0:T(8,128)S(1)}, f32[16,64,128]{2,1,0:T(8,128)}, u32[]{:S(2)}) copy-start(f32[16,64,128]{2,1,0:T(8,128)} %stiff_ref.5) | copy-start | bytes 1572868
  20.3 11.3 %collective-permute-start = (f32[2,64,128]{2,1,0:T(8,128)S(1)}, f32[2,64,128]{2,1,0:T(8,128)S(1)}, u32[]{:S(2)}, u32[]{:S(2)}) collective-permute-start(f32[2,64,128]{2,1,0:T(8,128)S(1)} %get-tuple-element.15), channel_id=1, source_target_pairs={{1,0},{2,1},{3,2},{4,3},{5,4},{6,5},{7,6},{9,8},{10,9},{11,10},{12... | collective-permute-start | bytes 196616 | tf_op jit(solution)/shard_map/ppermute | solution.py:381
  21.5 10.8 %collective-permute-start.1 = (f32[2,64,128]{2,1,0:T(8,128)S(1)}, f32[2,64,128]{2,1,0:T(8,128)S(1)}, u32[]{:S(2)}, u32[]{:S(2)}) collective-permute-start(f32[2,64,128]{2,1,0:T(8,128)S(1)} %get-tuple-element.16), channel_id=1, source_target_pairs={{0,1},{1,2},{2,3},{3,4},{4,5},{5,6},{6,7},{8,9},{9,10},{10,11},{11... | collective-permute-start | bytes 196616 | tf_op jit(solution)/shard_map/ppermute | solution.py:381
  32.5 17.3 %collective-permute-start.2 = (f32[208,128]{1,0:T(8,128)S(1)}, f32[208,128]{1,0:T(8,128)S(1)}, u32[]{:S(2)}, u32[]{:S(2)}) collective-permute-start(f32[208,128]{1,0:T(8,128)S(1)} %get-tuple-element.20), channel_id=1, source_target_pairs={{8,0},{16,8},{24,16},{9,1},{17,9},{25,17},{10,2},{18,10},{26,18},{... | collective-permute-start | bytes 319496 | tf_op jit(solution)/shard_map/ppermute | solution.py:381
  33.8 16.0 %collective-permute-start.3 = (f32[208,128]{1,0:T(8,128)S(1)}, f32[208,128]{1,0:T(8,128)S(1)}, u32[]{:S(2)}, u32[]{:S(2)}) collective-permute-start(f32[208,128]{1,0:T(8,128)S(1)} %get-tuple-element.21), channel_id=1, source_target_pairs={{0,8},{8,16},{16,24},{1,9},{9,17},{17,25},{2,10},{10,18},{18,26},{... | collective-permute-start | bytes 319496 | tf_op jit(solution)/shard_map/ppermute | solution.py:381
  37.8 22.3 %all-to-all-start.1 = ((f32[8,72,128]{2,1,0:T(8,128)}), f32[8,72,128]{2,1,0:T(8,128)S(1)}, u32[]{:S(2)}, u32[]{:S(2)}) async-start(f32[8,72,128]{2,1,0:T(8,128)} %rbf.1._), calls=%async_computation.1 | async-start | bytes 589824 | tf_op jit(solution)/shard_map/all_to_all | solution.py:415
  49.8 1.1 %copy-start.4 = (f32[208,128]{1,0:T(8,128)}, f32[208,128]{1,0:T(8,128)S(1)}, u32[]{:S(2)}) copy-start(f32[208,128]{1,0:T(8,128)S(1)} %collective-permute-done.3.ybelow_ref) | copy-start | bytes 319492
  50.9 0.7 copy-start.6
  51.5 11.4 %collective-permute-start.4 = (f32[13,72,128]{2,1,0:T(8,128)}, f32[13,72,128]{2,1,0:T(8,128)S(1)}, u32[]{:S(2)}, u32[]{:S(2)}) collective-permute-start(f32[13,72,128]{2,1,0:T(8,128)} %get-tuple-element.23), channel_id=1, source_target_pairs={{32,0},{64,32},{96,64},{128,96},{160,128},{192,160},{224,192},{256... | collective-permute-start | bytes 1437704 | tf_op jit(solution)/shard_map/ppermute | solution.py:381
  55.0 9.1 %collective-permute-start.5 = (f32[13,72,128]{2,1,0:T(8,128)}, f32[13,72,128]{2,1,0:T(8,128)S(1)}, u32[]{:S(2)}, u32[]{:S(2)}) collective-permute-start(f32[13,72,128]{2,1,0:T(8,128)} %get-tuple-element.24), channel_id=1, source_target_pairs={{0,32},{32,64},{64,96},{96,128},{128,160},{160,192},{192,224},{224... | collective-permute-start | bytes 1437704 | tf_op jit(solution)/shard_map/ppermute | solution.py:381
  64.2 0.9 %copy-start.5 = (f32[208,128]{1,0:T(8,128)S(1)}, f32[208,128]{1,0:T(8,128)}, u32[]{:S(2)}) copy-start(f32[208,128]{1,0:T(8,128)} %copy-done.4) | copy-start | bytes 319492
  65.1 0.9 %copy-start.7 = (f32[4,72,128]{2,1,0:T(8,128)S(1)}, f32[4,72,128]{2,1,0:T(8,128)}, u32[]{:S(2)}) copy-start(f32[4,72,128]{2,1,0:T(8,128)} %copy-done.6) | copy-start | bytes 442372

commit v3 on v2

v3 whole, which is shorter than its diff:
```python
import functools
import math

import jax
import jax.numpy as jnp
from jax import lax
from jax.experimental import pallas as pl
from jax.experimental.pallas import tpu as pltpu
from jax.sharding import PartitionSpec as P

SWEEPS = 3
RADIUS = 0.02
OMEGA = 0.8

HALO = 3
TOP = 8
WIN = 72
HALF = 40
ROWS = 88
LANES = 128
MEGA = 1_100_000
VMEM_LIMIT = 16 * 1024 * 1024


def lane_ids(rows=WIN):
    return lax.broadcasted_iota(jnp.int32, (rows, LANES), 1)


def roll_lanes(value, shift):
    if not isinstance(shift, int):
        return pltpu.roll(value, shift % LANES, 1)
    return pltpu.roll(value, shift % LANES, 1) if shift % LANES else value


def kernel_call(kernel, name, outs, flops, args, scratch=(), after=(), far=(), aliases=None):
    moved = sum(math.prod(a.shape) * 4 for a in (*args, *outs))
    anywhere = pl.BlockSpec(memory_space=pl.ANY)
    return pl.pallas_call(
        kernel,
        name=name,
        out_shape=outs,
        in_specs=[pl.BlockSpec(memory_space=pltpu.VMEM)] * len(args) + [anywhere] * (len(far) + len(after)),
        out_specs=tuple(anywhere if isinstance(o, Far) else pl.BlockSpec(memory_space=pltpu.VMEM) for o in outs),
        scratch_shapes=list(scratch),
        input_output_aliases=aliases or {},
        compiler_params=pltpu.CompilerParams(vmem_limit_bytes=VMEM_LIMIT),
        cost_estimate=pl.CostEstimate(flops=flops, bytes_accessed=moved, transcendentals=0),
    )(*args, *far, *after)


class Far(jax.ShapeDtypeStruct):
    pass


def f32(*shape):
    return jax.ShapeDtypeStruct(shape, jnp.float32)


def near(*shape):
    return pltpu.VMEM(shape, jnp.float32)


def wall_scale(count_z, cells_z):
    deep = (lax.axis_index("gz") * cells_z + lane_ids(1)).astype(jnp.float32) + 0.5
    return count_z / deep


def begin_kernel(
    count_z,
    coef_ref,
    index_ref,
    prev_ref,
    stiff_ref,
    rows_ref,
    low_ref,
    high_ref,
    ylow_ref,
    yhigh_ref,
    prevv_ref,
    raw_ref,
    edge_ref,
    sems,
):
    _, cells_x, cells_y, cells_z = prevv_ref.shape
    copies = [pltpu.make_async_copy(prev_ref.at[ch], prevv_ref.at[ch], sems.at[ch]) for ch in range(3)]
    copies.append(pltpu.make_async_copy(stiff_ref, raw_ref, sems.at[3]))
    for copy in copies:
        copy.start()
    row = jnp.concatenate(
        [coef_ref[f : f + 1, :] for f in range(3)] + [index_ref[...].astype(jnp.float32)], axis=1
    )
    rows_ref[...] = jnp.broadcast_to(row, rows_ref.shape)
    scale = wall_scale(count_z, cells_z)
    lane = lax.broadcasted_iota(jnp.int32, (8, LANES), 1)
    place = lane % 8
    pick = jnp.where(place <= 3, jnp.clip(3 - place, 0, 2), cells_z - 1 - jnp.clip(place - 4, 0, 2))
    for ch in range(4):
        copies[ch].wait()
        for tile in range(cells_y // 8):
            rows = pl.ds(8 * tile, 8)
            edge = jnp.zeros((8, LANES), jnp.float32)
            for x in range(cells_x):
                if ch < 3:
                    value = prevv_ref[ch, x, rows, :]
                else:
                    value = raw_ref[x, rows, :] * scale
                picked = jnp.take_along_axis(value, pick, axis=1)
                edge = jnp.where(lane // 8 == x, picked, edge)
            edge_ref[ch, rows, :] = edge
        for x in range(cells_x):
            at = pl.ds((ch * cells_x + x) * HALO, HALO)
            plane = prevv_ref.at[ch, x] if ch < 3 else raw_ref.at[x]
            factor = 1.0 if ch < 3 else scale
            ylow_ref[at, :] = plane[:HALO, :] * factor
            yhigh_ref[at, :] = plane[cells_y - HALO :, :] * factor
    place = lane_ids(cells_y) % 8
    for pair in range(2):
        even, odd = edge_ref[2 * pair], edge_ref[2 * pair + 1]
        low_ref[pair] = jnp.where(place <= 3, even, roll_lanes(odd, 3))
        high_ref[pair] = jnp.where(place >= 4, even, roll_lanes(odd, -3))


def pack_y_kernel(above_ref, below_ref, ylow_ref, yhigh_ref, _, edge_ref, outlow_ref, outhigh_ref):
    rows = above_ref.shape[1]
    place = lane_ids(rows) % 8
    upper = (place >= 1) & (place <= 3)
    lower = (place >= 4) & (place <= 6)
    base = ylow_ref.shape[0]
    outlow_ref[:base, :] = ylow_ref[...]
    outhigh_ref[:base, :] = yhigh_ref[...]
    for ch in range(4):
        above, below = above_ref[ch // 2], below_ref[ch // 2]
        if ch % 2:
            above, below = roll_lanes(above, -3), roll_lanes(below, 3)
        edge = jnp.where(upper, above, jnp.where(lower, below, 0.0))
        edge_ref[ch] = edge
        at = pl.ds(base + ch * HALO, HALO)
        outlow_ref[at, :] = edge[:HALO]
        outhigh_ref[at, :] = edge[rows - HALO :]
    rest = outlow_ref.shape[0] - base - 4 * HALO
    outlow_ref[base + 4 * HALO :, :] = jnp.zeros((rest, LANES), jnp.float32)
    outhigh_ref[base + 4 * HALO :, :] = jnp.zeros((rest, LANES), jnp.float32)


def fill(out, below_ref, middle, above_ref, at):
    cells_y = middle.shape[0]
    out[0:2, :] = below_ref[at + 1 : at + HALO, :]
    out[2 : 2 + cells_y, :] = middle
    out[2 + cells_y : 2 + cells_y + HALO, :] = above_ref[at : at + HALO, :]
    out[2 + cells_y + HALO : WIN, :] = jnp.zeros((WIN - 2 - cells_y - HALO, LANES), jnp.float32)


def pack_x_kernel(
    count_z, edge_ref, yabove_ref, ybelow_ref, prev_ref, stiff_ref, low_ref, high_ref, faces_ref, wide_ref, sems
):
    _, cells_x, cells_y, cells_z = prev_ref.shape
    copies = []
    for side, x in enumerate((0, cells_x - HALO)):
        for ch in range(4):
            source = prev_ref.at[ch, pl.ds(x, HALO)] if ch < 3 else stiff_ref.at[pl.ds(x, HALO)]
            copies.append(pltpu.make_async_copy(source, faces_ref.at[side, ch], sems.at[side, ch]))
    for copy in copies:
        copy.start()
    scale = wall_scale(count_z, cells_z)
    lane = lane_ids()
    base = 4 * cells_x * HALO
    low = jnp.zeros((WIN, LANES), jnp.float32)
    high = low

    for ch in range(4):
        fill(wide_ref.at[ch], ybelow_ref, edge_ref[ch], yabove_ref, base + ch * HALO)
        turned = roll_lanes(wide_ref[ch], 32 * ch)
        at_low = (lane - 32 * ch) & (LANES - 1)
        low = jnp.where(at_low < 8 * HALO, turned, low)
        high = jnp.where(at_low >= LANES - 8 * HALO, turned, high)
    low_ref[4 * HALO] = low
    high_ref[4 * HALO] = high
    for copy in copies:
        copy.wait()
    for side, out in enumerate((low_ref, high_ref)):
        for ch in range(4):
            for p in range(HALO):
                x = p + side * (cells_x - HALO)
                middle = faces_ref[side, ch, p] * (1.0 if ch < 3 else scale)
                fill(out.at[ch * HALO + p], ybelow_ref, middle, yabove_ref, (ch * cells_x + x) * HALO)


def stencil(count_x, count_y, count_z):
    table = {}
    for step_x in range(int(RADIUS * count_x) + 2):
        for step_y in range(int(RADIUS * count_y) + 2):
            square = (step_x / count_x) ** 2 + (step_y / count_y) ** 2 + (0.5 / count_z) ** 2
            ratio = math.sqrt(square) / RADIUS
            lead = max(1.0 - ratio, 0.0)
            if lead > 0.0:
                table[step_x, step_y] = lead**4 * (4.0 * ratio + 1.0)
    return table


REACH_X = 8
REACH_Y = 8
GRID_X = 32
GRID_Y = 80


def rbf_kernel(table, cells_x, cells_y, count_y, centres_ref, out_ref, grid_ref):
    slots = centres_ref.shape[0] // 4
    first_x = (lax.axis_index("gx") * cells_x - REACH_X).astype(jnp.float32)
    first_y = (lax.axis_index("gy") * cells_y - REACH_Y).astype(jnp.float32)
    quarter = lane_ids(slots) // 32
    fields = []
    for f in range(4):
        field = jnp.zeros((slots, LANES), jnp.float32)
        for k in range(4):
            part = roll_lanes(centres_ref[k * slots : (k + 1) * slots, :], 32 * (k - f))
            field = jnp.where(quarter == k, part, field)
        fields.append(field)
    index = fields[3]
    at_x = jnp.floor(index * (1.0 / count_y))
    at_y = index - at_x * count_y - first_y
    at_x = at_x - first_x
    heads = [f.astype(jnp.bfloat16).astype(jnp.float32) for f in fields[:3]]
    tails = [f - h for f, h in zip(fields[:3], heads)]
    row_y = lax.broadcasted_iota(jnp.int32, (GRID_Y, LANES), 0).astype(jnp.float32)
    row_x = lax.broadcasted_iota(jnp.int32, (GRID_X, LANES), 0).astype(jnp.float32)
    total = jnp.zeros((GRID_Y, 2 * LANES), jnp.float32)
    blank = jnp.zeros((LANES - 3 * GRID_X, LANES), jnp.float32)
    for q in range(0, slots, 2):
        left, right = [], []
        for r in (q, q + 1):
            hit_y = at_y[r : r + 1, :] == row_y
            hit_x = at_x[r : r + 1, :] == row_x
            left.append(jnp.where(hit_y, 1.0, 0.0).astype(jnp.bfloat16))
            pieces = []
            for group in (heads, tails):
                pieces += [jnp.where(hit_x, g[r : r + 1, :], 0.0) for g in group]
                pieces.append(blank)
            right.append(jnp.concatenate(pieces, axis=0).astype(jnp.bfloat16))
        total = total + lax.dot_general(
            jnp.concatenate(left, axis=1),
            jnp.concatenate(right, axis=1),
            (((1,), (1,)), ((), ())),
            preferred_element_type=jnp.float32,
        )
    grid = total[:, :LANES] + total[:, LANES:]
    reach_x = max(a for a, _ in table)
    reach_y = max(b for _, b in table)
    result = jnp.zeros((WIN, LANES), jnp.float32)
    for step_x in range(reach_x + 1):
        value = roll_lanes(grid, 2 - REACH_X + step_x)
        if step_x:
            value = value + roll_lanes(grid, 2 - REACH_X - step_x)
        grid_ref[:GRID_Y, :] = value
        for step_y in range(reach_y + 1):
            phi = table.get((step_x, step_y))
            if phi is None:
                continue
            start = REACH_Y - 2
            part = grid_ref[start + step_y : start + step_y + WIN, :]
            if step_y:
                part = part + grid_ref[start - step_y : start - step_y + WIN, :]
            result = result + phi * part
    lane = lane_ids()
    width = cells_x + 4
    close = jnp.where(
        lane < width,
        result,
        jnp.where(lane < 2 * width, roll_lanes(result, width - 32), roll_lanes(result, 2 * (width - 32))),
    )
    half = out_ref.shape[1]
    share = jnp.where(lane_ids(half) < LANES // 2, close[:half], roll_lanes(close[WIN - half :], LANES // 2))
    for k in range(out_ref.shape[0]):
        out_ref[k] = share


WINDOW = pl.ds(TOP, WIN)
BEFORE = pl.ds(TOP - 1, WIN)
AFTER = pl.ds(TOP + 1, WIN)


def spot(x):
    if isinstance(x, int):
        return (0 if 0 <= x < 16 else 1), x % 16
    return 0, x


def beside(value, edge):
    lane = lane_ids()
    down = jnp.where(lane == 0, edge, roll_lanes(value, 1))
    up = jnp.where(lane == LANES - 1, edge, roll_lanes(value, -1))
    return down, up


def from_edge(tile, g):
    return roll_lanes(tile, LANES - 4 - 8 * g)


def to_edge(old, plane, g):
    lane = lane_ids()
    here = (lane // 8 == g) & ((lane % 8 == 3) | (lane % 8 == 4))
    return jnp.where(here, roll_lanes(plane, 8 * g + 4), old)


def beside_edge(own_ref, other, middle):
    lane = lane_ids()
    place = lane % 8
    own = own_ref[WINDOW, :]
    left = jnp.where(lane >= 8, roll_lanes(own, 8), roll_lanes(other, 8))
    right = jnp.where(lane < LANES - 8, roll_lanes(own, -8), roll_lanes(other, -8))
    minus = jnp.where(place == 4, middle, roll_lanes(own, 1))
    plus = jnp.where(place == 3, middle, roll_lanes(own, -1))
    return left, right, own_ref[BEFORE, :], own_ref[AFTER, :], minus, plus


def normalised(own, others):
    faces = [0.5 * (own + other) for other in others]
    total = functools.reduce(lambda a, b: a + b, faces)
    inside = own > 0.0
    factor = jnp.where(inside, OMEGA / jnp.where(inside, total, 1.0), 0.0)
    return [face * factor for face in faces]


def relaxed(own, others, weights):
    new = (1.0 - OMEGA) * own
    for weight, other in zip(weights, others):
        new = new + weight * other
    return new


def zeros():
    return jnp.zeros((WIN, LANES), jnp.float32)


def wall_lane():
    return (lane_ids() == 0) & (lax.axis_index("gz") == 0)


def column_of(rbf, ch, x, cells_x):
    return roll_lanes(rbf, 2 * LANES - 2 - (cells_x + 4) * ch - x)


def inner_kernel(
    count_z, prev_ref, stiff_ref, edge_ref, yabove_ref, ybelow_ref, shares_ref,
    u0_ref, u1_ref, u2_ref, s_ref, w_ref, es_ref, cs_ref, c_ref, rbf_ref, widev_ref, out_ref,
    prevv_ref, raw_ref, own_ref, above_ref, below_ref, parts_ref, e_ref, ew_ref, done_ref, sems,
):
    _, cells_x, cells_y, cells_z = prevv_ref.shape
    fetched = ((stiff_ref, raw_ref), (yabove_ref, above_ref), (ybelow_ref, below_ref), (edge_ref, own_ref),
               (prev_ref, prevv_ref), (shares_ref, parts_ref))
    copies = [pltpu.make_async_copy(a, b, sems.at[k]) for k, (a, b) in enumerate(fetched)]
    for copy in copies:
        copy.start()
    first = wall_lane()
    scale = wall_scale(count_z, cells_z)
    main = pl.ds(TOP + 2, cells_y)

    def assemble(ch, x):
        at = (ch * cells_x + x) * HALO
        plane = u0_ref.at[ch, x] if ch < 3 else s_ref.at[x]
        plane[main, :] = prevv_ref[ch, x] if ch < 3 else raw_ref[x] * scale
        plane[TOP - 1 : TOP + 2, :] = below_ref[at : at + HALO, :]
        plane[TOP + 2 + cells_y : TOP + 2 + cells_y + HALO, :] = above_ref[at : at + HALO, :]

    for copy in copies[:4]:
        copy.wait()
    for x in range(cells_x):
        assemble(3, x)
    for ch in range(4):
        fill(widev_ref.at[ch], below_ref, own_ref[ch], above_ref, (4 * cells_x + ch) * HALO)
    es_ref[WINDOW, :] = widev_ref[3]
    cs_ref[...] = zeros()
    for x in (0, cells_x - 1):
        cs_ref[...] = to_edge(cs_ref[...], s_ref[x, WINDOW, :], x)

    def weigh(x, carry):
        own = s_ref[x, WINDOW, :]
        down, up = beside(own, from_edge(es_ref[WINDOW, :], x))
        others = (s_ref[x - 1, WINDOW, :], s_ref[x + 1, WINDOW, :], s_ref[x, BEFORE, :], s_ref[x, AFTER, :], down, up)
        for k, weight in enumerate(normalised(own, others)):
            w_ref[k, x] = weight
        cs_ref[...] = to_edge(cs_ref[...], own, x)
        return carry

    lax.fori_loop(1, cells_x - 1, weigh, 0, unroll=14)
    others = beside_edge(es_ref, zeros(), cs_ref[...])
    for k, weight in enumerate(normalised(es_ref[WINDOW, :], others)):
        ew_ref[k] = weight

    for copy in copies[4:]:
        copy.wait()
    for ch in range(3):
        e_ref[0, ch, WINDOW, :] = widev_ref[ch]
        for x in range(cells_x):
            assemble(ch, x)
    rbf_ref[...] = zeros()

    @pl.when(lax.axis_index("gz") == 0)
    def _():
        share = parts_ref[0]
        for k in range(1, parts_ref.shape[0]):
            share = share + parts_ref[k]
        half = share.shape[0]
        rbf_ref[WIN - half :, :] = roll_lanes(share, LANES // 2)
        rbf_ref[:half, :] = share
        rbf = rbf_ref[...]

        def layer(x, carry):
            own = first & (s_ref[x, WINDOW, :] > 0.0)
            for ch in range(3):
                column = column_of(rbf, ch, x, cells_x)
                u0_ref[ch, x, WINDOW, :] = jnp.where(own, column, u0_ref[ch, x, WINDOW, :])
            return carry

        lax.fori_loop(0, cells_x, layer, 0, unroll=16)

    for ch in range(3):
        ends = zeros()
        for x in range(cells_x):
            ends = to_edge(ends, u0_ref[ch, x, WINDOW, :], x)
        c_ref[0, ch] = ends
        c_ref[1, ch] = zeros()

    stages = (u0_ref, u1_ref, u2_ref)
    for sweep in range(SWEEPS):
        now, last = stages[sweep], sweep == SWEEPS - 1

        def relax(x, carry):
            weights = [w_ref[k, x] for k in range(6)]
            for ch in range(3):
                own = now[ch, x, WINDOW, :]
                down, up = beside(own, from_edge(e_ref[sweep, ch, WINDOW, :], x))
                others = (
                    now[ch, x - 1, WINDOW, :],
                    now[ch, x + 1, WINDOW, :],
                    now[ch, x, BEFORE, :],
                    now[ch, x, AFTER, :],
                    down,
                    up,
                )
                new = jnp.where(first, own, relaxed(own, others, weights))
                if last:
                    done_ref[ch, x] = new[2 : 2 + cells_y]
                else:
                    stages[sweep + 1][ch, x, WINDOW, :] = new
                if sweep == 0:
                    c_ref[1, ch] = to_edge(c_ref[1, ch], new, x)
            return carry

        lax.fori_loop(1 + sweep, cells_x - 1 - sweep, relax, 0, unroll=(14, 12, 10)[sweep])
        if not last:
            for ch in range(3):
                others = beside_edge(e_ref.at[sweep, ch], zeros(), c_ref[sweep, ch])
                weights = [ew_ref[k] for k in range(6)]
                e_ref[sweep + 1, ch, WINDOW, :] = relaxed(e_ref[sweep, ch, WINDOW, :], others, weights)
    inside = pl.ds(HALO, cells_x - 2 * HALO)
    copies = [
        pltpu.make_async_copy(done_ref.at[ch, inside], out_ref.at[ch, inside], sems.at[6 + ch]) for ch in range(3)
    ]
    for copy in copies:
        copy.start()
    for copy in copies:
        copy.wait()


def outer_kernel(
    u0_ref, u1_ref, u2_ref, s_ref, w_ref, wide_ref, es_ref, cs_ref, c_ref, rbf_ref, xabove_ref, xbelow_ref, _,
    out_ref,
    h0_ref, h1_ref, h2_ref, hs_ref, hw_ref, e_ref, eside_ref, ew_ref, c1_ref, done_ref, sem,
):
    _, cells_x, _, _ = u0_ref.shape
    cells_y = done_ref.shape[2]
    lane = lane_ids()
    first = wall_lane()

    def held(x):
        return x + HALO if x < HALO else x - cells_x + HALO + 6

    beyond = [x for p in range(HALO) for x in (p - HALO, cells_x + p)]
    for x in beyond:
        source, p = (xbelow_ref, x + HALO) if x < 0 else (xabove_ref, x - cells_x)
        own = source[3 * HALO + p]
        hs_ref[held(x), WINDOW, :] = own
        for ch in range(3):
            column = column_of(rbf_ref[...], ch, x, cells_x)
            h0_ref[ch, held(x), WINDOW, :] = jnp.where(first & (own > 0.0), column, source[ch * HALO + p])
    for ch in range(4):
        above = roll_lanes(xabove_ref[4 * HALO], -32 * ch)
        below = roll_lanes(xbelow_ref[4 * HALO], -32 * ch)
        side = jnp.where(lane < 8 * HALO, above, jnp.where(lane >= LANES - 8 * HALO, below, 0.0))
        if ch < 3:
            e_ref[0, ch, 0, WINDOW, :] = wide_ref[ch]
            e_ref[0, ch, 1, WINDOW, :] = side
        else:
            eside_ref[WINDOW, :] = side

    def stiff(x):
        return s_ref.at[x] if 0 <= x < cells_x else hs_ref.at[held(x)]

    def field(sweep, ch, x):
        if sweep <= x < cells_x - sweep:
            return (u0_ref, u1_ref, u2_ref)[sweep].at[ch, x]
        return (h0_ref, h1_ref, h2_ref)[sweep].at[ch, held(x)]

    edge_stiff = (es_ref, eside_ref)

    ends = zeros()
    for x in beyond:
        ends = to_edge(ends, stiff(x)[WINDOW, :], spot(x)[1])
    for tile, middle in ((0, cs_ref[...]), (1, ends)):
        others = beside_edge(edge_stiff[tile], edge_stiff[1 - tile][WINDOW, :], middle)
        for k, weight in enumerate(normalised(edge_stiff[tile][WINDOW, :], others)):
            ew_ref[k, tile] = weight
    for x in (-2, -1, 0, cells_x - 1, cells_x, cells_x + 1):
        own = stiff(x)[WINDOW, :]
        tile, g = spot(x)
        down, up = beside(own, from_edge(edge_stiff[tile][WINDOW, :], g))
        others = (
            stiff(x - 1)[WINDOW, :],
            stiff(x + 1)[WINDOW, :],
            stiff(x)[BEFORE, :],
            stiff(x)[AFTER, :],
            down,
            up,
        )
        for k, weight in enumerate(normalised(own, others)):
            hw_ref[k, held(x)] = weight

    for sweep in range(SWEEPS):
        last = sweep == SWEEPS - 1
        planes = [x for p in range(HALO) for x in (sweep - 2 + p, cells_x + 1 - sweep - p)]
        for x in planes:
            tile, g = spot(x)
            if 1 <= x < cells_x - 1:
                weights = [w_ref[k, x] for k in range(6)]
            else:
                weights = [hw_ref[k, held(x)] for k in range(6)]
            for ch in range(3):
                here = field(sweep, ch, x)
                own = here[WINDOW, :]
                down, up = beside(own, from_edge(e_ref[sweep, ch, tile, WINDOW, :], g))
                others = (
                    field(sweep, ch, x - 1)[WINDOW, :],
                    field(sweep, ch, x + 1)[WINDOW, :],
                    here[BEFORE, :],
                    here[AFTER, :],
                    down,
                    up,
                )
                new = jnp.where(first, own, relaxed(own, others, weights))
                if last:
                    done_ref[ch, x if x < HALO else x - cells_x + 2 * HALO] = new[2 : 2 + cells_y]
                else:
                    (h1_ref, h2_ref)[sweep][ch, held(x), WINDOW, :] = new
        if last:
            break
        for ch in range(3):
            if sweep == 0:
                ends = zeros()
                for x in beyond:
                    ends = to_edge(ends, field(0, ch, x)[WINDOW, :], spot(x)[1])
                middles = (c_ref[0, ch], ends)
            else:
                ends = c_ref[1, ch]
                for x in (0, cells_x - 1):
                    ends = to_edge(ends, field(1, ch, x)[WINDOW, :], x)
                middles = (ends,)
            for tile, middle in enumerate(middles):
                others = beside_edge(e_ref.at[sweep, ch, tile], e_ref[sweep, ch, 1 - tile, WINDOW, :], middle)
                weights = [ew_ref[k, tile] for k in range(6)]
                e_ref[sweep + 1, ch, tile, WINDOW, :] = relaxed(
                    e_ref[sweep, ch, tile, WINDOW, :], others, weights
                )
    copies = []
    for ch in range(3):
        for side, x in enumerate((0, cells_x - HALO)):
            copies.append(
                pltpu.make_async_copy(
                    done_ref.at[ch, pl.ds(side * HALO, HALO)],
                    out_ref.at[ch, pl.ds(x, HALO)],
                    sem.at[2 * ch + side],
                )
            )
    for copy in copies:
        copy.start()
    for copy in copies:
        copy.wait()


def step(value, axis, by):
    size = lax.axis_size(axis)
    return lax.ppermute(value, axis, [(i, i + by) for i in range(size) if 0 <= i + by < size])


def body(centre_coef, centre_index, stiff_factor, prev_disp):
    cells_x, cells_y, cells_z = stiff_factor.shape
    count_x = cells_x * lax.axis_size("gx")
    count_y = cells_y * lax.axis_size("gy")
    count_z = cells_z * lax.axis_size("gz")
    blocks = lax.axis_size("gx") * lax.axis_size("gy")
    depth = lax.axis_size("gz")
    scratch = pltpu.VMEM
    num = jnp.float32

    rows_y = 4 * cells_x * HALO
    rows, low, high, ylow, yhigh = kernel_call(
        functools.partial(begin_kernel, float(count_z)),
        "pack_z",
        (
            f32(blocks, LANES),
            f32(2, cells_y, LANES),
            f32(2, cells_y, LANES),
            f32(rows_y, LANES),
            f32(rows_y, LANES),
        ),
        2000 * MEGA,
        (centre_coef.T, centre_index[None]),
        (
            scratch((3, cells_x, cells_y, LANES), num),
            scratch((cells_x, cells_y, LANES), num),
            scratch((4, cells_y, LANES), num),
            pltpu.SemaphoreType.DMA((4,)),
        ),
        far=tuple(pltpu.with_memory_space_constraint(a, pltpu.HBM) for a in (prev_disp, stiff_factor)),
    )
    centres = lax.all_to_all(rows.reshape(blocks, 1, LANES), ("gx", "gy"), 0, 0, tiled=True)
    zabove, zbelow = step(low, "gz", -1), step(high, "gz", 1)

    table = stencil(count_x, count_y, count_z)
    (share,) = kernel_call(
        functools.partial(rbf_kernel, table, cells_x, cells_y, count_y),
        "rbf",
        (f32(depth, HALF, LANES),),
        1500 * MEGA,
        (centres.reshape(blocks, LANES),),
        (scratch((ROWS, LANES), num),),
    )
    shares = lax.all_to_all(share, "gz", 0, 0, tiled=True)

    rows_all = -(-(rows_y + 4 * HALO) // 8) * 8
    edge, ylow, yhigh = kernel_call(
        pack_y_kernel,
        "pack_y",
        (f32(4, cells_y, LANES), f32(rows_all, LANES), f32(rows_all, LANES)),
        300 * MEGA,
        (zabove, zbelow, ylow, yhigh),
        after=(share,),
    )
    yabove, ybelow = step(ylow, "gy", -1), step(yhigh, "gy", 1)

    xlow, xhigh = kernel_call(
        functools.partial(pack_x_kernel, float(count_z)),
        "pack_x",
        (f32(4 * HALO + 1, WIN, LANES), f32(4 * HALO + 1, WIN, LANES)),
        1000 * MEGA,
        (edge, yabove, ybelow),
        (scratch((2, 4, HALO, cells_y, LANES), num), scratch((4, WIN, LANES), num), pltpu.SemaphoreType.DMA((2, 4))),
        far=(prev_disp, stiff_factor),
    )
    xabove, xbelow = step(xlow, "gx", -1), step(xhigh, "gx", 1)

    u0, u1, u2, s, w, es, cs, c, rbf, wide, out = kernel_call(
        functools.partial(inner_kernel, float(count_z)),
        "inner",
        (
            near(3, cells_x, ROWS, LANES),
            near(3, cells_x, ROWS, LANES),
            near(3, cells_x, ROWS, LANES),
            near(cells_x, ROWS, LANES),
            near(6, cells_x, WIN, LANES),
            near(ROWS, LANES),
            near(WIN, LANES),
            near(2, 3, WIN, LANES),
            near(WIN, LANES),
            near(4, WIN, LANES),
            Far((3, cells_x, cells_y, cells_z), num),
        ),
        9000 * MEGA,
        (),
        (
            scratch((3, cells_x, cells_y, LANES), num),
            scratch((cells_x, cells_y, LANES), num),
            scratch((4, cells_y, LANES), num),
            scratch((rows_all, LANES), num),
            scratch((rows_all, LANES), num),
            scratch((depth, HALF, LANES), num),
            scratch((3, 3, ROWS, LANES), num),
            scratch((6, WIN, LANES), num),
            scratch((3, cells_x, cells_y, LANES), num),
            pltpu.SemaphoreType.DMA((9,)),
        ),
        far=(prev_disp, stiff_factor, edge, yabove, ybelow, shares),
    )

    (out,) = kernel_call(
        outer_kernel,
        "outer",
        (Far((3, cells_x, cells_y, cells_z), num),),
        5500 * MEGA,
        (u0, u1, u2, s, w, wide, es, cs, c, rbf, xabove, xbelow),
        (
            scratch((3, 12, ROWS, LANES), num),
            scratch((3, 12, ROWS, LANES), num),
            scratch((3, 12, ROWS, LANES), num),
            scratch((12, ROWS, LANES), num),
            scratch((6, 12, WIN, LANES), num),
            scratch((3, 3, 2, ROWS, LANES), num),
            scratch((ROWS, LANES), num),
            scratch((6, 2, WIN, LANES), num),
            scratch((WIN, LANES), num),
            scratch((3, 2 * HALO, cells_y, LANES), num),
            pltpu.SemaphoreType.DMA((6,)),
        ),
        far=(out,),
        aliases={12: 0},
    )
    return out


def solution(mesh):
    placed = (
        P(("gx", "gy", "gz"), None),
        P(("gx", "gy", "gz")),
        P("gx", "gy", "gz"),
        P(None, "gx", "gy", "gz"),
    )
    return jax.shard_map(
        body, mesh=mesh, in_specs=placed, out_specs=P(None, "gx", "gy", "gz"), check_vma=False
    )
```

time: 79.5 us -> 75.3 us (0.947)
  Pallas kernels: 16.1 us -> 22.2 us
  waiting for transfers between devices: 6.73 us -> 3.28 us
  local copies, waits for them, and re-layouts: 5.64 us -> 2.25 us
  starting transfers between devices: 48.4 us -> 46.5 us
  other arithmetic: 1.35 us -> 0 us
    pallas_call x5 -> x6, Pallas kernels: 16.1 us -> 22.2 us  [kernel_call(): pl.pallas_call(kernel, name=name, out_shape=outs, in_specs=[pl.BlockSpec(...]
    unnamed x16 -> x12, local copies, waits for them, and re-layouts: 4.92 us -> 2.25 us
    all_to_all x1, starting transfers between devices: 12 us -> 10 us  [body(): shares = lax.all_to_all(share, 'gz', 0, 0, tiled=True)]
    all_to_all x1, waiting for transfers between devices: 1.85 us -> 0.01 us  [body(): shares = lax.all_to_all(share, 'gz', 0, 0, tiled=True)]
    ppermute x6, waiting for transfers between devices: 4.88 us -> 3.27 us  [step(): lax.ppermute(value, axis, [(i, i + by) for i in range(size) if 0 <= i + b...]
  transfers between devices with their start and end apart: 8 -> 8, of which waited for: 4 -> 1; matrix products, arithmetic and copies ran while one was open for 0% -> 0% of each run, Pallas kernels for 5% -> 20%
where the time goes in v3:
time: 75.3 us; the launch traced here: 74.5 us
  starting transfers between devices  46.5 us (62%)
  Pallas kernels  22.2 us (29%)
  waiting for transfers between devices  3.28 us (4%)
  local copies, waits for them, and re-layouts  2.25 us (3%)
    pallas_call x6, Pallas kernels, kernel_call(): pl.pallas_call(kernel, name=name, out_shape=outs, in_specs=[pl.BlockSpec(...  22.2 us
    ppermute x6, starting transfers between devices, step(): lax.ppermute(value, axis, [(i, i + by) for i in range(size) if 0 <= i + b...  21.9 us
    all_to_all x1, starting transfers between devices, body(): lax.all_to_all(rows.reshape(blocks, 1, LANES), ('gx', 'gy'), 0, 0, tiled=...  14.6 us
    all_to_all x1, starting transfers between devices, body(): shares = lax.all_to_all(share, 'gz', 0, 0, tiled=True)  10 us
    ppermute x6, waiting for transfers between devices, step(): lax.ppermute(value, axis, [(i, i + by) for i in range(size) if 0 <= i + b...  3.27 us
    unnamed x12, local copies, waits for them, and re-layouts  2.25 us
  transfers between devices with their start and end apart: 8, of which 1 were waited for; matrix products, arithmetic and copies ran while one was open for 0% of the time, Pallas kernels for 20%

profile of v3, /device:TPU:1, one launch (start us, length us, event | category | flops | bytes accessed | tf_op | source)
XLA Modules:
  0.0 74.5 jit_solution(13557511662797653058)
XLA Ops:
  0.0 0.7 copy-done.2
  0.7 0.7 copy-done.3
  1.3 2.3 %pack_z.1 = (f32[64,128]{1,0:T(8,128)}, f32[2,64,128]{2,1,0:T(8,128)S(1)}, f32[2,64,128]{2,1,0:T(8,128)S(1)}, f32[192,128]{1,0:T(8,128)S(1)}, f32[192,128]{1,0:T(8,128)S(1)}) custom-call(f32[3,32]{1,0:T(4,128)S(1)} %bitcast.7, s32[1,32]{1,0:T(1,128)S(1)} %bitcast.8, f32[3,16,64,128]{3,2,1,0:T(8,128)} %prev_ref.5, f32[16,64,128]{2,1,0:T(8,128)} %stiff_ref.5), custom_call_target="tpu_custom_call" | custom-call | flops 2200000000 | bytes 360960 | tf_op jit(solution)/shard_map/pack_z/pallas_call | solution.py:38
  3.7 14.6 %all-to-all-start = ((f32[64,1,128]{2,1,0:T(1,128)}), f32[64,1,128]{2,1,0:T(1,128)S(1)}, u32[]{:S(2)}, u32[]{:S(2)}) async-start(f32[64,1,128]{2,1,0:T(1,128)} %bitcast.3), calls=%async_computation | async-start | bytes 65536 | tf_op jit(solution)/shard_map/all_to_all | solution.py:625
  18.3 1.3 %collective-permute-start = (f32[2,64,128]{2,1,0:T(8,128)S(1)}, f32[2,64,128]{2,1,0:T(8,128)S(1)}, u32[]{:S(2)}, u32[]{:S(2)}) collective-permute-start(f32[2,64,128]{2,1,0:T(8,128)S(1)} %get-tuple-element.26), channel_id=1, source_target_pairs={{1,0},{2,1},{3,2},{4,3},{5,4},{6,5},{7,6},{9,8},{10,9},{11,10},{12... | collective-permute-start | bytes 196616 | tf_op jit(solution)/shard_map/ppermute | solution.py:591
  19.6 8.6 %collective-permute-start.1 = (f32[2,64,128]{2,1,0:T(8,128)S(1)}, f32[2,64,128]{2,1,0:T(8,128)S(1)}, u32[]{:S(2)}, u32[]{:S(2)}) collective-permute-start(f32[2,64,128]{2,1,0:T(8,128)S(1)} %get-tuple-element.27), channel_id=1, source_target_pairs={{0,1},{1,2},{2,3},{3,4},{4,5},{5,6},{6,7},{8,9},{9,10},{10,11},{11... | collective-permute-start | bytes 196616 | tf_op jit(solution)/shard_map/ppermute | solution.py:591
  28.2 0.0 all-to-all-done
  28.2 0.0 copy-start
  28.2 0.0 copy-start.1
  28.2 1.5 %rbf.1._ = f32[8,40,128]{2,1,0:T(8,128)} custom-call(f32[64,128]{1,0:T(8,128)S(1)} %bitcast.6), custom_call_target="tpu_custom_call" | custom-call | flops 1650000000 | bytes 196608 | tf_op jit(solution)/shard_map/rbf/pallas_call | solution.py:38
  29.8 10.0 %all-to-all-start.1 = ((f32[8,40,128]{2,1,0:T(8,128)}), f32[8,40,128]{2,1,0:T(8,128)S(1)}, u32[]{:S(2)}, u32[]{:S(2)}) async-start(f32[8,40,128]{2,1,0:T(8,128)} %rbf.1._), calls=%async_computation.1 | async-start | bytes 327680 | tf_op jit(solution)/shard_map/all_to_all | solution.py:637
  39.7 0.0 collective-permute-done.above_ref
  39.8 0.0 collective-permute-done.1.below_ref
  39.8 0.1 pack_y.1
  39.9 0.0 copy-start.4
  39.9 1.3 %collective-permute-start.2 = (f32[208,128]{1,0:T(8,128)S(1)}, f32[208,128]{1,0:T(8,128)S(1)}, u32[]{:S(2)}, u32[]{:S(2)}) collective-permute-start(f32[208,128]{1,0:T(8,128)S(1)} %get-tuple-element.32), channel_id=1, source_target_pairs={{8,0},{16,8},{24,16},{9,1},{17,9},{25,17},{10,2},{18,10},{26,18},{... | collective-permute-start | bytes 319496 | tf_op jit(solution)/shard_map/ppermute | solution.py:591
  41.2 4.0 %collective-permute-start.3 = (f32[208,128]{1,0:T(8,128)S(1)}, f32[208,128]{1,0:T(8,128)S(1)}, u32[]{:S(2)}, u32[]{:S(2)}) collective-permute-start(f32[208,128]{1,0:T(8,128)S(1)} %get-tuple-element.33), channel_id=1, source_target_pairs={{0,8},{8,16},{16,24},{1,9},{9,17},{17,25},{2,10},{10,18},{18,26},{... | collective-permute-start | bytes 319496 | tf_op jit(solution)/shard_map/ppermute | solution.py:591
  45.2 3.3 %collective-permute-done.2.yabove_ref = f32[208,128]{1,0:T(8,128)S(1)} collective-permute-done((f32[208,128]{1,0:T(8,128)S(1)}, f32[208,128]{1,0:T(8,128)S(1)}, u32[]{:S(2)}, u32[]{:S(2)}) %collective-permute-start.2) | collective-permute-done | bytes 106528 | tf_op jit(solution)/shard_map/ppermute | solution.py:591
  48.4 0.0 collective-permute-done.3.ybelow_ref
  48.4 0.0 copy-done
  48.4 0.0 copy-done.1
  48.5 2.0 %pack_x.1 = (f32[13,72,128]{2,1,0:T(8,128)}, f32[13,72,128]{2,1,0:T(8,128)S(1)}) custom-call(f32[4,64,128]{2,1,0:T(8,128)S(1)} %get-tuple-element.31.edge_ref, f32[208,128]{1,0:T(8,128)S(1)} %collective-permute-done.2.yabove_ref, f32[208,128]{1,0:T(8,128)S(1)} %collective-permute-done.3.ybelow_ref, f32[3,16,64,128]{3,2,1,0:T(8,128)S(1)} %copy-done, ...), custom_call_target="tpu_custom_call" | custom-call | flops 1100000000 | bytes 1302528 | tf_op jit(solution)/shard_map/pack_x/pallas_call | solution.py:38
  50.5 0.0 copy-done.4
  50.5 3.6 %collective-permute-start.4 = (f32[13,72,128]{2,1,0:T(8,128)}, f32[13,72,128]{2,1,0:T(8,128)S(1)}, u32[]{:S(2)}, u32[]{:S(2)}) collective-permute-start(f32[13,72,128]{2,1,0:T(8,128)} %get-tuple-element.44), channel_id=1, source_target_pairs={{32,0},{64,32},{96,64},{128,96},{160,128},{192,160},{224,192},{256... | collective-permute-start | bytes 1437704 | tf_op jit(solution)/shard_map/ppermute | solution.py:591
  54.1 3.2 %collective-permute-start.5 = (f32[13,72,128]{2,1,0:T(8,128)S(1)}, f32[13,72,128]{2,1,0:T(8,128)}, u32[]{:S(2)}, u32[]{:S(2)}) collective-permute-start(f32[13,72,128]{2,1,0:T(8,128)S(1)} %get-tuple-element.45), channel_id=1, source_target_pairs={{0,32},{32,64},{64,96},{96,128},{128,160},{160,192},{192,224},{224... | collective-permute-start | bytes 1437704 | tf_op jit(solution)/shard_map/ppermute | solution.py:591
  57.3 0.0 all-to-all-done.1.shares_ref
  57.3 0.0 copy-start.5
  57.3 0.9 %copy-done.5 = f32[4,64,128]{2,1,0:T(8,128)S(1)} copy-done((f32[4,64,128]{2,1,0:T(8,128)S(1)}, f32[4,64,128]{2,1,0:T(8,128)}, u32[]{:S(2)}) %copy-start.5) | copy-done | bytes 131096
  58.2 10.9 %inner.1 = (f32[3,16,88,128]{3,2,1,0:T(8,128)S(1)}, f32[3,16,88,128]{3,2,1,0:T(8,128)S(1)}, f32[3,16,88,128]{3,2,1,0:T(8,128)S(1)}, f32[16,88,128]{2,1,0:T(8,128...) custom-call(f32[3,16,64,128]{3,2,1,0:T(8,128)S(1)} %copy-done, ...), custom_call_target="tpu_custom_call" | custom-call | flops 9900000256 | bytes 12808192 | tf_op jit(solution)/shard_map/inner/pallas_call | solution.py:38
  69.1 0.0 collective-permute-done.4.xabove_ref
  69.1 0.0 collective-permute-done.5.xbelow_ref
  69.1 5.2 %outer.1 = f32[3,16,64,128]{3,2,1,0:T(8,128)} custom-call(f32[3,16,88,128]{3,2,1,0:T(8,128)S(1)} %get-tuple-element.34.u0_ref, f32[3,16,88,128]{3,2,1,0:T(8,128)S(1)} %get-tuple-element.35.u1_ref, f32[3,16,88,128]{3,2,1,0:T(8,128)S(1)} %get-tuple-element.36.u2_ref, f32[16,88,128]{2,1,0:T(8,128)S(1)} %get-tuple-element.37.s_ref, ...), custom_call_target="tpu_custom_call", output_to_operand_aliasing={{}: (12, {})} | custom-call | flops 6049999872 | bytes 13766656 | tf_op jit(solution)/shard_map/outer/pallas_call | solution.py:38
  (2 shorter events, 0.0 us)
Async XLA Ops:
  0.0 0.7 copy-start.2
  0.7 0.7 copy-start.3
  3.7 24.5 %all-to-all-start = ((f32[64,1,128]{2,1,0:T(1,128)}), f32[64,1,128]{2,1,0:T(1,128)S(1)}, u32[]{:S(2)}, u32[]{:S(2)}) async-start(f32[64,1,128]{2,1,0:T(1,128)} %bitcast.3), calls=%async_computation | async-start | bytes 65536 | tf_op jit(solution)/shard_map/all_to_all | solution.py:625
  18.3 21.5 %collective-permute-start = (f32[2,64,128]{2,1,0:T(8,128)S(1)}, f32[2,64,128]{2,1,0:T(8,128)S(1)}, u32[]{:S(2)}, u32[]{:S(2)}) collective-permute-start(f32[2,64,128]{2,1,0:T(8,128)S(1)} %get-tuple-element.26), channel_id=1, source_target_pairs={{1,0},{2,1},{3,2},{4,3},{5,4},{6,5},{7,6},{9,8},{10,9},{11,10},{12... | collective-permute-start | bytes 196616 | tf_op jit(solution)/shard_map/ppermute | solution.py:591
  19.6 20.2 %collective-permute-start.1 = (f32[2,64,128]{2,1,0:T(8,128)S(1)}, f32[2,64,128]{2,1,0:T(8,128)S(1)}, u32[]{:S(2)}, u32[]{:S(2)}) collective-permute-start(f32[2,64,128]{2,1,0:T(8,128)S(1)} %get-tuple-element.27), channel_id=1, source_target_pairs={{0,1},{1,2},{2,3},{3,4},{4,5},{5,6},{6,7},{8,9},{9,10},{10,11},{11... | collective-permute-start | bytes 196616 | tf_op jit(solution)/shard_map/ppermute | solution.py:591
  28.2 20.3 %copy-start = (f32[3,16,64,128]{3,2,1,0:T(8,128)S(1)}, f32[3,16,64,128]{3,2,1,0:T(8,128)}, u32[]{:S(2)}) copy-start(f32[3,16,64,128]{3,2,1,0:T(8,128)} %prev_ref.5) | copy-start | bytes 4718596
  28.2 20.2 %copy-start.1 = (f32[16,64,128]{2,1,0:T(8,128)S(1)}, f32[16,64,128]{2,1,0:T(8,128)}, u32[]{:S(2)}) copy-start(f32[16,64,128]{2,1,0:T(8,128)} %stiff_ref.5) | copy-start | bytes 1572868
  29.8 27.5 %all-to-all-start.1 = ((f32[8,40,128]{2,1,0:T(8,128)}), f32[8,40,128]{2,1,0:T(8,128)S(1)}, u32[]{:S(2)}, u32[]{:S(2)}) async-start(f32[8,40,128]{2,1,0:T(8,128)} %rbf.1._), calls=%async_computation.1 | async-start | bytes 327680 | tf_op jit(solution)/shard_map/all_to_all | solution.py:637
  39.9 10.6 %copy-start.4 = (f32[4,64,128]{2,1,0:T(8,128)}, f32[4,64,128]{2,1,0:T(8,128)S(1)}, u32[]{:S(2)}) copy-start(f32[4,64,128]{2,1,0:T(8,128)S(1)} %get-tuple-element.31.edge_ref) | copy-start | bytes 393220
  39.9 8.6 %collective-permute-start.2 = (f32[208,128]{1,0:T(8,128)S(1)}, f32[208,128]{1,0:T(8,128)S(1)}, u32[]{:S(2)}, u32[]{:S(2)}) collective-permute-start(f32[208,128]{1,0:T(8,128)S(1)} %get-tuple-element.32), channel_id=1, source_target_pairs={{8,0},{16,8},{24,16},{9,1},{17,9},{25,17},{10,2},{18,10},{26,18},{... | collective-permute-start | bytes 319496 | tf_op jit(solution)/shard_map/ppermute | solution.py:591
  41.2 7.3 %collective-permute-start.3 = (f32[208,128]{1,0:T(8,128)S(1)}, f32[208,128]{1,0:T(8,128)S(1)}, u32[]{:S(2)}, u32[]{:S(2)}) collective-permute-start(f32[208,128]{1,0:T(8,128)S(1)} %get-tuple-element.33), channel_id=1, source_target_pairs={{0,8},{8,16},{16,24},{1,9},{9,17},{17,25},{2,10},{10,18},{18,26},{... | collective-permute-start | bytes 319496 | tf_op jit(solution)/shard_map/ppermute | solution.py:591
  50.5 18.6 %collective-permute-start.4 = (f32[13,72,128]{2,1,0:T(8,128)}, f32[13,72,128]{2,1,0:T(8,128)S(1)}, u32[]{:S(2)}, u32[]{:S(2)}) collective-permute-start(f32[13,72,128]{2,1,0:T(8,128)} %get-tuple-element.44), channel_id=1, source_target_pairs={{32,0},{64,32},{96,64},{128,96},{160,128},{192,160},{224,192},{256... | collective-permute-start | bytes 1437704 | tf_op jit(solution)/shard_map/ppermute | solution.py:591
  54.1 15.0 %collective-permute-start.5 = (f32[13,72,128]{2,1,0:T(8,128)S(1)}, f32[13,72,128]{2,1,0:T(8,128)}, u32[]{:S(2)}, u32[]{:S(2)}) collective-permute-start(f32[13,72,128]{2,1,0:T(8,128)S(1)} %get-tuple-element.45), channel_id=1, source_target_pairs={{0,32},{32,64},{64,96},{96,128},{128,160},{160,192},{192,224},{224... | collective-permute-start | bytes 1437704 | tf_op jit(solution)/shard_map/ppermute | solution.py:591
  57.3 0.9 %copy-start.5 = (f32[4,64,128]{2,1,0:T(8,128)S(1)}, f32[4,64,128]{2,1,0:T(8,128)}, u32[]{:S(2)}) copy-start(f32[4,64,128]{2,1,0:T(8,128)} %copy-done.4) | copy-start | bytes 393220

commit v4 on v3

--- a/solution.py
+++ b/solution.py
@@ -56,6 +56,10 @@
     return jax.ShapeDtypeStruct(shape, jnp.float32)
 
 
+def in_hbm(value):
+    return pltpu.with_memory_space_constraint(value, pltpu.HBM)
+
+
 def near(*shape):
     return pltpu.VMEM(shape, jnp.float32)
 
@@ -67,10 +71,10 @@
 
 def begin_kernel(
     count_z,
-    coef_ref,
-    index_ref,
     prev_ref,
     stiff_ref,
+    coefs_ref,
+    indices_ref,
     rows_ref,
     low_ref,
     high_ref,
@@ -79,13 +83,21 @@
     prevv_ref,
     raw_ref,
     edge_ref,
+    coef_ref,
+    index_ref,
     sems,
 ):
     _, cells_x, cells_y, cells_z = prevv_ref.shape
     copies = [pltpu.make_async_copy(prev_ref.at[ch], prevv_ref.at[ch], sems.at[ch]) for ch in range(3)]
     copies.append(pltpu.make_async_copy(stiff_ref, raw_ref, sems.at[3]))
-    for copy in copies:
+    short = [
+        pltpu.make_async_copy(coefs_ref, coef_ref, sems.at[4]),
+        pltpu.make_async_copy(indices_ref, index_ref, sems.at[5]),
+    ]
+    for copy in short + copies:
         copy.start()
+    for copy in short:
+        copy.wait()
     row = jnp.concatenate(
         [coef_ref[f : f + 1, :] for f in range(3)] + [index_ref[...].astype(jnp.float32)], axis=1
     )
@@ -120,7 +132,7 @@
         high_ref[pair] = jnp.where(place >= 4, even, roll_lanes(odd, -3))
 
 
-def pack_y_kernel(above_ref, below_ref, ylow_ref, yhigh_ref, _, edge_ref, outlow_ref, outhigh_ref):
+def pack_y_kernel(above_ref, below_ref, ylow_ref, yhigh_ref, edge_ref, outlow_ref, outhigh_ref):
     rows = above_ref.shape[1]
     place = lane_ids(rows) % 8
     upper = (place >= 1) & (place <= 3)
@@ -151,16 +163,9 @@
 
 
 def pack_x_kernel(
-    count_z, edge_ref, yabove_ref, ybelow_ref, prev_ref, stiff_ref, low_ref, high_ref, faces_ref, wide_ref, sems
+    count_z, edge_ref, yabove_ref, ybelow_ref, prev_ref, stiff_ref, low_ref, high_ref, wide_ref
 ):
     _, cells_x, cells_y, cells_z = prev_ref.shape
-    copies = []
-    for side, x in enumerate((0, cells_x - HALO)):
-        for ch in range(4):
-            source = prev_ref.at[ch, pl.ds(x, HALO)] if ch < 3 else stiff_ref.at[pl.ds(x, HALO)]
-            copies.append(pltpu.make_async_copy(source, faces_ref.at[side, ch], sems.at[side, ch]))
-    for copy in copies:
-        copy.start()
     scale = wall_scale(count_z, cells_z)
     lane = lane_ids()
     base = 4 * cells_x * HALO
@@ -175,13 +180,11 @@
         high = jnp.where(at_low >= LANES - 8 * HALO, turned, high)
     low_ref[4 * HALO] = low
     high_ref[4 * HALO] = high
-    for copy in copies:
-        copy.wait()
     for side, out in enumerate((low_ref, high_ref)):
         for ch in range(4):
             for p in range(HALO):
                 x = p + side * (cells_x - HALO)
-                middle = faces_ref[side, ch, p] * (1.0 if ch < 3 else scale)
+                middle = prev_ref[ch, x] if ch < 3 else stiff_ref[x] * scale
                 fill(out.at[ch * HALO + p], ybelow_ref, middle, yabove_ref, (ch * cells_x + x) * HALO)
 
 
@@ -203,7 +206,7 @@
 GRID_Y = 80
 
 
-def rbf_kernel(table, cells_x, cells_y, count_y, centres_ref, out_ref, grid_ref):
+def rbf_kernel(table, cells_x, cells_y, count_y, centres_ref, _, out_ref, grid_ref):
     slots = centres_ref.shape[0] // 4
     first_x = (lax.axis_index("gx") * cells_x - REACH_X).astype(jnp.float32)
     first_y = (lax.axis_index("gy") * cells_y - REACH_Y).astype(jnp.float32)
@@ -341,15 +344,10 @@
 
 def inner_kernel(
     count_z, prev_ref, stiff_ref, edge_ref, yabove_ref, ybelow_ref, shares_ref,
-    u0_ref, u1_ref, u2_ref, s_ref, w_ref, es_ref, cs_ref, c_ref, rbf_ref, widev_ref, out_ref,
-    prevv_ref, raw_ref, own_ref, above_ref, below_ref, parts_ref, e_ref, ew_ref, done_ref, sems,
+    u0_ref, u1_ref, u2_ref, s_ref, w_ref, es_ref, cs_ref, c_ref, rbf_ref, widev_ref, done_ref,
+    e_ref, ew_ref,
 ):
-    _, cells_x, cells_y, cells_z = prevv_ref.shape
-    fetched = ((stiff_ref, raw_ref), (yabove_ref, above_ref), (ybelow_ref, below_ref), (edge_ref, own_ref),
-               (prev_ref, prevv_ref), (shares_ref, parts_ref))
-    copies = [pltpu.make_async_copy(a, b, sems.at[k]) for k, (a, b) in enumerate(fetched)]
-    for copy in copies:
-        copy.start()
+    _, cells_x, cells_y, cells_z = prev_ref.shape
     first = wall_lane()
     scale = wall_scale(count_z, cells_z)
     main = pl.ds(TOP + 2, cells_y)
@@ -357,16 +355,14 @@
     def assemble(ch, x):
         at = (ch * cells_x + x) * HALO
         plane = u0_ref.at[ch, x] if ch < 3 else s_ref.at[x]
-        plane[main, :] = prevv_ref[ch, x] if ch < 3 else raw_ref[x] * scale
-        plane[TOP - 1 : TOP + 2, :] = below_ref[at : at + HALO, :]
-        plane[TOP + 2 + cells_y : TOP + 2 + cells_y + HALO, :] = above_ref[at : at + HALO, :]
-
-    for copy in copies[:4]:
-        copy.wait()
+        plane[main, :] = prev_ref[ch, x] if ch < 3 else stiff_ref[x] * scale
+        plane[TOP - 1 : TOP + 2, :] = ybelow_ref[at : at + HALO, :]
+        plane[TOP + 2 + cells_y : TOP + 2 + cells_y + HALO, :] = yabove_ref[at : at + HALO, :]
+
     for x in range(cells_x):
         assemble(3, x)
     for ch in range(4):
-        fill(widev_ref.at[ch], below_ref, own_ref[ch], above_ref, (4 * cells_x + ch) * HALO)
+        fill(widev_ref.at[ch], ybelow_ref, edge_ref[ch], yabove_ref, (4 * cells_x + ch) * HALO)
     es_ref[WINDOW, :] = widev_ref[3]
     cs_ref[...] = zeros()
     for x in (0, cells_x - 1):
@@ -386,8 +382,6 @@
     for k, weight in enumerate(normalised(es_ref[WINDOW, :], others)):
         ew_ref[k] = weight
 
-    for copy in copies[4:]:
-        copy.wait()
     for ch in range(3):
         e_ref[0, ch, WINDOW, :] = widev_ref[ch]
         for x in range(cells_x):
@@ -396,9 +390,9 @@
 
     @pl.when(lax.axis_index("gz") == 0)
     def _():
-        share = parts_ref[0]
-        for k in range(1, parts_ref.shape[0]):
-            share = share + parts_ref[k]
+        share = shares_ref[0]
+        for k in range(1, shares_ref.shape[0]):
+            share = share + shares_ref[k]
         half = share.shape[0]
         rbf_ref[WIN - half :, :] = roll_lanes(share, LANES // 2)
         rbf_ref[:half, :] = share
@@ -452,25 +446,21 @@
                 others = beside_edge(e_ref.at[sweep, ch], zeros(), c_ref[sweep, ch])
                 weights = [ew_ref[k] for k in range(6)]
                 e_ref[sweep + 1, ch, WINDOW, :] = relaxed(e_ref[sweep, ch, WINDOW, :], others, weights)
-    inside = pl.ds(HALO, cells_x - 2 * HALO)
-    copies = [
-        pltpu.make_async_copy(done_ref.at[ch, inside], out_ref.at[ch, inside], sems.at[6 + ch]) for ch in range(3)
-    ]
-    for copy in copies:
-        copy.start()
-    for copy in copies:
-        copy.wait()
 
 
 def outer_kernel(
-    u0_ref, u1_ref, u2_ref, s_ref, w_ref, wide_ref, es_ref, cs_ref, c_ref, rbf_ref, xabove_ref, xbelow_ref, _,
+    u0_ref, u1_ref, u2_ref, s_ref, w_ref, wide_ref, es_ref, cs_ref, c_ref, rbf_ref, done_ref, xabove_ref, xbelow_ref,
     out_ref,
-    h0_ref, h1_ref, h2_ref, hs_ref, hw_ref, e_ref, eside_ref, ew_ref, c1_ref, done_ref, sem,
+    h0_ref, h1_ref, h2_ref, hs_ref, hw_ref, e_ref, eside_ref, ew_ref, new_ref, sems,
 ):
     _, cells_x, _, _ = u0_ref.shape
     cells_y = done_ref.shape[2]
     lane = lane_ids()
     first = wall_lane()
+    inside = pl.ds(HALO, cells_x - 2 * HALO)
+    copies = [pltpu.make_async_copy(done_ref.at[ch, inside], out_ref.at[ch, inside], sems.at[ch]) for ch in range(3)]
+    for copy in copies:
+        copy.start()
 
     def held(x):
         return x + HALO if x < HALO else x - cells_x + HALO + 6
@@ -548,7 +538,11 @@
                 )
                 new = jnp.where(first, own, relaxed(own, others, weights))
                 if last:
-                    done_ref[ch, x if x < HALO else x - cells_x + 2 * HALO] = new[2 : 2 + cells_y]
+                    place = x if x < HALO else x - cells_x + 2 * HALO
+                    new_ref[ch, place] = new[2 : 2 + cells_y]
+                    sem = sems.at[3 + 6 * ch + place]
+                    copies.append(pltpu.make_async_copy(new_ref.at[ch, place], out_ref.at[ch, x], sem))
+                    copies[-1].start()
                 else:
                     (h1_ref, h2_ref)[sweep][ch, held(x), WINDOW, :] = new
         if last:
@@ -570,18 +564,6 @@
                 e_ref[sweep + 1, ch, tile, WINDOW, :] = relaxed(
                     e_ref[sweep, ch, tile, WINDOW, :], others, weights
                 )
-    copies = []
-    for ch in range(3):
-        for side, x in enumerate((0, cells_x - HALO)):
-            copies.append(
-                pltpu.make_async_copy(
-                    done_ref.at[ch, pl.ds(side * HALO, HALO)],
-                    out_ref.at[ch, pl.ds(x, HALO)],
-                    sem.at[2 * ch + side],
-                )
-            )
-    for copy in copies:
-        copy.start()
     for copy in copies:
         copy.wait()
 
@@ -613,17 +595,29 @@
             f32(rows_y, LANES),
         ),
         2000 * MEGA,
-        (centre_coef.T, centre_index[None]),
+        (),
         (
             scratch((3, cells_x, cells_y, LANES), num),
             scratch((cells_x, cells_y, LANES), num),
             scratch((4, cells_y, LANES), num),
-            pltpu.SemaphoreType.DMA((4,)),
+            scratch((3, centre_index.shape[0]), num),
+            scratch((1, centre_index.shape[0]), jnp.int32),
+            pltpu.SemaphoreType.DMA((6,)),
         ),
-        far=tuple(pltpu.with_memory_space_constraint(a, pltpu.HBM) for a in (prev_disp, stiff_factor)),
+        far=tuple(in_hbm(a) for a in (prev_disp, stiff_factor, centre_coef.T, centre_index[None])),
     )
     centres = lax.all_to_all(rows.reshape(blocks, 1, LANES), ("gx", "gy"), 0, 0, tiled=True)
     zabove, zbelow = step(low, "gz", -1), step(high, "gz", 1)
+
+    rows_all = -(-(rows_y + 4 * HALO) // 8) * 8
+    edge, ylow, yhigh = kernel_call(
+        pack_y_kernel,
+        "pack_y",
+        (f32(4, cells_y, LANES), f32(rows_all, LANES), f32(rows_all, LANES)),
+        300 * MEGA,
+        (zabove, zbelow, ylow, yhigh),
+    )
+    yabove, ybelow = step(ylow, "gy", -1), step(yhigh, "gy", 1)
 
     table = stencil(count_x, count_y, count_z)
     (share,) = kernel_call(
@@ -633,32 +627,21 @@
         1500 * MEGA,
         (centres.reshape(blocks, LANES),),
         (scratch((ROWS, LANES), num),),
+        after=(ylow,),
     )
     shares = lax.all_to_all(share, "gz", 0, 0, tiled=True)
-
-    rows_all = -(-(rows_y + 4 * HALO) // 8) * 8
-    edge, ylow, yhigh = kernel_call(
-        pack_y_kernel,
-        "pack_y",
-        (f32(4, cells_y, LANES), f32(rows_all, LANES), f32(rows_all, LANES)),
-        300 * MEGA,
-        (zabove, zbelow, ylow, yhigh),
-        after=(share,),
-    )
-    yabove, ybelow = step(ylow, "gy", -1), step(yhigh, "gy", 1)
 
     xlow, xhigh = kernel_call(
         functools.partial(pack_x_kernel, float(count_z)),
         "pack_x",
         (f32(4 * HALO + 1, WIN, LANES), f32(4 * HALO + 1, WIN, LANES)),
-        1000 * MEGA,
-        (edge, yabove, ybelow),
-        (scratch((2, 4, HALO, cells_y, LANES), num), scratch((4, WIN, LANES), num), pltpu.SemaphoreType.DMA((2, 4))),
-        far=(prev_disp, stiff_factor),
+        8000 * MEGA,
+        (edge, yabove, ybelow, prev_disp, stiff_factor),
+        (scratch((4, WIN, LANES), num),),
     )
     xabove, xbelow = step(xlow, "gx", -1), step(xhigh, "gx", 1)
 
-    u0, u1, u2, s, w, es, cs, c, rbf, wide, out = kernel_call(
+    u0, u1, u2, s, w, es, cs, c, rbf, wide, done = kernel_call(
         functools.partial(inner_kernel, float(count_z)),
         "inner",
         (
@@ -672,23 +655,14 @@
             near(2, 3, WIN, LANES),
             near(WIN, LANES),
             near(4, WIN, LANES),
-            Far((3, cells_x, cells_y, cells_z), num),
+            near(3, cells_x, cells_y, cells_z),
         ),
         9000 * MEGA,
-        (),
+        (prev_disp, stiff_factor, in_hbm(edge), yabove, ybelow, shares),
         (
-            scratch((3, cells_x, cells_y, LANES), num),
-            scratch((cells_x, cells_y, LANES), num),
-            scratch((4, cells_y, LANES), num),
-            scratch((rows_all, LANES), num),
-            scratch((rows_all, LANES), num),
-            scratch((depth, HALF, LANES), num),
             scratch((3, 3, ROWS, LANES), num),
             scratch((6, WIN, LANES), num),
-            scratch((3, cells_x, cells_y, LANES), num),
-            pltpu.SemaphoreType.DMA((9,)),
         ),
-        far=(prev_disp, stiff_factor, edge, yabove, ybelow, shares),
     )
 
     (out,) = kernel_call(
@@ -696,7 +670,7 @@
         "outer",
         (Far((3, cells_x, cells_y, cells_z), num),),
         5500 * MEGA,
-        (u0, u1, u2, s, w, wide, es, cs, c, rbf, xabove, xbelow),
+        (u0, u1, u2, s, w, wide, es, cs, c, rbf, done, xabove, xbelow),
         (
             scratch((3, 12, ROWS, LANES), num),
             scratch((3, 12, ROWS, LANES), num),
@@ -706,12 +680,9 @@
             scratch((3, 3, 2, ROWS, LANES), num),
             scratch((ROWS, LANES), num),
             scratch((6, 2, WIN, LANES), num),
-            scratch((WIN, LANES), num),
             scratch((3, 2 * HALO, cells_y, LANES), num),
-            pltpu.SemaphoreType.DMA((6,)),
+            pltpu.SemaphoreType.DMA((21,)),
         ),
-        far=(out,),
-        aliases={12: 0},
     )
     return out
 

time: 75.3 us -> 73.8 us (0.980)
  waiting for transfers between devices: 3.28 us -> 7.82 us
  local copies, waits for them, and re-layouts: 2.25 us -> 0.01 us
  Pallas kernels: 22.2 us -> 20 us
  starting transfers between devices: 46.5 us -> 45.2 us
    all_to_all x1, waiting for transfers between devices: 0.01 us -> 4.63 us  [body(): lax.all_to_all(rows.reshape(blocks, 1, LANES), ('gx', 'gy'), 0, 0, tiled=...]
    ppermute x6, waiting for transfers between devices: 3.27 us -> 0.02 us  [step(): lax.ppermute(value, axis, [(i, i + by) for i in range(size) if 0 <= i + b...]
    all_to_all x1, starting transfers between devices: 14.6 us -> 11.4 us  [body(): lax.all_to_all(rows.reshape(blocks, 1, LANES), ('gx', 'gy'), 0, 0, tiled=...]
    all_to_all x1, waiting for transfers between devices: 0.01 us -> 3.18 us  [body(): shares = lax.all_to_all(share, 'gz', 0, 0, tiled=True)]
    unnamed x12 -> x6, local copies, waits for them, and re-layouts: 2.25 us -> 0.01 us
    pallas_call x6, Pallas kernels: 22.2 us -> 20 us  [kernel_call(): pl.pallas_call(kernel, name=name, out_shape=outs, in_specs=[pl.BlockSpec(...]
    ppermute x6, starting transfers between devices: 21.9 us -> 23.5 us  [step(): lax.ppermute(value, axis, [(i, i + by) for i in range(size) if 0 <= i + b...]
  transfers between devices with their start and end apart: 8 -> 8, of which waited for: 1 -> 2; matrix products, arithmetic and copies ran while one was open for 0% -> 0% of each run, Pallas kernels for 20% -> 17%
where the time goes in v4:
time: 73.8 us; the launch traced here: 73.3 us
  starting transfers between devices  45.2 us (61%)
  Pallas kernels  20 us (27%)
  waiting for transfers between devices  7.82 us (11%)
    ppermute x6, starting transfers between devices, step(): lax.ppermute(value, axis, [(i, i + by) for i in range(size) if 0 <= i + b...  23.5 us
    pallas_call x6, Pallas kernels, kernel_call(): pl.pallas_call(kernel, name=name, out_shape=outs, in_specs=[pl.BlockSpec(...  20 us
    all_to_all x1, starting transfers between devices, body(): lax.all_to_all(rows.reshape(blocks, 1, LANES), ('gx', 'gy'), 0, 0, tiled=...  11.4 us
    all_to_all x1, starting transfers between devices, body(): shares = lax.all_to_all(share, 'gz', 0, 0, tiled=True)  10.3 us
    all_to_all x1, waiting for transfers between devices, body(): lax.all_to_all(rows.reshape(blocks, 1, LANES), ('gx', 'gy'), 0, 0, tiled=...  4.63 us
    all_to_all x1, waiting for transfers between devices, body(): shares = lax.all_to_all(share, 'gz', 0, 0, tiled=True)  3.18 us
  transfers between devices with their start and end apart: 8, of which 2 were waited for; matrix products, arithmetic and copies ran while one was open for 0% of the time, Pallas kernels for 17%

profile of v4, /device:TPU:1, one launch (start us, length us, event | category | flops | bytes accessed | tf_op | source)
XLA Modules:
  0.0 73.3 jit_solution(10782383660275107197)
XLA Ops:
  0.0 2.4 %pack_z.1 = (f32[64,128]{1,0:T(8,128)}, f32[2,64,128]{2,1,0:T(8,128)S(1)}, f32[2,64,128]{2,1,0:T(8,128)S(1)}, f32[192,128]{1,0:T(8,128)S(1)}, f32[192,128]{1,0:T(8,128)S(1)}) custom-call(f32[3,16,64,128]{3,2,1,0:T(8,128)} %prev_ref.5, f32[16,64,128]{2,1,0:T(8,128)} %stiff_ref.5, f32[3,32]{1,0:T(4,128)} %bitcast.7, s32[1,32]{1,0:T(1,128)} %bitcast.8), custom_call_target="tpu_custom_call" | custom-call | flops 2200000000 | bytes 360448 | tf_op jit(solution)/shard_map/pack_z/pallas_call | solution.py:38
  2.4 1.3 %collective-permute-start = (f32[2,64,128]{2,1,0:T(8,128)S(1)}, f32[2,64,128]{2,1,0:T(8,128)S(1)}, u32[]{:S(2)}, u32[]{:S(2)}) collective-permute-start(f32[2,64,128]{2,1,0:T(8,128)S(1)} %get-tuple-element.26), channel_id=1, source_target_pairs={{1,0},{2,1},{3,2},{4,3},{5,4},{6,5},{7,6},{9,8},{10,9},{11,10},{12... | collective-permute-start | bytes 196616 | tf_op jit(solution)/shard_map/ppermute | solution.py:573
  3.7 12.1 %collective-permute-start.1 = (f32[2,64,128]{2,1,0:T(8,128)S(1)}, f32[2,64,128]{2,1,0:T(8,128)S(1)}, u32[]{:S(2)}, u32[]{:S(2)}) collective-permute-start(f32[2,64,128]{2,1,0:T(8,128)S(1)} %get-tuple-element.27), channel_id=1, source_target_pairs={{0,1},{1,2},{2,3},{3,4},{4,5},{5,6},{6,7},{8,9},{9,10},{10,11},{11... | collective-permute-start | bytes 196616 | tf_op jit(solution)/shard_map/ppermute | solution.py:573
  15.8 11.4 %all-to-all-start = ((f32[64,1,128]{2,1,0:T(1,128)}), f32[64,1,128]{2,1,0:T(1,128)S(1)}, u32[]{:S(2)}, u32[]{:S(2)}) async-start(f32[64,1,128]{2,1,0:T(1,128)} %bitcast.3), calls=%async_computation | async-start | bytes 65536 | tf_op jit(solution)/shard_map/all_to_all | solution.py:609
  27.2 0.0 collective-permute-done.above_ref
  27.2 0.0 collective-permute-done.1.below_ref
  27.2 0.1 pack_y.1
  27.3 0.0 copy-start.2
  27.3 3.3 %collective-permute-start.3 = (f32[208,128]{1,0:T(8,128)S(1)}, f32[208,128]{1,0:T(8,128)S(1)}, u32[]{:S(2)}, u32[]{:S(2)}) collective-permute-start(f32[208,128]{1,0:T(8,128)S(1)} %get-tuple-element.32), channel_id=1, source_target_pairs={{0,8},{8,16},{16,24},{1,9},{9,17},{17,25},{2,10},{10,18},{18,26},{... | collective-permute-start | bytes 319496 | tf_op jit(solution)/shard_map/ppermute | solution.py:573
  30.6 1.3 %collective-permute-start.2 = (f32[208,128]{1,0:T(8,128)S(1)}, f32[208,128]{1,0:T(8,128)S(1)}, u32[]{:S(2)}, u32[]{:S(2)}) collective-permute-start(f32[208,128]{1,0:T(8,128)S(1)} %get-tuple-element.31._), channel_id=1, source_target_pairs={{8,0},{16,8},{24,16},{9,1},{17,9},{25,17},{10,2},{18,10},{26,18},{... | collective-permute-start | bytes 319496 | tf_op jit(solution)/shard_map/ppermute | solution.py:573
  31.9 4.6 %all-to-all-done = f32[64,1,128]{2,1,0:T(1,128)S(1)} async-done(((f32[64,1,128]{2,1,0:T(1,128)}), f32[64,1,128]{2,1,0:T(1,128)S(1)}, u32[]{:S(2)}, u32[]{:S(2)}) %all-to-all-start) | async-done | bytes 32800 | tf_op jit(solution)/shard_map/all_to_all | solution.py:609
  36.5 0.0 copy-start
  36.5 0.0 copy-start.1
  36.5 1.5 %rbf.1 = f32[8,40,128]{2,1,0:T(8,128)} custom-call(f32[64,128]{1,0:T(8,128)S(1)} %bitcast.6, f32[208,128]{1,0:T(8,128)S(1)} %get-tuple-element.31._), custom_call_target="tpu_custom_call" | custom-call | flops 1650000000 | bytes 196608 | tf_op jit(solution)/shard_map/rbf/pallas_call | solution.py:38
  38.1 10.3 %all-to-all-start.1 = ((f32[8,40,128]{2,1,0:T(8,128)}), f32[8,40,128]{2,1,0:T(8,128)S(1)}, u32[]{:S(2)}, u32[]{:S(2)}) async-start(f32[8,40,128]{2,1,0:T(8,128)} %rbf.1), calls=%async_computation.1 | async-start | bytes 327680 | tf_op jit(solution)/shard_map/all_to_all | solution.py:632
  48.4 0.0 collective-permute-done.3.ybelow_ref
  48.4 0.0 collective-permute-done.2.yabove_ref
  48.4 0.0 copy-done.2
  48.4 0.0 copy-done
  48.4 0.0 copy-done.1
  48.4 0.9 %pack_x.1 = (f32[13,72,128]{2,1,0:T(8,128)}, f32[13,72,128]{2,1,0:T(8,128)S(1)}) custom-call(f32[4,64,128]{2,1,0:T(8,128)S(1)} %get-tuple-element.30.edge_ref, f32[208,128]{1,0:T(8,128)S(1)} %collective-permute-done.2.yabove_ref, f32[208,128]{1,0:T(8,128)S(1)} %collective-permute-done.3.ybelow_ref, f32[3,16,64,128]{3,2,1,0:T(8,128)S(1)} %copy-done, ...), custom_call_target="tpu_custom_call" | custom-call | flops 8800000000 | bytes 3399680 | tf_op jit(solution)/shard_map/pack_x/pallas_call | solution.py:38
  49.3 3.1 %collective-permute-start.4 = (f32[13,72,128]{2,1,0:T(8,128)}, f32[13,72,128]{2,1,0:T(8,128)S(1)}, u32[]{:S(2)}, u32[]{:S(2)}) collective-permute-start(f32[13,72,128]{2,1,0:T(8,128)} %get-tuple-element.45), channel_id=1, source_target_pairs={{32,0},{64,32},{96,64},{128,96},{160,128},{192,160},{224,192},{256... | collective-permute-start | bytes 1437704 | tf_op jit(solution)/shard_map/ppermute | solution.py:573
  52.4 2.4 %collective-permute-start.5 = (f32[13,72,128]{2,1,0:T(8,128)S(1)}, f32[13,72,128]{2,1,0:T(8,128)}, u32[]{:S(2)}, u32[]{:S(2)}) collective-permute-start(f32[13,72,128]{2,1,0:T(8,128)S(1)} %get-tuple-element.46), channel_id=1, source_target_pairs={{0,32},{32,64},{64,96},{96,128},{128,160},{160,192},{192,224},{224... | collective-permute-start | bytes 1437704 | tf_op jit(solution)/shard_map/ppermute | solution.py:573
  54.9 3.2 %all-to-all-done.1.shares_ref = f32[8,40,128]{2,1,0:T(8,128)S(1)} async-done(((f32[8,40,128]{2,1,0:T(8,128)}), f32[8,40,128]{2,1,0:T(8,128)S(1)}, u32[]{:S(2)}, u32[]{:S(2)}) %all-to-all-start.1) | async-done | bytes 163872 | tf_op jit(solution)/shard_map/all_to_all | solution.py:632
  58.0 10.0 %inner.1 = (f32[3,16,88,128]{3,2,1,0:T(8,128)S(1)}, f32[3,16,88,128]{3,2,1,0:T(8,128)S(1)}, f32[3,16,88,128]{3,2,1,0:T(8,128)S(1)}, f32[16,88,128]{2,1,0:T(8,128...) custom-call(f32[3,16,64,128]{3,2,1,0:T(8,128)S(1)} %copy-done, ...), custom_call_target="tpu_custom_call" | custom-call | flops 9900000256 | bytes 15413248 | tf_op jit(solution)/shard_map/inner/pallas_call | solution.py:38
  68.1 0.0 collective-permute-done.4.xabove_ref
  68.1 0.0 collective-permute-done.5.xbelow_ref
  68.1 5.1 %outer.1 = f32[3,16,64,128]{3,2,1,0:T(8,128)} custom-call(f32[3,16,88,128]{3,2,1,0:T(8,128)S(1)} %get-tuple-element.34.u0_ref, f32[3,16,88,128]{3,2,1,0:T(8,128)S(1)} %get-tuple-element.35.u1_ref, f32[3,16,88,128]{3,2,1,0:T(8,128)S(1)} %get-tuple-element.36.u2_ref, f32[16,88,128]{2,1,0:T(8,128)S(1)} %get-tuple-element.37.s_ref, ...), custom_call_target="tpu_custom_call" | custom-call | flops 6049999872 | bytes 15339520 | tf_op jit(solution)/shard_map/outer/pallas_call | solution.py:38
Async XLA Ops:
  2.4 24.8 %collective-permute-start = (f32[2,64,128]{2,1,0:T(8,128)S(1)}, f32[2,64,128]{2,1,0:T(8,128)S(1)}, u32[]{:S(2)}, u32[]{:S(2)}) collective-permute-start(f32[2,64,128]{2,1,0:T(8,128)S(1)} %get-tuple-element.26), channel_id=1, source_target_pairs={{1,0},{2,1},{3,2},{4,3},{5,4},{6,5},{7,6},{9,8},{10,9},{11,10},{12... | collective-permute-start | bytes 196616 | tf_op jit(solution)/shard_map/ppermute | solution.py:573
  3.7 23.5 %collective-permute-start.1 = (f32[2,64,128]{2,1,0:T(8,128)S(1)}, f32[2,64,128]{2,1,0:T(8,128)S(1)}, u32[]{:S(2)}, u32[]{:S(2)}) collective-permute-start(f32[2,64,128]{2,1,0:T(8,128)S(1)} %get-tuple-element.27), channel_id=1, source_target_pairs={{0,1},{1,2},{2,3},{3,4},{4,5},{5,6},{6,7},{8,9},{9,10},{10,11},{11... | collective-permute-start | bytes 196616 | tf_op jit(solution)/shard_map/ppermute | solution.py:573
  15.8 20.7 %all-to-all-start = ((f32[64,1,128]{2,1,0:T(1,128)}), f32[64,1,128]{2,1,0:T(1,128)S(1)}, u32[]{:S(2)}, u32[]{:S(2)}) async-start(f32[64,1,128]{2,1,0:T(1,128)} %bitcast.3), calls=%async_computation | async-start | bytes 65536 | tf_op jit(solution)/shard_map/all_to_all | solution.py:609
  27.3 21.1 %copy-start.2 = (f32[4,64,128]{2,1,0:T(8,128)}, f32[4,64,128]{2,1,0:T(8,128)S(1)}, u32[]{:S(2)}) copy-start(f32[4,64,128]{2,1,0:T(8,128)S(1)} %get-tuple-element.30.edge_ref) | copy-start | bytes 393220
  27.3 21.1 %collective-permute-start.3 = (f32[208,128]{1,0:T(8,128)S(1)}, f32[208,128]{1,0:T(8,128)S(1)}, u32[]{:S(2)}, u32[]{:S(2)}) collective-permute-start(f32[208,128]{1,0:T(8,128)S(1)} %get-tuple-element.32), channel_id=1, source_target_pairs={{0,8},{8,16},{16,24},{1,9},{9,17},{17,25},{2,10},{10,18},{18,26},{... | collective-permute-start | bytes 319496 | tf_op jit(solution)/shard_map/ppermute | solution.py:573
  30.6 17.8 %collective-permute-start.2 = (f32[208,128]{1,0:T(8,128)S(1)}, f32[208,128]{1,0:T(8,128)S(1)}, u32[]{:S(2)}, u32[]{:S(2)}) collective-permute-start(f32[208,128]{1,0:T(8,128)S(1)} %get-tuple-element.31._), channel_id=1, source_target_pairs={{8,0},{16,8},{24,16},{9,1},{17,9},{25,17},{10,2},{18,10},{26,18},{... | collective-permute-start | bytes 319496 | tf_op jit(solution)/shard_map/ppermute | solution.py:573
  36.5 11.9 %copy-start = (f32[3,16,64,128]{3,2,1,0:T(8,128)S(1)}, f32[3,16,64,128]{3,2,1,0:T(8,128)}, u32[]{:S(2)}) copy-start(f32[3,16,64,128]{3,2,1,0:T(8,128)} %prev_ref.5) | copy-start | bytes 4718596
  36.5 11.9 %copy-start.1 = (f32[16,64,128]{2,1,0:T(8,128)S(1)}, f32[16,64,128]{2,1,0:T(8,128)}, u32[]{:S(2)}) copy-start(f32[16,64,128]{2,1,0:T(8,128)} %stiff_ref.5) | copy-start | bytes 1572868
  38.1 20.0 %all-to-all-start.1 = ((f32[8,40,128]{2,1,0:T(8,128)}), f32[8,40,128]{2,1,0:T(8,128)S(1)}, u32[]{:S(2)}, u32[]{:S(2)}) async-start(f32[8,40,128]{2,1,0:T(8,128)} %rbf.1), calls=%async_computation.1 | async-start | bytes 327680 | tf_op jit(solution)/shard_map/all_to_all | solution.py:632
  49.3 18.8 %collective-permute-start.4 = (f32[13,72,128]{2,1,0:T(8,128)}, f32[13,72,128]{2,1,0:T(8,128)S(1)}, u32[]{:S(2)}, u32[]{:S(2)}) collective-permute-start(f32[13,72,128]{2,1,0:T(8,128)} %get-tuple-element.45), channel_id=1, source_target_pairs={{32,0},{64,32},{96,64},{128,96},{160,128},{192,160},{224,192},{256... | collective-permute-start | bytes 1437704 | tf_op jit(solution)/shard_map/ppermute | solution.py:573
  52.4 15.7 %collective-permute-start.5 = (f32[13,72,128]{2,1,0:T(8,128)S(1)}, f32[13,72,128]{2,1,0:T(8,128)}, u32[]{:S(2)}, u32[]{:S(2)}) collective-permute-start(f32[13,72,128]{2,1,0:T(8,128)S(1)} %get-tuple-element.46), channel_id=1, source_target_pairs={{0,32},{32,64},{64,96},{96,128},{128,160},{160,192},{192,224},{224... | collective-permute-start | bytes 1437704 | tf_op jit(solution)/shard_map/ppermute | solution.py:573

commit v5 on v4

--- a/solution.py
+++ b/solution.py
@@ -364,9 +364,10 @@
     for ch in range(4):
         fill(widev_ref.at[ch], ybelow_ref, edge_ref[ch], yabove_ref, (4 * cells_x + ch) * HALO)
     es_ref[WINDOW, :] = widev_ref[3]
-    cs_ref[...] = zeros()
-    for x in (0, cells_x - 1):
-        cs_ref[...] = to_edge(cs_ref[...], s_ref[x, WINDOW, :], x)
+    ends = zeros()
+    for x in range(cells_x):
+        ends = to_edge(ends, s_ref[x, WINDOW, :], x)
+    cs_ref[...] = ends
 
     def weigh(x, carry):
         own = s_ref[x, WINDOW, :]
@@ -374,10 +375,10 @@
         others = (s_ref[x - 1, WINDOW, :], s_ref[x + 1, WINDOW, :], s_ref[x, BEFORE, :], s_ref[x, AFTER, :], down, up)
         for k, weight in enumerate(normalised(own, others)):
             w_ref[k, x] = weight
-        cs_ref[...] = to_edge(cs_ref[...], own, x)
         return carry
 
-    lax.fori_loop(1, cells_x - 1, weigh, 0, unroll=14)
+    for x in range(1, cells_x - 1):
+        weigh(x, 0)
     others = beside_edge(es_ref, zeros(), cs_ref[...])
     for k, weight in enumerate(normalised(es_ref[WINDOW, :], others)):
         ew_ref[k] = weight
@@ -405,14 +406,8 @@
                 u0_ref[ch, x, WINDOW, :] = jnp.where(own, column, u0_ref[ch, x, WINDOW, :])
             return carry
 
-        lax.fori_loop(0, cells_x, layer, 0, unroll=16)
-
-    for ch in range(3):
-        ends = zeros()
         for x in range(cells_x):
-            ends = to_edge(ends, u0_ref[ch, x, WINDOW, :], x)
-        c_ref[0, ch] = ends
-        c_ref[1, ch] = zeros()
+            layer(x, 0)
 
     stages = (u0_ref, u1_ref, u2_ref)
     for sweep in range(SWEEPS):
@@ -436,14 +431,17 @@
                     done_ref[ch, x] = new[2 : 2 + cells_y]
                 else:
                     stages[sweep + 1][ch, x, WINDOW, :] = new
-                if sweep == 0:
-                    c_ref[1, ch] = to_edge(c_ref[1, ch], new, x)
             return carry
 
-        lax.fori_loop(1 + sweep, cells_x - 1 - sweep, relax, 0, unroll=(14, 12, 10)[sweep])
+        for x in range(1 + sweep, cells_x - 1 - sweep):
+            relax(x, 0)
         if not last:
             for ch in range(3):
-                others = beside_edge(e_ref.at[sweep, ch], zeros(), c_ref[sweep, ch])
+                ends = zeros()
+                for x in range(sweep, cells_x - sweep):
+                    ends = to_edge(ends, now[ch, x, WINDOW, :], x)
+                c_ref[sweep, ch] = ends
+                others = beside_edge(e_ref.at[sweep, ch], zeros(), ends)
                 weights = [ew_ref[k] for k in range(6)]
                 e_ref[sweep + 1, ch, WINDOW, :] = relaxed(e_ref[sweep, ch, WINDOW, :], others, weights)
 

time: 73.8 us -> 71.3 us (0.966)
  Pallas kernels: 20 us -> 17.6 us
    pallas_call x6, Pallas kernels: 20 us -> 17.6 us  [kernel_call(): pl.pallas_call(kernel, name=name, out_shape=outs, in_specs=[pl.BlockSpec(...]
  transfers between devices with their start and end apart: 8 -> 8, of which waited for: 2 -> 2; matrix products, arithmetic and copies ran while one was open for 0% -> 0% of each run, Pallas kernels for 17% -> 14%
where the time goes in v5:
time: 71.3 us; the launch traced here: 70.9 us
  starting transfers between devices  45.2 us (63%)
  Pallas kernels  17.6 us (25%)
  waiting for transfers between devices  7.82 us (11%)
    ppermute x6, starting transfers between devices, step(): lax.ppermute(value, axis, [(i, i + by) for i in range(size) if 0 <= i + b...  23.5 us
    pallas_call x6, Pallas kernels, kernel_call(): pl.pallas_call(kernel, name=name, out_shape=outs, in_specs=[pl.BlockSpec(...  17.6 us
    all_to_all x1, starting transfers between devices, body(): lax.all_to_all(rows.reshape(blocks, 1, LANES), ('gx', 'gy'), 0, 0, tiled=...  11.4 us
    all_to_all x1, starting transfers between devices, body(): shares = lax.all_to_all(share, 'gz', 0, 0, tiled=True)  10.3 us
    all_to_all x1, waiting for transfers between devices, body(): lax.all_to_all(rows.reshape(blocks, 1, LANES), ('gx', 'gy'), 0, 0, tiled=...  4.63 us
    all_to_all x1, waiting for transfers between devices, body(): shares = lax.all_to_all(share, 'gz', 0, 0, tiled=True)  3.18 us
  transfers between devices with their start and end apart: 8, of which 2 were waited for; matrix products, arithmetic and copies ran while one was open for 0% of the time, Pallas kernels for 14%

profile of v5, /device:TPU:1, one launch (start us, length us, event | category | flops | bytes accessed | tf_op | source)
XLA Modules:
  0.0 70.9 jit_solution(5447016057734944767)
XLA Ops:
  0.0 2.4 %pack_z.1 = (f32[64,128]{1,0:T(8,128)}, f32[2,64,128]{2,1,0:T(8,128)S(1)}, f32[2,64,128]{2,1,0:T(8,128)S(1)}, f32[192,128]{1,0:T(8,128)S(1)}, f32[192,128]{1,0:T(8,128)S(1)}) custom-call(f32[3,16,64,128]{3,2,1,0:T(8,128)} %prev_ref.5, f32[16,64,128]{2,1,0:T(8,128)} %stiff_ref.5, f32[3,32]{1,0:T(4,128)} %bitcast.7, s32[1,32]{1,0:T(1,128)} %bitcast.8), custom_call_target="tpu_custom_call" | custom-call | flops 2200000000 | bytes 360448 | tf_op jit(solution)/shard_map/pack_z/pallas_call | solution.py:38
  2.4 1.3 %collective-permute-start = (f32[2,64,128]{2,1,0:T(8,128)S(1)}, f32[2,64,128]{2,1,0:T(8,128)S(1)}, u32[]{:S(2)}, u32[]{:S(2)}) collective-permute-start(f32[2,64,128]{2,1,0:T(8,128)S(1)} %get-tuple-element.26), channel_id=1, source_target_pairs={{1,0},{2,1},{3,2},{4,3},{5,4},{6,5},{7,6},{9,8},{10,9},{11,10},{12... | collective-permute-start | bytes 196616 | tf_op jit(solution)/shard_map/ppermute | solution.py:571
  3.7 12.1 %collective-permute-start.1 = (f32[2,64,128]{2,1,0:T(8,128)S(1)}, f32[2,64,128]{2,1,0:T(8,128)S(1)}, u32[]{:S(2)}, u32[]{:S(2)}) collective-permute-start(f32[2,64,128]{2,1,0:T(8,128)S(1)} %get-tuple-element.27), channel_id=1, source_target_pairs={{0,1},{1,2},{2,3},{3,4},{4,5},{5,6},{6,7},{8,9},{9,10},{10,11},{11... | collective-permute-start | bytes 196616 | tf_op jit(solution)/shard_map/ppermute | solution.py:571
  15.8 11.4 %all-to-all-start = ((f32[64,1,128]{2,1,0:T(1,128)}), f32[64,1,128]{2,1,0:T(1,128)S(1)}, u32[]{:S(2)}, u32[]{:S(2)}) async-start(f32[64,1,128]{2,1,0:T(1,128)} %bitcast.3), calls=%async_computation | async-start | bytes 65536 | tf_op jit(solution)/shard_map/all_to_all | solution.py:607
  27.2 0.0 collective-permute-done.above_ref
  27.2 0.0 collective-permute-done.1.below_ref
  27.2 0.1 pack_y.1
  27.3 0.0 copy-start.2
  27.3 3.3 %collective-permute-start.3 = (f32[208,128]{1,0:T(8,128)S(1)}, f32[208,128]{1,0:T(8,128)S(1)}, u32[]{:S(2)}, u32[]{:S(2)}) collective-permute-start(f32[208,128]{1,0:T(8,128)S(1)} %get-tuple-element.32), channel_id=1, source_target_pairs={{0,8},{8,16},{16,24},{1,9},{9,17},{17,25},{2,10},{10,18},{18,26},{... | collective-permute-start | bytes 319496 | tf_op jit(solution)/shard_map/ppermute | solution.py:571
  30.6 1.3 %collective-permute-start.2 = (f32[208,128]{1,0:T(8,128)S(1)}, f32[208,128]{1,0:T(8,128)S(1)}, u32[]{:S(2)}, u32[]{:S(2)}) collective-permute-start(f32[208,128]{1,0:T(8,128)S(1)} %get-tuple-element.31._), channel_id=1, source_target_pairs={{8,0},{16,8},{24,16},{9,1},{17,9},{25,17},{10,2},{18,10},{26,18},{... | collective-permute-start | bytes 319496 | tf_op jit(solution)/shard_map/ppermute | solution.py:571
  31.9 4.6 %all-to-all-done = f32[64,1,128]{2,1,0:T(1,128)S(1)} async-done(((f32[64,1,128]{2,1,0:T(1,128)}), f32[64,1,128]{2,1,0:T(1,128)S(1)}, u32[]{:S(2)}, u32[]{:S(2)}) %all-to-all-start) | async-done | bytes 32800 | tf_op jit(solution)/shard_map/all_to_all | solution.py:607
  36.5 0.0 copy-start
  36.5 0.0 copy-start.1
  36.5 1.5 %rbf.1 = f32[8,40,128]{2,1,0:T(8,128)} custom-call(f32[64,128]{1,0:T(8,128)S(1)} %bitcast.6, f32[208,128]{1,0:T(8,128)S(1)} %get-tuple-element.31._), custom_call_target="tpu_custom_call" | custom-call | flops 1650000000 | bytes 196608 | tf_op jit(solution)/shard_map/rbf/pallas_call | solution.py:38
  38.1 10.3 %all-to-all-start.1 = ((f32[8,40,128]{2,1,0:T(8,128)}), f32[8,40,128]{2,1,0:T(8,128)S(1)}, u32[]{:S(2)}, u32[]{:S(2)}) async-start(f32[8,40,128]{2,1,0:T(8,128)} %rbf.1), calls=%async_computation.1 | async-start | bytes 327680 | tf_op jit(solution)/shard_map/all_to_all | solution.py:630
  48.4 0.0 collective-permute-done.3.ybelow_ref
  48.4 0.0 collective-permute-done.2.yabove_ref
  48.4 0.0 copy-done.2
  48.4 0.0 copy-done
  48.4 0.0 copy-done.1
  48.4 0.9 %pack_x.1 = (f32[13,72,128]{2,1,0:T(8,128)}, f32[13,72,128]{2,1,0:T(8,128)S(1)}) custom-call(f32[4,64,128]{2,1,0:T(8,128)S(1)} %get-tuple-element.30.edge_ref, f32[208,128]{1,0:T(8,128)S(1)} %collective-permute-done.2.yabove_ref, f32[208,128]{1,0:T(8,128)S(1)} %collective-permute-done.3.ybelow_ref, f32[3,16,64,128]{3,2,1,0:T(8,128)S(1)} %copy-done, ...), custom_call_target="tpu_custom_call" | custom-call | flops 8800000000 | bytes 3399680 | tf_op jit(solution)/shard_map/pack_x/pallas_call | solution.py:38
  49.3 3.1 %collective-permute-start.4 = (f32[13,72,128]{2,1,0:T(8,128)}, f32[13,72,128]{2,1,0:T(8,128)S(1)}, u32[]{:S(2)}, u32[]{:S(2)}) collective-permute-start(f32[13,72,128]{2,1,0:T(8,128)} %get-tuple-element.45), channel_id=1, source_target_pairs={{32,0},{64,32},{96,64},{128,96},{160,128},{192,160},{224,192},{256... | collective-permute-start | bytes 1437704 | tf_op jit(solution)/shard_map/ppermute | solution.py:571
  52.4 2.4 %collective-permute-start.5 = (f32[13,72,128]{2,1,0:T(8,128)S(1)}, f32[13,72,128]{2,1,0:T(8,128)}, u32[]{:S(2)}, u32[]{:S(2)}) collective-permute-start(f32[13,72,128]{2,1,0:T(8,128)S(1)} %get-tuple-element.46), channel_id=1, source_target_pairs={{0,32},{32,64},{64,96},{96,128},{128,160},{160,192},{192,224},{224... | collective-permute-start | bytes 1437704 | tf_op jit(solution)/shard_map/ppermute | solution.py:571
  54.9 3.2 %all-to-all-done.1.shares_ref = f32[8,40,128]{2,1,0:T(8,128)S(1)} async-done(((f32[8,40,128]{2,1,0:T(8,128)}), f32[8,40,128]{2,1,0:T(8,128)S(1)}, u32[]{:S(2)}, u32[]{:S(2)}) %all-to-all-start.1) | async-done | bytes 163872 | tf_op jit(solution)/shard_map/all_to_all | solution.py:630
  58.0 7.6 %inner.1 = (f32[3,16,88,128]{3,2,1,0:T(8,128)S(1)}, f32[3,16,88,128]{3,2,1,0:T(8,128)S(1)}, f32[3,16,88,128]{3,2,1,0:T(8,128)S(1)}, f32[16,88,128]{2,1,0:T(8,128...) custom-call(f32[3,16,64,128]{3,2,1,0:T(8,128)S(1)} %copy-done, ...), custom_call_target="tpu_custom_call" | custom-call | flops 9900000256 | bytes 15413248 | tf_op jit(solution)/shard_map/inner/pallas_call | solution.py:38
  65.6 0.0 collective-permute-done.4.xabove_ref
  65.6 0.0 collective-permute-done.5.xbelow_ref
  65.6 5.1 %outer.1 = f32[3,16,64,128]{3,2,1,0:T(8,128)} custom-call(f32[3,16,88,128]{3,2,1,0:T(8,128)S(1)} %get-tuple-element.34.u0_ref, f32[3,16,88,128]{3,2,1,0:T(8,128)S(1)} %get-tuple-element.35.u1_ref, f32[3,16,88,128]{3,2,1,0:T(8,128)S(1)} %get-tuple-element.36.u2_ref, f32[16,88,128]{2,1,0:T(8,128)S(1)} %get-tuple-element.37.s_ref, ...), custom_call_target="tpu_custom_call" | custom-call | flops 6049999872 | bytes 15339520 | tf_op jit(solution)/shard_map/outer/pallas_call | solution.py:38
Async XLA Ops:
  2.4 24.8 %collective-permute-start = (f32[2,64,128]{2,1,0:T(8,128)S(1)}, f32[2,64,128]{2,1,0:T(8,128)S(1)}, u32[]{:S(2)}, u32[]{:S(2)}) collective-permute-start(f32[2,64,128]{2,1,0:T(8,128)S(1)} %get-tuple-element.26), channel_id=1, source_target_pairs={{1,0},{2,1},{3,2},{4,3},{5,4},{6,5},{7,6},{9,8},{10,9},{11,10},{12... | collective-permute-start | bytes 196616 | tf_op jit(solution)/shard_map/ppermute | solution.py:571
  3.7 23.5 %collective-permute-start.1 = (f32[2,64,128]{2,1,0:T(8,128)S(1)}, f32[2,64,128]{2,1,0:T(8,128)S(1)}, u32[]{:S(2)}, u32[]{:S(2)}) collective-permute-start(f32[2,64,128]{2,1,0:T(8,128)S(1)} %get-tuple-element.27), channel_id=1, source_target_pairs={{0,1},{1,2},{2,3},{3,4},{4,5},{5,6},{6,7},{8,9},{9,10},{10,11},{11... | collective-permute-start | bytes 196616 | tf_op jit(solution)/shard_map/ppermute | solution.py:571
  15.8 20.7 %all-to-all-start = ((f32[64,1,128]{2,1,0:T(1,128)}), f32[64,1,128]{2,1,0:T(1,128)S(1)}, u32[]{:S(2)}, u32[]{:S(2)}) async-start(f32[64,1,128]{2,1,0:T(1,128)} %bitcast.3), calls=%async_computation | async-start | bytes 65536 | tf_op jit(solution)/shard_map/all_to_all | solution.py:607
  27.3 21.1 %copy-start.2 = (f32[4,64,128]{2,1,0:T(8,128)}, f32[4,64,128]{2,1,0:T(8,128)S(1)}, u32[]{:S(2)}) copy-start(f32[4,64,128]{2,1,0:T(8,128)S(1)} %get-tuple-element.30.edge_ref) | copy-start | bytes 393220
  27.3 21.1 %collective-permute-start.3 = (f32[208,128]{1,0:T(8,128)S(1)}, f32[208,128]{1,0:T(8,128)S(1)}, u32[]{:S(2)}, u32[]{:S(2)}) collective-permute-start(f32[208,128]{1,0:T(8,128)S(1)} %get-tuple-element.32), channel_id=1, source_target_pairs={{0,8},{8,16},{16,24},{1,9},{9,17},{17,25},{2,10},{10,18},{18,26},{... | collective-permute-start | bytes 319496 | tf_op jit(solution)/shard_map/ppermute | solution.py:571
  30.6 17.8 %collective-permute-start.2 = (f32[208,128]{1,0:T(8,128)S(1)}, f32[208,128]{1,0:T(8,128)S(1)}, u32[]{:S(2)}, u32[]{:S(2)}) collective-permute-start(f32[208,128]{1,0:T(8,128)S(1)} %get-tuple-element.31._), channel_id=1, source_target_pairs={{8,0},{16,8},{24,16},{9,1},{17,9},{25,17},{10,2},{18,10},{26,18},{... | collective-permute-start | bytes 319496 | tf_op jit(solution)/shard_map/ppermute | solution.py:571
  36.5 11.9 %copy-start = (f32[3,16,64,128]{3,2,1,0:T(8,128)S(1)}, f32[3,16,64,128]{3,2,1,0:T(8,128)}, u32[]{:S(2)}) copy-start(f32[3,16,64,128]{3,2,1,0:T(8,128)} %prev_ref.5) | copy-start | bytes 4718596
  36.5 11.9 %copy-start.1 = (f32[16,64,128]{2,1,0:T(8,128)S(1)}, f32[16,64,128]{2,1,0:T(8,128)}, u32[]{:S(2)}) copy-start(f32[16,64,128]{2,1,0:T(8,128)} %stiff_ref.5) | copy-start | bytes 1572868
  38.1 20.0 %all-to-all-start.1 = ((f32[8,40,128]{2,1,0:T(8,128)}), f32[8,40,128]{2,1,0:T(8,128)S(1)}, u32[]{:S(2)}, u32[]{:S(2)}) async-start(f32[8,40,128]{2,1,0:T(8,128)} %rbf.1), calls=%async_computation.1 | async-start | bytes 327680 | tf_op jit(solution)/shard_map/all_to_all | solution.py:630
  49.3 16.3 %collective-permute-start.4 = (f32[13,72,128]{2,1,0:T(8,128)}, f32[13,72,128]{2,1,0:T(8,128)S(1)}, u32[]{:S(2)}, u32[]{:S(2)}) collective-permute-start(f32[13,72,128]{2,1,0:T(8,128)} %get-tuple-element.45), channel_id=1, source_target_pairs={{32,0},{64,32},{96,64},{128,96},{160,128},{192,160},{224,192},{256... | collective-permute-start | bytes 1437704 | tf_op jit(solution)/shard_map/ppermute | solution.py:571
  52.4 13.2 %collective-permute-start.5 = (f32[13,72,128]{2,1,0:T(8,128)S(1)}, f32[13,72,128]{2,1,0:T(8,128)}, u32[]{:S(2)}, u32[]{:S(2)}) collective-permute-start(f32[13,72,128]{2,1,0:T(8,128)S(1)} %get-tuple-element.46), channel_id=1, source_target_pairs={{0,32},{32,64},{64,96},{96,128},{128,160},{160,192},{192,224},{224... | collective-permute-start | bytes 1437704 | tf_op jit(solution)/shard_map/ppermute | solution.py:571

commit v6 on v5

--- a/solution.py
+++ b/solution.py
@@ -58,6 +58,10 @@
 
 def in_hbm(value):
     return pltpu.with_memory_space_constraint(value, pltpu.HBM)
+
+
+def far_out(*shape):
+    return pltpu.HBM(shape, jnp.float32)
 
 
 def near(*shape):
@@ -288,7 +292,7 @@
 
 
 def beside(value, edge):
-    lane = lane_ids()
+    lane = lane_ids(value.shape[0])
     down = jnp.where(lane == 0, edge, roll_lanes(value, 1))
     up = jnp.where(lane == LANES - 1, edge, roll_lanes(value, -1))
     return down, up
@@ -413,28 +417,29 @@
     for sweep in range(SWEEPS):
         now, last = stages[sweep], sweep == SWEEPS - 1
 
-        def relax(x, carry):
-            weights = [w_ref[k, x] for k in range(6)]
+        rows, weigh_rows, above, below, held = (
+            (pl.ds(TOP + 2, cells_y), pl.ds(2, cells_y), pl.ds(TOP + 1, cells_y), pl.ds(TOP + 3, cells_y), first[:cells_y])
+            if last
+            else (WINDOW, pl.ds(0, WIN), BEFORE, AFTER, first)
+        )
+        for x in range(1 + sweep, cells_x - 1 - sweep):
+            weights = [w_ref[k, x, weigh_rows, :] for k in range(6)]
             for ch in range(3):
-                own = now[ch, x, WINDOW, :]
-                down, up = beside(own, from_edge(e_ref[sweep, ch, WINDOW, :], x))
+                own = now[ch, x, rows, :]
+                down, up = beside(own, from_edge(e_ref[sweep, ch, rows, :], x))
                 others = (
-                    now[ch, x - 1, WINDOW, :],
-                    now[ch, x + 1, WINDOW, :],
-                    now[ch, x, BEFORE, :],
-                    now[ch, x, AFTER, :],
+                    now[ch, x - 1, rows, :],
+                    now[ch, x + 1, rows, :],
+                    now[ch, x, above, :],
+                    now[ch, x, below, :],
                     down,
                     up,
                 )
-                new = jnp.where(first, own, relaxed(own, others, weights))
+                new = jnp.where(held, own, relaxed(own, others, weights))
                 if last:
-                    done_ref[ch, x] = new[2 : 2 + cells_y]
+                    done_ref[ch, x] = new
                 else:
                     stages[sweep + 1][ch, x, WINDOW, :] = new
-            return carry
-
-        for x in range(1 + sweep, cells_x - 1 - sweep):
-            relax(x, 0)
         if not last:
             for ch in range(3):
                 ends = zeros()
@@ -492,7 +497,7 @@
     edge_stiff = (es_ref, eside_ref)
 
     ends = zeros()
-    for x in beyond:
+    for x in (-1, cells_x):
         ends = to_edge(ends, stiff(x)[WINDOW, :], spot(x)[1])
     for tile, middle in ((0, cs_ref[...]), (1, ends)):
         others = beside_edge(edge_stiff[tile], edge_stiff[1 - tile][WINDOW, :], middle)
@@ -515,29 +520,34 @@
 
     for sweep in range(SWEEPS):
         last = sweep == SWEEPS - 1
+        rows, weigh_rows, above, below, fixed = (
+            (pl.ds(TOP + 2, cells_y), pl.ds(2, cells_y), pl.ds(TOP + 1, cells_y), pl.ds(TOP + 3, cells_y), first[:cells_y])
+            if last
+            else (WINDOW, pl.ds(0, WIN), BEFORE, AFTER, first)
+        )
         planes = [x for p in range(HALO) for x in (sweep - 2 + p, cells_x + 1 - sweep - p)]
         for x in planes:
             tile, g = spot(x)
             if 1 <= x < cells_x - 1:
-                weights = [w_ref[k, x] for k in range(6)]
+                weights = [w_ref[k, x, weigh_rows, :] for k in range(6)]
             else:
-                weights = [hw_ref[k, held(x)] for k in range(6)]
+                weights = [hw_ref[k, held(x), weigh_rows, :] for k in range(6)]
             for ch in range(3):
                 here = field(sweep, ch, x)
-                own = here[WINDOW, :]
-                down, up = beside(own, from_edge(e_ref[sweep, ch, tile, WINDOW, :], g))
+                own = here[rows, :]
+                down, up = beside(own, from_edge(e_ref[sweep, ch, tile, rows, :], g))
                 others = (
-                    field(sweep, ch, x - 1)[WINDOW, :],
-                    field(sweep, ch, x + 1)[WINDOW, :],
-                    here[BEFORE, :],
-                    here[AFTER, :],
+                    field(sweep, ch, x - 1)[rows, :],
+                    field(sweep, ch, x + 1)[rows, :],
+                    here[above, :],
+                    here[below, :],
                     down,
                     up,
                 )
-                new = jnp.where(first, own, relaxed(own, others, weights))
+                new = jnp.where(fixed, own, relaxed(own, others, weights))
                 if last:
                     place = x if x < HALO else x - cells_x + 2 * HALO
-                    new_ref[ch, place] = new[2 : 2 + cells_y]
+                    new_ref[ch, place] = new
                     sem = sems.at[3 + 6 * ch + place]
                     copies.append(pltpu.make_async_copy(new_ref.at[ch, place], out_ref.at[ch, x], sem))
                     copies[-1].start()
@@ -548,7 +558,7 @@
         for ch in range(3):
             if sweep == 0:
                 ends = zeros()
-                for x in beyond:
+                for x in (-1, cells_x):
                     ends = to_edge(ends, field(0, ch, x)[WINDOW, :], spot(x)[1])
                 middles = (c_ref[0, ch], ends)
             else:
@@ -632,7 +642,7 @@
     xlow, xhigh = kernel_call(
         functools.partial(pack_x_kernel, float(count_z)),
         "pack_x",
-        (f32(4 * HALO + 1, WIN, LANES), f32(4 * HALO + 1, WIN, LANES)),
+        (far_out(4 * HALO + 1, WIN, LANES), far_out(4 * HALO + 1, WIN, LANES)),
         8000 * MEGA,
         (edge, yabove, ybelow, prev_disp, stiff_factor),
         (scratch((4, WIN, LANES), num),),

time: 71.3 us -> 69.6 us (0.976)
  Pallas kernels: 17.6 us -> 16.2 us
    pallas_call x6, Pallas kernels: 17.6 us -> 16.2 us  [kernel_call(): pl.pallas_call(kernel, name=name, out_shape=outs, in_specs=[pl.BlockSpec(...]
where the time goes in v6:
time: 69.6 us; the launch traced here: 69.2 us
  starting transfers between devices  45.2 us (65%)
  Pallas kernels  16.2 us (23%)
  waiting for transfers between devices  7.66 us (11%)
    ppermute x6, starting transfers between devices, step(): lax.ppermute(value, axis, [(i, i + by) for i in range(size) if 0 <= i + b...  23.5 us
    pallas_call x6, Pallas kernels, kernel_call(): pl.pallas_call(kernel, name=name, out_shape=outs, in_specs=[pl.BlockSpec(...  16.2 us
    all_to_all x1, starting transfers between devices, body(): lax.all_to_all(rows.reshape(blocks, 1, LANES), ('gx', 'gy'), 0, 0, tiled=...  11.4 us
    all_to_all x1, starting transfers between devices, body(): shares = lax.all_to_all(share, 'gz', 0, 0, tiled=True)  10.3 us
    all_to_all x1, waiting for transfers between devices, body(): lax.all_to_all(rows.reshape(blocks, 1, LANES), ('gx', 'gy'), 0, 0, tiled=...  4.63 us
    all_to_all x1, waiting for transfers between devices, body(): shares = lax.all_to_all(share, 'gz', 0, 0, tiled=True)  3.02 us
  transfers between devices with their start and end apart: 8, of which 2 were waited for; matrix products, arithmetic and copies ran while one was open for 0% of the time, Pallas kernels for 14%

profile of v6, /device:TPU:1, one launch (start us, length us, event | category | flops | bytes accessed | tf_op | source)
XLA Modules:
  0.0 69.2 jit_solution(2321711057631218637)
XLA Ops:
  0.0 2.4 %pack_z.1 = (f32[64,128]{1,0:T(8,128)}, f32[2,64,128]{2,1,0:T(8,128)S(1)}, f32[2,64,128]{2,1,0:T(8,128)S(1)}, f32[192,128]{1,0:T(8,128)S(1)}, f32[192,128]{1,0:T(8,128)S(1)}) custom-call(f32[3,16,64,128]{3,2,1,0:T(8,128)} %prev_ref.5, f32[16,64,128]{2,1,0:T(8,128)} %stiff_ref.5, f32[3,32]{1,0:T(4,128)} %bitcast.7, s32[1,32]{1,0:T(1,128)} %bitcast.8), custom_call_target="tpu_custom_call" | custom-call | flops 2200000000 | bytes 360448 | tf_op jit(solution)/shard_map/pack_z/pallas_call | solution.py:38
  2.4 1.3 %collective-permute-start = (f32[2,64,128]{2,1,0:T(8,128)S(1)}, f32[2,64,128]{2,1,0:T(8,128)S(1)}, u32[]{:S(2)}, u32[]{:S(2)}) collective-permute-start(f32[2,64,128]{2,1,0:T(8,128)S(1)} %get-tuple-element.26), channel_id=1, source_target_pairs={{1,0},{2,1},{3,2},{4,3},{5,4},{6,5},{7,6},{9,8},{10,9},{11,10},{12... | collective-permute-start | bytes 196616 | tf_op jit(solution)/shard_map/ppermute | solution.py:581
  3.7 12.1 %collective-permute-start.1 = (f32[2,64,128]{2,1,0:T(8,128)S(1)}, f32[2,64,128]{2,1,0:T(8,128)S(1)}, u32[]{:S(2)}, u32[]{:S(2)}) collective-permute-start(f32[2,64,128]{2,1,0:T(8,128)S(1)} %get-tuple-element.27), channel_id=1, source_target_pairs={{0,1},{1,2},{2,3},{3,4},{4,5},{5,6},{6,7},{8,9},{9,10},{10,11},{11... | collective-permute-start | bytes 196616 | tf_op jit(solution)/shard_map/ppermute | solution.py:581
  15.8 11.4 %all-to-all-start = ((f32[64,1,128]{2,1,0:T(1,128)}), f32[64,1,128]{2,1,0:T(1,128)S(1)}, u32[]{:S(2)}, u32[]{:S(2)}) async-start(f32[64,1,128]{2,1,0:T(1,128)} %bitcast.3), calls=%async_computation | async-start | bytes 65536 | tf_op jit(solution)/shard_map/all_to_all | solution.py:617
  27.2 0.0 collective-permute-done.above_ref
  27.2 0.0 collective-permute-done.1.below_ref
  27.2 0.1 pack_y.1
  27.3 0.0 copy-start.2
  27.3 3.3 %collective-permute-start.3 = (f32[208,128]{1,0:T(8,128)S(1)}, f32[208,128]{1,0:T(8,128)S(1)}, u32[]{:S(2)}, u32[]{:S(2)}) collective-permute-start(f32[208,128]{1,0:T(8,128)S(1)} %get-tuple-element.32), channel_id=1, source_target_pairs={{0,8},{8,16},{16,24},{1,9},{9,17},{17,25},{2,10},{10,18},{18,26},{... | collective-permute-start | bytes 319496 | tf_op jit(solution)/shard_map/ppermute | solution.py:581
  30.6 1.3 %collective-permute-start.2 = (f32[208,128]{1,0:T(8,128)S(1)}, f32[208,128]{1,0:T(8,128)S(1)}, u32[]{:S(2)}, u32[]{:S(2)}) collective-permute-start(f32[208,128]{1,0:T(8,128)S(1)} %get-tuple-element.31._), channel_id=1, source_target_pairs={{8,0},{16,8},{24,16},{9,1},{17,9},{25,17},{10,2},{18,10},{26,18},{... | collective-permute-start | bytes 319496 | tf_op jit(solution)/shard_map/ppermute | solution.py:581
  31.9 4.6 %all-to-all-done = f32[64,1,128]{2,1,0:T(1,128)S(1)} async-done(((f32[64,1,128]{2,1,0:T(1,128)}), f32[64,1,128]{2,1,0:T(1,128)S(1)}, u32[]{:S(2)}, u32[]{:S(2)}) %all-to-all-start) | async-done | bytes 32800 | tf_op jit(solution)/shard_map/all_to_all | solution.py:617
  36.5 0.0 copy-start
  36.5 0.0 copy-start.1
  36.5 1.5 %rbf.1 = f32[8,40,128]{2,1,0:T(8,128)} custom-call(f32[64,128]{1,0:T(8,128)S(1)} %bitcast.6, f32[208,128]{1,0:T(8,128)S(1)} %get-tuple-element.31._), custom_call_target="tpu_custom_call" | custom-call | flops 1650000000 | bytes 196608 | tf_op jit(solution)/shard_map/rbf/pallas_call | solution.py:38
  38.1 10.3 %all-to-all-start.1 = ((f32[8,40,128]{2,1,0:T(8,128)}), f32[8,40,128]{2,1,0:T(8,128)S(1)}, u32[]{:S(2)}, u32[]{:S(2)}) async-start(f32[8,40,128]{2,1,0:T(8,128)} %rbf.1), calls=%async_computation.1 | async-start | bytes 327680 | tf_op jit(solution)/shard_map/all_to_all | solution.py:640
  48.4 0.0 collective-permute-done.3.ybelow_ref
  48.4 0.0 collective-permute-done.2.yabove_ref
  48.4 0.0 copy-done.2
  48.4 0.0 copy-done
  48.4 0.0 copy-done.1
  48.4 1.1 %pack_x.1 = (f32[13,72,128]{2,1,0:T(8,128)}, f32[13,72,128]{2,1,0:T(8,128)}) custom-call(f32[4,64,128]{2,1,0:T(8,128)S(1)} %get-tuple-element.30.edge_ref, f32[208,128]{1,0:T(8,128)S(1)} %collective-permute-done.2.yabove_ref, f32[208,128]{1,0:T(8,128)S(1)} %collective-permute-done.3.ybelow_ref, f32[3,16,64,128]{3,2,1,0:T(8,128)S(1)} %copy-done, ...), custom_call_target="tpu_custom_call" | custom-call | flops 8800000000 | bytes 3399680 | tf_op jit(solution)/shard_map/pack_x/pallas_call | solution.py:38
  49.5 3.1 %collective-permute-start.4 = (f32[13,72,128]{2,1,0:T(8,128)}, f32[13,72,128]{2,1,0:T(8,128)S(1)}, u32[]{:S(2)}, u32[]{:S(2)}) collective-permute-start(f32[13,72,128]{2,1,0:T(8,128)} %get-tuple-element.45), channel_id=1, source_target_pairs={{32,0},{64,32},{96,64},{128,96},{160,128},{192,160},{224,192},{256... | collective-permute-start | bytes 1437704 | tf_op jit(solution)/shard_map/ppermute | solution.py:581
  52.6 2.4 %collective-permute-start.5 = (f32[13,72,128]{2,1,0:T(8,128)}, f32[13,72,128]{2,1,0:T(8,128)S(1)}, u32[]{:S(2)}, u32[]{:S(2)}) collective-permute-start(f32[13,72,128]{2,1,0:T(8,128)} %get-tuple-element.46), channel_id=1, source_target_pairs={{0,32},{32,64},{64,96},{96,128},{128,160},{160,192},{192,224},{224... | collective-permute-start | bytes 1437704 | tf_op jit(solution)/shard_map/ppermute | solution.py:581
  55.0 3.0 %all-to-all-done.1.shares_ref = f32[8,40,128]{2,1,0:T(8,128)S(1)} async-done(((f32[8,40,128]{2,1,0:T(8,128)}), f32[8,40,128]{2,1,0:T(8,128)S(1)}, u32[]{:S(2)}, u32[]{:S(2)}) %all-to-all-start.1) | async-done | bytes 163872 | tf_op jit(solution)/shard_map/all_to_all | solution.py:640
  58.0 7.3 %inner.1 = (f32[3,16,88,128]{3,2,1,0:T(8,128)S(1)}, f32[3,16,88,128]{3,2,1,0:T(8,128)S(1)}, f32[3,16,88,128]{3,2,1,0:T(8,128)S(1)}, f32[16,88,128]{2,1,0:T(8,128...) custom-call(f32[3,16,64,128]{3,2,1,0:T(8,128)S(1)} %copy-done, ...), custom_call_target="tpu_custom_call" | custom-call | flops 9900000256 | bytes 15413248 | tf_op jit(solution)/shard_map/inner/pallas_call | solution.py:38
  65.3 0.0 collective-permute-done.4.xabove_ref
  65.4 0.0 collective-permute-done.5.xbelow_ref
  65.4 3.8 %outer.1 = f32[3,16,64,128]{3,2,1,0:T(8,128)} custom-call(f32[3,16,88,128]{3,2,1,0:T(8,128)S(1)} %get-tuple-element.34.u0_ref, f32[3,16,88,128]{3,2,1,0:T(8,128)S(1)} %get-tuple-element.35.u1_ref, f32[3,16,88,128]{3,2,1,0:T(8,128)S(1)} %get-tuple-element.36.u2_ref, f32[16,88,128]{2,1,0:T(8,128)S(1)} %get-tuple-element.37.s_ref, ...), custom_call_target="tpu_custom_call" | custom-call | flops 6049999872 | bytes 15339520 | tf_op jit(solution)/shard_map/outer/pallas_call | solution.py:38
Async XLA Ops:
  2.4 24.8 %collective-permute-start = (f32[2,64,128]{2,1,0:T(8,128)S(1)}, f32[2,64,128]{2,1,0:T(8,128)S(1)}, u32[]{:S(2)}, u32[]{:S(2)}) collective-permute-start(f32[2,64,128]{2,1,0:T(8,128)S(1)} %get-tuple-element.26), channel_id=1, source_target_pairs={{1,0},{2,1},{3,2},{4,3},{5,4},{6,5},{7,6},{9,8},{10,9},{11,10},{12... | collective-permute-start | bytes 196616 | tf_op jit(solution)/shard_map/ppermute | solution.py:581
  3.7 23.5 %collective-permute-start.1 = (f32[2,64,128]{2,1,0:T(8,128)S(1)}, f32[2,64,128]{2,1,0:T(8,128)S(1)}, u32[]{:S(2)}, u32[]{:S(2)}) collective-permute-start(f32[2,64,128]{2,1,0:T(8,128)S(1)} %get-tuple-element.27), channel_id=1, source_target_pairs={{0,1},{1,2},{2,3},{3,4},{4,5},{5,6},{6,7},{8,9},{9,10},{10,11},{11... | collective-permute-start | bytes 196616 | tf_op jit(solution)/shard_map/ppermute | solution.py:581
  15.8 20.7 %all-to-all-start = ((f32[64,1,128]{2,1,0:T(1,128)}), f32[64,1,128]{2,1,0:T(1,128)S(1)}, u32[]{:S(2)}, u32[]{:S(2)}) async-start(f32[64,1,128]{2,1,0:T(1,128)} %bitcast.3), calls=%async_computation | async-start | bytes 65536 | tf_op jit(solution)/shard_map/all_to_all | solution.py:617
  27.3 21.1 %copy-start.2 = (f32[4,64,128]{2,1,0:T(8,128)}, f32[4,64,128]{2,1,0:T(8,128)S(1)}, u32[]{:S(2)}) copy-start(f32[4,64,128]{2,1,0:T(8,128)S(1)} %get-tuple-element.30.edge_ref) | copy-start | bytes 393220
  27.3 21.1 %collective-permute-start.3 = (f32[208,128]{1,0:T(8,128)S(1)}, f32[208,128]{1,0:T(8,128)S(1)}, u32[]{:S(2)}, u32[]{:S(2)}) collective-permute-start(f32[208,128]{1,0:T(8,128)S(1)} %get-tuple-element.32), channel_id=1, source_target_pairs={{0,8},{8,16},{16,24},{1,9},{9,17},{17,25},{2,10},{10,18},{18,26},{... | collective-permute-start | bytes 319496 | tf_op jit(solution)/shard_map/ppermute | solution.py:581
  30.6 17.8 %collective-permute-start.2 = (f32[208,128]{1,0:T(8,128)S(1)}, f32[208,128]{1,0:T(8,128)S(1)}, u32[]{:S(2)}, u32[]{:S(2)}) collective-permute-start(f32[208,128]{1,0:T(8,128)S(1)} %get-tuple-element.31._), channel_id=1, source_target_pairs={{8,0},{16,8},{24,16},{9,1},{17,9},{25,17},{10,2},{18,10},{26,18},{... | collective-permute-start | bytes 319496 | tf_op jit(solution)/shard_map/ppermute | solution.py:581
  36.5 11.9 %copy-start = (f32[3,16,64,128]{3,2,1,0:T(8,128)S(1)}, f32[3,16,64,128]{3,2,1,0:T(8,128)}, u32[]{:S(2)}) copy-start(f32[3,16,64,128]{3,2,1,0:T(8,128)} %prev_ref.5) | copy-start | bytes 4718596
  36.5 11.9 %copy-start.1 = (f32[16,64,128]{2,1,0:T(8,128)S(1)}, f32[16,64,128]{2,1,0:T(8,128)}, u32[]{:S(2)}) copy-start(f32[16,64,128]{2,1,0:T(8,128)} %stiff_ref.5) | copy-start | bytes 1572868
  38.1 20.0 %all-to-all-start.1 = ((f32[8,40,128]{2,1,0:T(8,128)}), f32[8,40,128]{2,1,0:T(8,128)S(1)}, u32[]{:S(2)}, u32[]{:S(2)}) async-start(f32[8,40,128]{2,1,0:T(8,128)} %rbf.1), calls=%async_computation.1 | async-start | bytes 327680 | tf_op jit(solution)/shard_map/all_to_all | solution.py:640
  49.5 15.9 %collective-permute-start.4 = (f32[13,72,128]{2,1,0:T(8,128)}, f32[13,72,128]{2,1,0:T(8,128)S(1)}, u32[]{:S(2)}, u32[]{:S(2)}) collective-permute-start(f32[13,72,128]{2,1,0:T(8,128)} %get-tuple-element.45), channel_id=1, source_target_pairs={{32,0},{64,32},{96,64},{128,96},{160,128},{192,160},{224,192},{256... | collective-permute-start | bytes 1437704 | tf_op jit(solution)/shard_map/ppermute | solution.py:581
  52.6 12.8 %collective-permute-start.5 = (f32[13,72,128]{2,1,0:T(8,128)}, f32[13,72,128]{2,1,0:T(8,128)S(1)}, u32[]{:S(2)}, u32[]{:S(2)}) collective-permute-start(f32[13,72,128]{2,1,0:T(8,128)} %get-tuple-element.46), channel_id=1, source_target_pairs={{0,32},{32,64},{64,96},{96,128},{128,160},{160,192},{192,224},{224... | collective-permute-start | bytes 1437704 | tf_op jit(solution)/shard_map/ppermute | solution.py:581

commit v7 on v6

--- a/solution.py
+++ b/solution.py
@@ -134,6 +134,12 @@
         even, odd = edge_ref[2 * pair], edge_ref[2 * pair + 1]
         low_ref[pair] = jnp.where(place <= 3, even, roll_lanes(odd, 3))
         high_ref[pair] = jnp.where(place >= 4, even, roll_lanes(odd, -3))
+
+
+def pair_kernel(own_ref, other_ref, out_ref):
+    rows = lax.broadcasted_iota(jnp.int32, out_ref.shape, 0)
+    own, other = (jnp.broadcast_to(ref[0:1, :], out_ref.shape) for ref in (own_ref, other_ref))
+    out_ref[...] = jnp.where(rows % 2 == 0, own, other)
 
 
 def pack_y_kernel(above_ref, below_ref, ylow_ref, yhigh_ref, edge_ref, outlow_ref, outhigh_ref):
@@ -592,11 +598,11 @@
     num = jnp.float32
 
     rows_y = 4 * cells_x * HALO
-    rows, low, high, ylow, yhigh = kernel_call(
+    row, low, high, ylow, yhigh = kernel_call(
         functools.partial(begin_kernel, float(count_z)),
         "pack_z",
         (
-            f32(blocks, LANES),
+            f32(8, LANES),
             f32(2, cells_y, LANES),
             f32(2, cells_y, LANES),
             f32(rows_y, LANES),
@@ -614,8 +620,15 @@
         ),
         far=tuple(in_hbm(a) for a in (prev_disp, stiff_factor, centre_coef.T, centre_index[None])),
     )
-    centres = lax.all_to_all(rows.reshape(blocks, 1, LANES), ("gx", "gy"), 0, 0, tiled=True)
     zabove, zbelow = step(low, "gz", -1), step(high, "gz", 1)
+
+    along_x, along_y = lax.axis_size("gx"), lax.axis_size("gy")
+    other = lax.ppermute(row, "gx", [(i, i ^ 1) for i in range(along_x)])
+    (rows,) = kernel_call(pair_kernel, "pair", (f32(blocks, LANES),), 500 * MEGA, (row, other))
+    every_second = [[x * along_y + y for x in range(k, along_x, 2) for y in range(along_y)] for k in range(2)]
+    centres = lax.all_to_all(
+        rows.reshape(blocks // 2, 2, LANES), ("gx", "gy"), 0, 0, tiled=True, axis_index_groups=every_second
+    )
 
     rows_all = -(-(rows_y + 4 * HALO) // 8) * 8
     edge, ylow, yhigh = kernel_call(

time: 69.6 us -> 71.5 us (1.027)
  the two profiles are of different devices: /device:TPU:1 before, /device:TPU:8 now
where the time goes in v7:
time: 71.5 us; the launch traced here: 71.1 us
  starting transfers between devices  44.8 us (63%)
  Pallas kernels  16.5 us (23%)
  waiting for transfers between devices  9.64 us (13%)
    ppermute x6, starting transfers between devices, step(): lax.ppermute(value, axis, [(i, i + by) for i in range(size) if 0 <= i + b...  21.8 us
    pallas_call x7, Pallas kernels, kernel_call(): pl.pallas_call(kernel, name=name, out_shape=outs, in_specs=[pl.BlockSpec(...  16.5 us
    all_to_all x1, starting transfers between devices, body(): shares = lax.all_to_all(share, 'gz', 0, 0, tiled=True)  10.6 us
    all_to_all x1, starting transfers between devices, body(): lax.all_to_all(rows.reshape(blocks // 2, 2, LANES), ('gx', 'gy'), 0, 0, t...  10.4 us
    all_to_all x1, waiting for transfers between devices, body(): shares = lax.all_to_all(share, 'gz', 0, 0, tiled=True)  5.3 us
    all_to_all x1, waiting for transfers between devices, body(): lax.all_to_all(rows.reshape(blocks // 2, 2, LANES), ('gx', 'gy'), 0, 0, t...  4.32 us
    ppermute x1, starting transfers between devices, body(): other = lax.ppermute(row, 'gx', [(i, i ^ 1) for i in range(along_x)])  1.92 us
  transfers between devices with their start and end apart: 9, of which 2 were waited for; matrix products, arithmetic and copies ran while one was open for 0% of the time, Pallas kernels for 15%

profile of v7, /device:TPU:8, one launch (start us, length us, event | category | flops | bytes accessed | tf_op | source)
XLA Modules:
  0.0 71.1 jit_solution(9681672364459674644)
XLA Ops:
  0.0 2.1 %pack_z.1 = (f32[8,128]{1,0:T(8,128)S(1)}, f32[2,64,128]{2,1,0:T(8,128)S(1)}, f32[2,64,128]{2,1,0:T(8,128)S(1)}, f32[192,128]{1,0:T(8,128)S(1)}, f32[192,128]{1,0:T(8,128)S(1)}) custom-call(f32[3,16,64,128]{3,2,1,0:T(8,128)} %prev_ref.5, f32[16,64,128]{2,1,0:T(8,128)} %stiff_ref.5, f32[3,32]{1,0:T(4,128)} %bitcast.5, s32[1,32]{1,0:T(1,128)} %bitcast.6), custom_call_target="tpu_custom_call" | custom-call | flops 2200000000 | bytes 331776 | tf_op jit(solution)/shard_map/pack_z/pallas_call | solution.py:38
  2.1 1.9 %collective-permute-start.4 = (f32[8,128]{1,0:T(8,128)S(1)}, f32[8,128]{1,0:T(8,128)S(1)}, u32[]{:S(2)}, u32[]{:S(2)}) collective-permute-start(f32[8,128]{1,0:T(8,128)S(1)} %get-tuple-element.33.own_ref), channel_id=1, source_target_pairs={{0,32},{32,0},{64,96},{96,64},{128,160},{160,128},{192,224},{224,1... | collective-permute-start | bytes 12296 | tf_op jit(solution)/shard_map/ppermute | solution.py:626
  4.0 1.3 %collective-permute-start = (f32[2,64,128]{2,1,0:T(8,128)S(1)}, f32[2,64,128]{2,1,0:T(8,128)S(1)}, u32[]{:S(2)}, u32[]{:S(2)}) collective-permute-start(f32[2,64,128]{2,1,0:T(8,128)S(1)} %get-tuple-element.26), channel_id=1, source_target_pairs={{1,0},{2,1},{3,2},{4,3},{5,4},{6,5},{7,6},{9,8},{10,9},{11,10},{12... | collective-permute-start | bytes 196616 | tf_op jit(solution)/shard_map/ppermute | solution.py:587
  5.3 11.5 %collective-permute-start.1 = (f32[2,64,128]{2,1,0:T(8,128)S(1)}, f32[2,64,128]{2,1,0:T(8,128)S(1)}, u32[]{:S(2)}, u32[]{:S(2)}) collective-permute-start(f32[2,64,128]{2,1,0:T(8,128)S(1)} %get-tuple-element.27), channel_id=1, source_target_pairs={{0,1},{1,2},{2,3},{3,4},{4,5},{5,6},{6,7},{8,9},{9,10},{10,11},{11... | collective-permute-start | bytes 196616 | tf_op jit(solution)/shard_map/ppermute | solution.py:587
  16.8 0.0 collective-permute-done.4.other_ref
  16.9 0.6 pair.1
  17.5 10.4 %all-to-all-start = ((f32[32,2,128]{2,1,0:T(2,128)}), f32[32,2,128]{2,1,0:T(2,128)S(1)}, u32[]{:S(2)}, u32[]{:S(2)}) async-start(f32[32,2,128]{2,1,0:T(2,128)} %bitcast.2), calls=%async_computation | async-start | bytes 65536 | tf_op jit(solution)/shard_map/all_to_all | solution.py:629
  27.9 0.0 collective-permute-done.above_ref
  27.9 0.0 collective-permute-done.1.below_ref
  27.9 0.1 pack_y.1
  28.0 0.0 copy-start.2
  28.1 3.4 %collective-permute-start.3 = (f32[208,128]{1,0:T(8,128)S(1)}, f32[208,128]{1,0:T(8,128)S(1)}, u32[]{:S(2)}, u32[]{:S(2)}) collective-permute-start(f32[208,128]{1,0:T(8,128)S(1)} %get-tuple-element.32), channel_id=1, source_target_pairs={{0,8},{8,16},{16,24},{1,9},{9,17},{17,25},{2,10},{10,18},{18,26},{... | collective-permute-start | bytes 319496 | tf_op jit(solution)/shard_map/ppermute | solution.py:587
  31.4 1.3 %collective-permute-start.2 = (f32[208,128]{1,0:T(8,128)S(1)}, f32[208,128]{1,0:T(8,128)S(1)}, u32[]{:S(2)}, u32[]{:S(2)}) collective-permute-start(f32[208,128]{1,0:T(8,128)S(1)} %get-tuple-element.31._), channel_id=1, source_target_pairs={{8,0},{16,8},{24,16},{9,1},{17,9},{25,17},{10,2},{18,10},{26,18},{... | collective-permute-start | bytes 319496 | tf_op jit(solution)/shard_map/ppermute | solution.py:587
  32.7 4.3 %all-to-all-done = f32[32,2,128]{2,1,0:T(2,128)S(1)} async-done(((f32[32,2,128]{2,1,0:T(2,128)}), f32[32,2,128]{2,1,0:T(2,128)S(1)}, u32[]{:S(2)}, u32[]{:S(2)}) %all-to-all-start) | async-done | bytes 32800 | tf_op jit(solution)/shard_map/all_to_all | solution.py:629
  37.1 0.0 copy-start
  37.1 0.0 copy-start.1
  37.1 1.5 %rbf.1 = f32[8,40,128]{2,1,0:T(8,128)} custom-call(f32[64,128]{1,0:T(8,128)S(1)} %bitcast.4, f32[208,128]{1,0:T(8,128)S(1)} %get-tuple-element.31._), custom_call_target="tpu_custom_call" | custom-call | flops 1650000000 | bytes 196608 | tf_op jit(solution)/shard_map/rbf/pallas_call | solution.py:38
  38.6 10.6 %all-to-all-start.1 = ((f32[8,40,128]{2,1,0:T(8,128)}), f32[8,40,128]{2,1,0:T(8,128)S(1)}, u32[]{:S(2)}, u32[]{:S(2)}) async-start(f32[8,40,128]{2,1,0:T(8,128)} %rbf.1), calls=%async_computation.1 | async-start | bytes 327680 | tf_op jit(solution)/shard_map/all_to_all | solution.py:653
  49.2 0.0 collective-permute-done.3.ybelow_ref
  49.2 0.0 collective-permute-done.2.yabove_ref
  49.2 0.0 copy-done.2
  49.2 0.0 copy-done
  49.2 0.0 copy-done.1
  49.2 1.1 %pack_x.1 = (f32[13,72,128]{2,1,0:T(8,128)}, f32[13,72,128]{2,1,0:T(8,128)}) custom-call(f32[4,64,128]{2,1,0:T(8,128)S(1)} %get-tuple-element.30.edge_ref, f32[208,128]{1,0:T(8,128)S(1)} %collective-permute-done.2.yabove_ref, f32[208,128]{1,0:T(8,128)S(1)} %collective-permute-done.3.ybelow_ref, f32[3,16,64,128]{3,2,1,0:T(8,128)S(1)} %copy-done, ...), custom_call_target="tpu_custom_call" | custom-call | flops 8800000000 | bytes 3399680 | tf_op jit(solution)/shard_map/pack_x/pallas_call | solution.py:38
  50.3 1.9 %collective-permute-start.5 = (f32[13,72,128]{2,1,0:T(8,128)}, f32[13,72,128]{2,1,0:T(8,128)S(1)}, u32[]{:S(2)}, u32[]{:S(2)}) collective-permute-start(f32[13,72,128]{2,1,0:T(8,128)} %get-tuple-element.45), channel_id=1, source_target_pairs={{32,0},{64,32},{96,64},{128,96},{160,128},{192,160},{224,192},{256... | collective-permute-start | bytes 1437704 | tf_op jit(solution)/shard_map/ppermute | solution.py:587
  52.2 2.4 %collective-permute-start.6 = (f32[13,72,128]{2,1,0:T(8,128)}, f32[13,72,128]{2,1,0:T(8,128)S(1)}, u32[]{:S(2)}, u32[]{:S(2)}) collective-permute-start(f32[13,72,128]{2,1,0:T(8,128)} %get-tuple-element.46), channel_id=1, source_target_pairs={{0,32},{32,64},{64,96},{96,128},{128,160},{160,192},{192,224},{224... | collective-permute-start | bytes 1437704 | tf_op jit(solution)/shard_map/ppermute | solution.py:587
  54.6 5.3 %all-to-all-done.1.shares_ref = f32[8,40,128]{2,1,0:T(8,128)S(1)} async-done(((f32[8,40,128]{2,1,0:T(8,128)}), f32[8,40,128]{2,1,0:T(8,128)S(1)}, u32[]{:S(2)}, u32[]{:S(2)}) %all-to-all-start.1) | async-done | bytes 163872 | tf_op jit(solution)/shard_map/all_to_all | solution.py:653
  59.9 7.3 %inner.1 = (f32[3,16,88,128]{3,2,1,0:T(8,128)S(1)}, f32[3,16,88,128]{3,2,1,0:T(8,128)S(1)}, f32[3,16,88,128]{3,2,1,0:T(8,128)S(1)}, f32[16,88,128]{2,1,0:T(8,128...) custom-call(f32[3,16,64,128]{3,2,1,0:T(8,128)S(1)} %copy-done, ...), custom_call_target="tpu_custom_call" | custom-call | flops 9900000256 | bytes 15413248 | tf_op jit(solution)/shard_map/inner/pallas_call | solution.py:38
  67.2 0.0 collective-permute-done.5.xabove_ref
  67.2 0.0 collective-permute-done.6.xbelow_ref
  67.3 3.8 %outer.1 = f32[3,16,64,128]{3,2,1,0:T(8,128)} custom-call(f32[3,16,88,128]{3,2,1,0:T(8,128)S(1)} %get-tuple-element.34.u0_ref, f32[3,16,88,128]{3,2,1,0:T(8,128)S(1)} %get-tuple-element.35.u1_ref, f32[3,16,88,128]{3,2,1,0:T(8,128)S(1)} %get-tuple-element.36.u2_ref, f32[16,88,128]{2,1,0:T(8,128)S(1)} %get-tuple-element.37.s_ref, ...), custom_call_target="tpu_custom_call" | custom-call | flops 6049999872 | bytes 15339520 | tf_op jit(solution)/shard_map/outer/pallas_call | solution.py:38
Async XLA Ops:
  2.1 14.8 %collective-permute-start.4 = (f32[8,128]{1,0:T(8,128)S(1)}, f32[8,128]{1,0:T(8,128)S(1)}, u32[]{:S(2)}, u32[]{:S(2)}) collective-permute-start(f32[8,128]{1,0:T(8,128)S(1)} %get-tuple-element.33.own_ref), channel_id=1, source_target_pairs={{0,32},{32,0},{64,96},{96,64},{128,160},{160,128},{192,224},{224,1... | collective-permute-start | bytes 12296 | tf_op jit(solution)/shard_map/ppermute | solution.py:626
  4.0 23.9 %collective-permute-start = (f32[2,64,128]{2,1,0:T(8,128)S(1)}, f32[2,64,128]{2,1,0:T(8,128)S(1)}, u32[]{:S(2)}, u32[]{:S(2)}) collective-permute-start(f32[2,64,128]{2,1,0:T(8,128)S(1)} %get-tuple-element.26), channel_id=1, source_target_pairs={{1,0},{2,1},{3,2},{4,3},{5,4},{6,5},{7,6},{9,8},{10,9},{11,10},{12... | collective-permute-start | bytes 196616 | tf_op jit(solution)/shard_map/ppermute | solution.py:587
  5.3 22.6 %collective-permute-start.1 = (f32[2,64,128]{2,1,0:T(8,128)S(1)}, f32[2,64,128]{2,1,0:T(8,128)S(1)}, u32[]{:S(2)}, u32[]{:S(2)}) collective-permute-start(f32[2,64,128]{2,1,0:T(8,128)S(1)} %get-tuple-element.27), channel_id=1, source_target_pairs={{0,1},{1,2},{2,3},{3,4},{4,5},{5,6},{6,7},{8,9},{9,10},{10,11},{11... | collective-permute-start | bytes 196616 | tf_op jit(solution)/shard_map/ppermute | solution.py:587
  17.5 19.6 %all-to-all-start = ((f32[32,2,128]{2,1,0:T(2,128)}), f32[32,2,128]{2,1,0:T(2,128)S(1)}, u32[]{:S(2)}, u32[]{:S(2)}) async-start(f32[32,2,128]{2,1,0:T(2,128)} %bitcast.2), calls=%async_computation | async-start | bytes 65536 | tf_op jit(solution)/shard_map/all_to_all | solution.py:629
  28.0 21.2 %copy-start.2 = (f32[4,64,128]{2,1,0:T(8,128)}, f32[4,64,128]{2,1,0:T(8,128)S(1)}, u32[]{:S(2)}) copy-start(f32[4,64,128]{2,1,0:T(8,128)S(1)} %get-tuple-element.30.edge_ref) | copy-start | bytes 393220
  28.1 21.1 %collective-permute-start.3 = (f32[208,128]{1,0:T(8,128)S(1)}, f32[208,128]{1,0:T(8,128)S(1)}, u32[]{:S(2)}, u32[]{:S(2)}) collective-permute-start(f32[208,128]{1,0:T(8,128)S(1)} %get-tuple-element.32), channel_id=1, source_target_pairs={{0,8},{8,16},{16,24},{1,9},{9,17},{17,25},{2,10},{10,18},{18,26},{... | collective-permute-start | bytes 319496 | tf_op jit(solution)/shard_map/ppermute | solution.py:587
  31.4 17.8 %collective-permute-start.2 = (f32[208,128]{1,0:T(8,128)S(1)}, f32[208,128]{1,0:T(8,128)S(1)}, u32[]{:S(2)}, u32[]{:S(2)}) collective-permute-start(f32[208,128]{1,0:T(8,128)S(1)} %get-tuple-element.31._), channel_id=1, source_target_pairs={{8,0},{16,8},{24,16},{9,1},{17,9},{25,17},{10,2},{18,10},{26,18},{... | collective-permute-start | bytes 319496 | tf_op jit(solution)/shard_map/ppermute | solution.py:587
  37.1 12.2 %copy-start = (f32[3,16,64,128]{3,2,1,0:T(8,128)S(1)}, f32[3,16,64,128]{3,2,1,0:T(8,128)}, u32[]{:S(2)}) copy-start(f32[3,16,64,128]{3,2,1,0:T(8,128)} %prev_ref.5) | copy-start | bytes 4718596
  37.1 12.2 %copy-start.1 = (f32[16,64,128]{2,1,0:T(8,128)S(1)}, f32[16,64,128]{2,1,0:T(8,128)}, u32[]{:S(2)}) copy-start(f32[16,64,128]{2,1,0:T(8,128)} %stiff_ref.5) | copy-start | bytes 1572868
  38.6 21.3 %all-to-all-start.1 = ((f32[8,40,128]{2,1,0:T(8,128)}), f32[8,40,128]{2,1,0:T(8,128)S(1)}, u32[]{:S(2)}, u32[]{:S(2)}) async-start(f32[8,40,128]{2,1,0:T(8,128)} %rbf.1), calls=%async_computation.1 | async-start | bytes 327680 | tf_op jit(solution)/shard_map/all_to_all | solution.py:653
  50.3 16.9 %collective-permute-start.5 = (f32[13,72,128]{2,1,0:T(8,128)}, f32[13,72,128]{2,1,0:T(8,128)S(1)}, u32[]{:S(2)}, u32[]{:S(2)}) collective-permute-start(f32[13,72,128]{2,1,0:T(8,128)} %get-tuple-element.45), channel_id=1, source_target_pairs={{32,0},{64,32},{96,64},{128,96},{160,128},{192,160},{224,192},{256... | collective-permute-start | bytes 1437704 | tf_op jit(solution)/shard_map/ppermute | solution.py:587
  52.2 15.0 %collective-permute-start.6 = (f32[13,72,128]{2,1,0:T(8,128)}, f32[13,72,128]{2,1,0:T(8,128)S(1)}, u32[]{:S(2)}, u32[]{:S(2)}) collective-permute-start(f32[13,72,128]{2,1,0:T(8,128)} %get-tuple-element.46), channel_id=1, source_target_pairs={{0,32},{32,64},{64,96},{96,128},{128,160},{160,192},{192,224},{224... | collective-permute-start | bytes 1437704 | tf_op jit(solution)/shard_map/ppermute | solution.py:587
